TPU v7x, 32 devices: a whole 2x2x4 slice. The times are simulated.
32 devices in a mesh: dp: 4 (over z), ctx: 4 (over y, x), heads: 2 (over core).
Axes of the slice: x: 2, y: 2, z: 4, core: 2. Of those that a mesh axis runs over, the one named last changes fastest.
Arguments:
- tokens: bfloat16 [8, 512, 768], P('dp', 'ctx'), may hold values from -6 to 6
- cotangent: bfloat16 [8, 512, 768], P('dp', 'ctx'), may hold values from -6 to 6
- lengths: int32 [8], replicated, may hold values from 256 to 512, as said below
- dealing: int32 [8], replicated, may hold values from 0 to 7, each once
- qkv_weight: bfloat16 [2, 768, 3, 768], P(None, 'dp', None, 'heads')
- out_weight: bfloat16 [2, 768, 768], P(None, 'dp', 'heads'), may hold values from -0.875 to 0.875
- glu_weight: bfloat16 [2, 768, 2, 3072], P(None, 'dp', None, 'heads'), may hold values from -0.21875 to 0.21875
- down_weight: bfloat16 [2, 768, 3072], P(None, 'dp', 'heads'), may hold values from -0.109375 to 0.109375
- biases: float32 [2, 6, 768], replicated, may hold values from -3 to 3
- gains: float32 [2, 2, 768], replicated, may hold values from 0.1 to 1.9
Outputs:
- outputs: bfloat16 [8, 512, 768], P('dp', 'ctx')
- grad_tokens: float32 [8, 512, 768], P('dp', 'ctx')
- grad_qkv: float32 [2, 768, 3, 768], P(None, 'dp', None, 'heads')
- grad_out: float32 [2, 768, 768], P(None, 'dp', 'heads')
- grad_glu: float32 [2, 768, 2, 3072], P(None, 'dp', None, 'heads')
- grad_down: float32 [2, 768, 3072], P(None, 'dp', 'heads')
- grad_biases: float32 [2, 6, 768], P(None, None, 'dp')
- grad_gains: float32 [2, 2, 768], P(None, None, 'dp')
- clipped_qk: float32 [2, 768, 2, 768], P(None, 'dp', None, 'heads')
Inputs may be any that keep to these rules, and one draw needn't show every extreme that they name: `lengths`: at least one sequence has exactly 512 tokens. `dealing`: a permutation of the 8 sequences.
All inputs are finite; a program needn't handle non-finite values.
Results may differ from a plain program's by a relative error of at most 0.023.
Values may be sent and summed in bfloat16 or wider, within the bound.
No kernel may reach another device: no remote copies, remote signals or barrier semaphores. Data moves between devices by JAX's collectives and lax.ppermute only.
A program may use at most 192 MiB of HBM per device.

v0:
```python
import math

import jax
import jax.numpy as jnp
from jax import lax
from jax.sharding import PartitionSpec as P

HEADS = 12
HEAD_DIM = 64


EPSILON = 1e-12
NEGATIVE = -1e30
CLIP_LIMIT = 4.0
STEP_SIZE = 0.0008
HALF_SHARE = 0.5


def power_slopes(head_count):
    first_slope = 2.0 ** (-8.0 / head_count)
    return [first_slope ** (position + 1) for position in range(head_count)]


def alibi_slopes(head_count):
    closest = 2 ** int(math.floor(math.log2(head_count)))
    slopes = power_slopes(closest)
    slopes = slopes + power_slopes(2 * closest)[0::2][: head_count - closest]
    return slopes


def layer_norm(values, gain_row, shift_row):
    average = jnp.mean(values, axis=-1, keepdims=True)
    centred = values - average
    spread = jnp.mean(centred * centred, axis=-1, keepdims=True)
    return centred * lax.rsqrt(spread + EPSILON) * gain_row + shift_row


def glu_act(packed):
    half_width = packed.shape[-1] // 2
    return jax.nn.gelu(packed[:, :half_width], approximate=False) * packed[:, half_width:]


def contract_rows(former, latter):
    return lax.dot_general(
        former, latter, (((0,), (0,)), ((), ())), preferred_element_type=jnp.float32
    )


def contract_cols(former, latter):
    return lax.dot_general(
        former, latter, (((1,), (1,)), ((), ())), preferred_element_type=jnp.float32
    )


def split_heads(values, head_count):
    row_count = values.shape[0]
    return values.reshape(row_count, head_count, -1).transpose(1, 0, 2)


def join_heads(values):
    return values.transpose(1, 0, 2).reshape(values.shape[1], -1)


def shards(
    tokens,
    cotangent,
    lengths,
    dealing,
    qkv_weight,
    out_weight,
    glu_weight,
    down_weight,
    biases,
    gains,
):
    micro_count, row_count, feature_count = tokens.shape
    layer_count = qkv_weight.shape[0]
    local_width = qkv_weight.shape[3]
    local_heads = local_width // HEAD_DIM
    local_ff = glu_weight.shape[3]
    total_len = row_count * lax.axis_size("ctx")
    ctx_index = lax.axis_index("ctx")
    head_index = lax.axis_index("heads")
    group_index = lax.axis_index("dp")
    score_scale = float(HEAD_DIM) ** (-0.5)
    slopes = lax.dynamic_slice_in_dim(
        jnp.array(alibi_slopes(HEADS), jnp.float32), head_index * local_heads, local_heads
    )
    query_positions = ctx_index * row_count + jnp.arange(row_count, dtype=jnp.int32)
    key_positions = jnp.arange(total_len, dtype=jnp.int32)
    distance = jnp.abs(query_positions[:, None] - key_positions[None, :]).astype(jnp.float32)
    column_start = head_index * local_width
    slot_ids = jnp.arange(lengths.shape[0], dtype=jnp.int32)

    def forward_layer(layer_index, residual, weights, key_valid, query_valid):
        qkv_full, out_full, glu_full, down_full = weights
        qkv_flat = qkv_full.reshape(qkv_full.shape[0], -1)
        glu_flat = glu_full.reshape(glu_full.shape[0], -1)
        vectors = biases[layer_index]
        low_input = residual.astype(jnp.bfloat16)
        projected = jnp.dot(low_input, qkv_flat, preferred_element_type=jnp.float32)
        bias_query = lax.dynamic_slice_in_dim(vectors[0], column_start, local_width)
        bias_value = lax.dynamic_slice_in_dim(vectors[1], column_start, local_width)
        queries = split_heads(
            (projected[:, :local_width] + bias_query).astype(jnp.bfloat16), local_heads
        )
        keys_local = split_heads(
            projected[:, local_width : 2 * local_width].astype(jnp.bfloat16), local_heads
        )
        values_local = split_heads(
            (projected[:, 2 * local_width :] + bias_value).astype(jnp.bfloat16), local_heads
        )
        keys_all, values_all = (
            lax.all_gather(keys_local, "ctx", axis=1, tiled=True),
            lax.all_gather(values_local, "ctx", axis=1, tiled=True),
        )
        pair_valid = query_valid[:, None] & key_valid[None, :]

        def attend(head_items):
            query_head, key_head, value_head, head_slope = head_items
            raw_scores = (
                jnp.einsum("qd,kd->qk", query_head, key_head, preferred_element_type=jnp.float32)
                * score_scale
            )
            top_logit = jnp.max(jnp.where(pair_valid, raw_scores, NEGATIVE))
            scores = jnp.where(key_valid[None, :], raw_scores - head_slope * distance, NEGATIVE)
            row_max = jnp.max(scores, axis=-1, keepdims=True)
            exponent = jnp.exp(scores - row_max)
            totals = jnp.sum(exponent, axis=-1, keepdims=True)
            attn_probs = (exponent / totals).astype(jnp.bfloat16)
            head_mixed = jnp.dot(attn_probs, value_head, preferred_element_type=jnp.float32)
            return (head_mixed.astype(jnp.bfloat16), (row_max + jnp.log(totals))[:, 0], top_logit)

        mixed_heads, log_totals, top_logits = lax.map(
            attend, (queries, keys_all, values_all, slopes)
        )
        mixed_low = join_heads(mixed_heads)
        attention = lax.psum(contract_cols(mixed_low, out_full), "heads") + vectors[2]
        first_sum = residual + attention
        hidden_in = layer_norm(first_sum, gains[layer_index, 0], vectors[4])
        hidden_low = hidden_in.astype(jnp.bfloat16)
        gate_up = jnp.dot(hidden_low, glu_flat, preferred_element_type=jnp.float32)
        activated = glu_act(gate_up).astype(jnp.bfloat16)
        feed_out = lax.psum(contract_cols(activated, down_full), "heads") + vectors[3]
        second_sum = hidden_in + feed_out
        result = layer_norm(second_sum, gains[layer_index, 1], vectors[5])
        saved_state = (
            low_input,
            queries,
            keys_all,
            values_all,
            log_totals,
            mixed_low,
            first_sum,
            hidden_low,
            gate_up,
            activated,
            second_sum,
        )
        return (result, saved_state, top_logits)

    def backward_layer(layer_index, grad_above, saved_state, weights, key_valid):
        qkv_full, out_full, glu_full, down_full = weights
        qkv_flat = qkv_full.reshape(qkv_full.shape[0], -1)
        glu_flat = glu_full.reshape(glu_full.shape[0], -1)
        (
            low_input,
            queries,
            keys_all,
            values_all,
            log_totals,
            mixed_low,
            first_sum,
            hidden_low,
            gate_up,
            activated,
            second_sum,
        ) = saved_state
        vectors = biases[layer_index]
        unused_second, second_back = jax.vjp(
            layer_norm, second_sum, gains[layer_index, 1], vectors[5]
        )
        grad_second, grad_gain_two, grad_shift_two = second_back(grad_above)
        feed_grad = grad_second.astype(jnp.bfloat16)
        grad_down = contract_rows(feed_grad, activated)
        grad_act = jnp.dot(feed_grad, down_full, preferred_element_type=jnp.float32)
        unused_glu, glu_back = jax.vjp(glu_act, gate_up)
        grad_gate_up = glu_back(grad_act)[0].astype(jnp.bfloat16)
        grad_glu = contract_rows(hidden_low, grad_gate_up)
        grad_hidden = grad_second + lax.psum(contract_cols(grad_gate_up, glu_flat), "heads")
        unused_first, first_back = jax.vjp(layer_norm, first_sum, gains[layer_index, 0], vectors[4])
        grad_first, grad_gain_one, grad_shift_one = first_back(grad_hidden)
        attn_grad = grad_first.astype(jnp.bfloat16)
        grad_out_weight = contract_rows(attn_grad, mixed_low)
        grad_mixed = split_heads(
            jnp.dot(attn_grad, out_full, preferred_element_type=jnp.float32).astype(jnp.bfloat16),
            local_heads,
        )

        def attend_back(head_items):
            query_head, key_head, value_head, log_total, grad_head, head_slope = head_items
            raw_scores = (
                jnp.einsum("qd,kd->qk", query_head, key_head, preferred_element_type=jnp.float32)
                * score_scale
            )
            scores = jnp.where(key_valid[None, :], raw_scores - head_slope * distance, NEGATIVE)
            attn_probs = jnp.exp(scores - log_total[:, None])
            grad_probs = jnp.einsum(
                "qd,kd->qk", grad_head, value_head, preferred_element_type=jnp.float32
            )
            inner_sum = jnp.sum(grad_probs * attn_probs, axis=-1, keepdims=True)
            grad_scores = (attn_probs * (grad_probs - inner_sum)).astype(jnp.bfloat16)
            grad_query = (
                jnp.dot(grad_scores, key_head, preferred_element_type=jnp.float32) * score_scale
            )
            grad_key = (
                jnp.einsum("qk,qd->kd", grad_scores, query_head, preferred_element_type=jnp.float32)
                * score_scale
            )
            grad_value = jnp.einsum(
                "qk,qd->kd",
                attn_probs.astype(jnp.bfloat16),
                grad_head,
                preferred_element_type=jnp.float32,
            )
            return (grad_query, grad_key, grad_value)

        grad_queries, key_terms, value_terms = lax.map(
            attend_back, (queries, keys_all, values_all, log_totals, grad_mixed, slopes)
        )
        grad_keys, grad_values = (
            lax.psum_scatter(key_terms, "ctx", scatter_dimension=1, tiled=True),
            lax.psum_scatter(value_terms, "ctx", scatter_dimension=1, tiled=True),
        )
        grad_qkv_low = jnp.concatenate(
            [
                join_heads(grad_queries.astype(jnp.bfloat16)),
                join_heads(grad_keys.astype(jnp.bfloat16)),
                join_heads(grad_values.astype(jnp.bfloat16)),
            ],
            axis=1,
        )
        grad_qkv = contract_rows(low_input, grad_qkv_low)
        grad_input = grad_first + lax.psum(contract_cols(grad_qkv_low, qkv_flat), "heads")
        column_sums = jnp.sum(grad_qkv_low.astype(jnp.float32), axis=0)
        empty_row = jnp.zeros((feature_count,), jnp.float32)
        bias_query_grad = lax.dynamic_update_slice_in_dim(
            empty_row, column_sums[:local_width], column_start, 0
        )
        bias_value_grad = lax.dynamic_update_slice_in_dim(
            empty_row, column_sums[2 * local_width :], column_start, 0
        )
        bias_grads = jnp.stack(
            [
                bias_query_grad,
                bias_value_grad,
                HALF_SHARE * jnp.sum(attn_grad.astype(jnp.float32), axis=0),
                HALF_SHARE * jnp.sum(feed_grad.astype(jnp.float32), axis=0),
                HALF_SHARE * grad_shift_one,
                HALF_SHARE * grad_shift_two,
            ]
        )
        gain_grads = HALF_SHARE * jnp.stack([grad_gain_one, grad_gain_two])
        weight_grads = (
            grad_qkv.reshape(feature_count, 3, local_width),
            grad_out_weight,
            grad_glu.reshape(feature_count, 2, local_ff),
            grad_down,
        )
        return (grad_input, weight_grads, bias_grads, gain_grads)

    weight_totals = [
        (
            jnp.zeros((feature_count, 3, local_width), jnp.float32),
            jnp.zeros((feature_count, local_width), jnp.float32),
            jnp.zeros((feature_count, 2, local_ff), jnp.float32),
            jnp.zeros((feature_count, local_ff), jnp.float32),
        )
        for layer_index in range(layer_count)
    ]
    bias_total = jnp.zeros((layer_count, 6, feature_count), jnp.float32)
    gain_total = jnp.zeros((layer_count, 2, feature_count), jnp.float32)
    top_totals = [
        jnp.full((local_heads,), NEGATIVE, jnp.float32) for layer_index in range(layer_count)
    ]
    output_list = []
    grad_list = []
    for micro_index in range(micro_count):
        slot_index = group_index * micro_count + micro_index
        sequence_id = jnp.sum(jnp.where(slot_ids == slot_index, dealing, 0))
        sequence_length = jnp.sum(jnp.where(slot_ids == sequence_id, lengths, 0))
        key_valid = key_positions < sequence_length
        query_valid = query_positions < sequence_length
        row_mask = query_valid[:, None].astype(jnp.float32)
        residual = tokens[micro_index].astype(jnp.float32)
        saved_list = []
        for layer_index in range(layer_count):
            residual, saved_state, top_logits = forward_layer(
                layer_index,
                residual,
                (
                    lax.all_gather(qkv_weight[layer_index], "dp", axis=0, tiled=True),
                    lax.all_gather(out_weight[layer_index], "dp", axis=0, tiled=True),
                    lax.all_gather(glu_weight[layer_index], "dp", axis=0, tiled=True),
                    lax.all_gather(down_weight[layer_index], "dp", axis=0, tiled=True),
                ),
                key_valid,
                query_valid,
            )
            saved_list.append(saved_state)
            top_totals[layer_index] = jnp.maximum(top_totals[layer_index], top_logits)
        output_list.append((residual * row_mask).astype(jnp.bfloat16))
        grad_residual = cotangent[micro_index].astype(jnp.float32) * row_mask
        for layer_index in reversed(range(layer_count)):
            grad_residual, weight_grads, bias_grads, gain_grads = backward_layer(
                layer_index,
                grad_residual,
                saved_list[layer_index],
                (
                    lax.all_gather(qkv_weight[layer_index], "dp", axis=0, tiled=True),
                    lax.all_gather(out_weight[layer_index], "dp", axis=0, tiled=True),
                    lax.all_gather(glu_weight[layer_index], "dp", axis=0, tiled=True),
                    lax.all_gather(down_weight[layer_index], "dp", axis=0, tiled=True),
                ),
                key_valid,
            )
            weight_totals[layer_index] = tuple(
                (total + update for total, update in zip(weight_totals[layer_index], weight_grads))
            )
            bias_total = bias_total.at[layer_index].add(bias_grads)
            gain_total = gain_total.at[layer_index].add(gain_grads)
        grad_list.append(grad_residual)
    stacked = tuple(
        (
            jnp.stack(
                [weight_totals[layer_index][member_index] for layer_index in range(layer_count)]
            )
            for member_index in range(4)
        )
    )
    shard_grads = (
        lax.psum_scatter(stacked[0], "dp", scatter_dimension=1, tiled=True),
        lax.psum_scatter(stacked[1], "dp", scatter_dimension=1, tiled=True),
        lax.psum_scatter(stacked[2], "dp", scatter_dimension=1, tiled=True),
        lax.psum_scatter(stacked[3], "dp", scatter_dimension=1, tiled=True),
        lax.psum_scatter(bias_total, "dp", scatter_dimension=2, tiled=True),
        lax.psum_scatter(gain_total, "dp", scatter_dimension=2, tiled=True),
    )
    grad_qkv, grad_out, grad_glu, grad_down, bias_part, gain_part = lax.psum(
        (
            shard_grads[0],
            shard_grads[1],
            shard_grads[2],
            shard_grads[3],
            shard_grads[4],
            shard_grads[5],
        ),
        "ctx",
    )
    grad_biases, grad_gains = lax.psum((bias_part, gain_part), "heads")
    top_global = lax.pmax(jnp.stack(top_totals), ("dp", "ctx"))
    factor = CLIP_LIMIT / jnp.maximum(top_global, CLIP_LIMIT)
    factor_cols = jnp.repeat(factor, HEAD_DIM, axis=1)
    clipped_qk = (
        qkv_weight[:, :, :2, :].astype(jnp.float32) - STEP_SIZE * grad_qkv[:, :, :2, :]
    ) * factor_cols[:, None, None, :]
    return (
        jnp.stack(output_list),
        jnp.stack(grad_list),
        grad_qkv,
        grad_out,
        grad_glu,
        grad_down,
        grad_biases,
        grad_gains,
        clipped_qk,
    )


def solution(mesh):
    in_specs = (
        P("dp", "ctx", None),
        P("dp", "ctx", None),
        P(),
        P(),
        P(None, "dp", None, "heads"),
        P(None, "dp", "heads"),
        P(None, "dp", None, "heads"),
        P(None, "dp", "heads"),
        P(),
        P(),
    )
    out_specs = (
        P("dp", "ctx", None),
        P("dp", "ctx", None),
        P(None, "dp", None, "heads"),
        P(None, "dp", "heads"),
        P(None, "dp", None, "heads"),
        P(None, "dp", "heads"),
        P(None, None, "dp"),
        P(None, None, "dp"),
        P(None, "dp", None, "heads"),
    )
    return jax.shard_map(shards, mesh=mesh, in_specs=in_specs, out_specs=out_specs, check_vma=False)
```

profile of v0, /device:TPU:0, one launch (start us, length us, event | category | flops | bytes accessed | tf_op | source)
XLA Modules:
  0.0 2197.0 jit_solution(5474925276679920204)
XLA Ops:
  18.5 25.8 %all-gather.1 = bf16[1,768,384]{2,1,0:T(8,128)(2,1)S(1)} all-gather(bf16[1,192,384]{2,1,0:T(8,128)(2,1)S(1)} %get-tuple-element.1453), channel_id=3, replica_groups=mesh['dp'=4,'ctx'=4,'heads'=2] {'dp'}, dimensions={1}, use_global_device_ids=true | all-gather | bytes 737280 | tf_op jit(solution)/shard_map/all_gather | solution.py:303
  44.4 18.6 all-gather.15.cloned.1.call-done
  69.7 9.5 all_gather.84
  79.7 9.5 all_gather.85
  89.6 32.0 %while.130 = (s32[]{:T(128)}, bf16[6,128,64]{1,2,0:T(8,128)(2,1)S(1)}, f32[6,128]{1,0:T(8,128)S(1)}, f32[6]{0:T(128)S(1)}, bf16[6,128,64]{2,1,0:T(8,128)(2,1)S(1...) while((s32[]{:T(128)}, ...), condition=%wide.region_30.31_spmd.clone, body=%wide.region_26.30_spmd.clone.sunk | while | flops 18620800 | bytes 1109309 | solution.py:134
  123.3 9.5 all_gather.33
  133.3 9.0 all_gather.34
  142.8 32.4 %while.128 = (s32[]{:T(128)}, bf16[6,128,64]{1,2,0:T(8,128)(2,1)S(1)}, f32[6,128]{1,0:T(8,128)S(1)}, f32[6]{0:T(128)S(1)}, bf16[6,128,64]{2,1,0:T(8,128)(2,1)S(1...) while((s32[]{:T(128)}, ...), condition=%wide.region_6.7_spmd.clone, body=%wide.region_2.6_spmd.clone.sunk | while | flops 18620800 | bytes 1109309 | solution.py:134
  184.8 10.3 all-reduce.49.cloned.1.call-done
  197.4 90.6 %all-gather.17.cloned.1.call-done = bf16[1,768,2,1536]{3,2,0,1:T(2,128)(2,1)} async-done(((bf16[1,192,2,1536]{3,2,0,1:T(2,128)(2,1)}), bf16[1,768,2,1536]{3,2,0,1:T(2,128)(2,1)}) %all-gather.17.cloned.1.call-update) | async-done | bytes 4718608 | tf_op jit(solution)/shard_map/all_gather | solution.py:304
  297.3 41.7 %all-gather.19.cloned.1.call-done = bf16[1,768,1536]{2,1,0:T(8,128)(2,1)} async-done(((bf16[1,192,1536]{2,1,0:T(8,128)(2,1)}), bf16[1,768,1536]{2,1,0:T(8,128)(2,1)}) %all-gather.19.cloned.1.call-update) | async-done | bytes 2359312 | tf_op jit(solution)/shard_map/all_gather | solution.py:305
  351.7 24.1 %all-gather.5 = bf16[1,768,384]{2,1,0:T(8,128)(2,1)} all-gather(bf16[1,192,384]{2,1,0:T(8,128)(2,1)S(1)} %copy-done.125), channel_id=7, replica_groups=mesh['dp'=4,'ctx'=4,'heads'=2] {'dp'}, dimensions={1}, use_global_device_ids=true | all-gather | bytes 737280 | tf_op jit(solution)/shard_map/all_gather | solution.py:303
  375.8 13.4 all-gather.21.cloned.1.call-done
  391.8 18.5 all-reduce.47.cloned.1.call-done
  417.4 10.3 all_gather.86
  429.6 8.9 all_gather.87
  439.7 43.7 %while.131 = (s32[]{:T(128)}, bf16[6,128,64]{1,2,0:T(8,128)(2,1)S(1)}, f32[6,128]{1,0:T(8,128)S(1)}, f32[6]{0:T(128)S(1)}, bf16[6,128,64]{2,1,0:T(8,128)(2,1)}, ...) while((s32[]{:T(128)}, ...), condition=%wide.region_41.42_spmd.clone, body=%wide.region_37.41_spmd.clone.sunk | while | flops 18620800 | bytes 1110325 | solution.py:134
  486.2 9.7 all_gather.39
  498.6 9.1 all_gather.80
  511.1 43.4 %while.129 = (s32[]{:T(128)}, bf16[6,128,64]{1,2,0:T(8,128)(2,1)S(1)}, f32[6,128]{1,0:T(8,128)S(1)}, f32[6]{0:T(128)S(1)}, bf16[6,128,64]{2,1,0:T(8,128)(2,1)}, ...) while((s32[]{:T(128)}, ...), condition=%wide.region_17.18_spmd.clone, body=%wide.region_13.17_spmd.clone.sunk | while | flops 18620800 | bytes 1110325 | solution.py:134
  563.2 12.9 all-reduce.45.cloned.1.call-done
  588.2 41.8 %all-gather.25.cloned.1.call-done = bf16[1,768,1536]{2,1,0:T(8,128)(2,1)} async-done(((bf16[1,192,1536]{2,1,0:T(8,128)(2,1)}), bf16[1,768,1536]{2,1,0:T(8,128)(2,1)}) %all-gather.25.cloned.1.call-update) | async-done | bytes 2359312 | tf_op jit(solution)/shard_map/all_gather | solution.py:305
  635.4 17.9 all-reduce.43.cloned.1.call-done
  669.0 20.5 all-reduce.41.cloned.1.call-done
  697.6 51.5 %while.134 = (s32[]{:T(128)}, bf16[6,128,64]{1,2,0:T(8,128)(2,1)S(1)}, f32[6,512,64]{1,2,0:T(8,128)}, f32[6,512,64]{1,2,0:T(8,128)}, bf16[6,128,64]{2,1,0:T(8,12...) while((s32[]{:T(128)}, ...), condition=%wide.region_77.78_spmd.clone, body=%wide.region_75.77_spmd.clone.sunk | while | flops 42901888 | bytes 2762393 | solution.py:228
  754.1 47.1 %while.132 = (s32[]{:T(128)}, bf16[6,128,64]{1,2,0:T(8,128)(2,1)S(1)}, f32[6,512,64]{1,2,0:T(8,128)}, f32[6,512,64]{1,2,0:T(8,128)}, bf16[6,128,64]{2,1,0:T(8,12...) while((s32[]{:T(128)}, ...), condition=%wide.region_55.56_spmd.clone, body=%wide.region_53.55_spmd.clone.sunk | while | flops 42901888 | bytes 2762393 | solution.py:228
  806.9 28.7 %reduce-scatter.23.cloned.1.call-done = f32[6,128,64]{1,2,0:T(8,128)} async-done(((f32[6,512,64]{1,2,0:T(8,128)}), f32[6,128,64]{1,2,0:T(8,128)}) %reduce-scatter.23.cloned.1.call-update) | async-done | bytes 196624 | tf_op jit(solution)/shard_map/reduce_scatter | solution.py:233
  838.4 26.9 %reduce-scatter.21.cloned.1.call-done = f32[6,128,64]{1,2,0:T(8,128)} async-done(((f32[6,512,64]{1,2,0:T(8,128)}), f32[6,128,64]{1,2,0:T(8,128)}) %reduce-scatter.21.cloned.1.call-update) | async-done | bytes 196624 | tf_op jit(solution)/shard_map/reduce_scatter | solution.py:232
  869.5 18.9 all-reduce.39.cloned.1.call-done
  901.9 20.5 all-reduce.37.cloned.1.call-done
  929.3 51.1 %while.135 = (s32[]{:T(128)}, bf16[6,128,64]{1,2,0:T(8,128)(2,1)S(1)}, f32[6,512,64]{1,2,0:T(8,128)}, f32[6,512,64]{1,2,0:T(8,128)}, bf16[6,128,64]{2,1,0:T(8,12...) while((s32[]{:T(128)}, ...), condition=%wide.region_88.89_spmd.clone, body=%wide.region_86.88_spmd.clone.sunk | while | flops 42901888 | bytes 2762393 | solution.py:228
  982.7 47.6 %while.133 = (s32[]{:T(128)}, bf16[6,128,64]{1,2,0:T(8,128)(2,1)S(1)}, f32[6,512,64]{1,2,0:T(8,128)S(1)}, f32[6,512,64]{1,2,0:T(8,128)}, bf16[6,128,64]{2,1,0:T(...) while((s32[]{:T(128)}, ...), condition=%wide.region_66.67_spmd.clone, body=%wide.region_64.66_spmd.clone.sunk | while | flops 42901888 | bytes 2762393 | solution.py:228
  1042.6 15.2 reduce-scatter.27.cloned.1.call-done
  1058.8 28.2 %reduce-scatter.25.cloned.1.call-done = f32[6,128,64]{1,2,0:T(8,128)} async-done(((f32[6,512,64]{1,2,0:T(8,128)}), f32[6,128,64]{1,2,0:T(8,128)}) %reduce-scatter.25.cloned.1.call-update) | async-done | bytes 196624 | tf_op jit(solution)/shard_map/reduce_scatter | solution.py:232
  1090.3 26.5 %reduce-scatter.33.cloned.1.call-done = f32[6,128,64]{1,2,0:T(8,128)} async-done(((f32[6,512,64]{1,2,0:T(8,128)}), f32[6,128,64]{1,2,0:T(8,128)}) %reduce-scatter.33.cloned.1.call-update) | async-done | bytes 196624 | tf_op jit(solution)/shard_map/reduce_scatter | solution.py:232
  1124.2 13.6 copy.142
  1146.9 13.3 add.762
  1168.2 13.1 add.760
  1181.3 13.9 copy_bitcast_fusion
  1195.2 24.0 %reshape.1245 = f32[768,6144]{1,0:T(8,128)} reshape(f32[768,2,2,1536]{3,2,1,0:T(2,128)} %copy_bitcast_fusion) | data formatting | bytes 37748736
  1249.0 137.3 %all-reduce.31.cloned.1.call-done = f32[2,768,3,384]{3,0,2,1:T(2,128)} async-done(((f32[2,768,3,384]{3,0,2,1:T(2,128)}), f32[2,768,3,384]{3,0,2,1:T(2,128)}) %all-reduce.31.cloned.1.call-update) | async-done | bytes 7077904
  1389.5 311.9 %reduce-scatter.41.cloned.1.call-done = f32[192,6144]{1,0:T(8,128)} async-done(((f32[768,6144]{1,0:T(8,128)}), f32[192,6144]{1,0:T(8,128)}) %reduce-scatter.41.cloned.1.call-update) | async-done | bytes 4718608
  1701.5 7.1 reshape.1246
  1714.6 38.7 %reduce-scatter.37.cloned.1.call-done = f32[2,192,384]{2,1,0:T(8,128)} async-done(((f32[2,768,384]{2,1,0:T(8,128)}), f32[2,192,384]{2,1,0:T(8,128)}) %reduce-scatter.37.cloned.1.call-update) | async-done | bytes 589840 | tf_op jit(solution)/shard_map/reduce_scatter | solution.py:343
  1753.4 163.2 %reduce-scatter.39.cloned.1.call-done = f32[2,192,1536]{2,1,0:T(8,128)} async-done(((f32[2,768,1536]{2,1,0:T(8,128)}), f32[2,192,1536]{2,1,0:T(8,128)}) %reduce-scatter.39.cloned.1.call-update) | async-done | bytes 2359312 | tf_op jit(solution)/shard_map/reduce_scatter | solution.py:345
  1917.2 41.6 %pmax.7 = f32[2,6]{1,0:T(2,128)S(1)} all-reduce(f32[2,6]{1,0:T(2,128)S(1)} %pad_maximum_fusion.12), channel_id=1, replica_groups=mesh['dp'=4,'ctx'=4,'heads'=2] {'dp','ctx'}, use_global_device_ids=true, to_apply=%region_134.135 | all-reduce | flops 12 | bytes 96 | tf_op jit(solution)/shard_map/pmax | solution.py:361
  1963.1 16.2 all-reduce.9
  1987.1 191.9 %all-reduce.33.cloned.1.call-done = (f32[2,192,3,384]{3,0,2,1:T(2,128)}, f32[2,192,384]{2,1,0:T(8,128)}, f32[2,192,2,1536]{3,2,1,0:T(2,128)}, f32[2,192,1536]{2,1,0:T(8,128)}) async-done(((f32[2,192,3,384]{3,0,2,1:T(2,128)}, f32[2,192,384]{2,1,0:T(8,128)}, f32[2,192,2,1536]{3,2,1,0:T(2,128)}, f32[2,192,1536]{2,1,0:T(8,128)}), (f32[2,192,3,384]{3,0,2,1:T(2,128)}, f32[2,192,384]{2,1,0:T(8,128)}, ...) | async-done | bytes 9437200 | tf_op jit(solution)/shard_map/psum | solution.py:349
  (1211 shorter events, 615.7 us)
Async XLA Ops:
  7.2 55.7 %all-gather.15.cloned.1.call-start = ((), (), s32[]{:S(2)}) async-start(), calls=%async_computation.23 | async-start | bytes 2211840 | tf_op jit(solution)/shard_map/all_gather | solution.py:302
  9.5 185.6 %all-reduce.49.cloned.1.call-start = ((), (), s32[]{:S(2)}) async-start(), calls=%async_computation.41 | async-start | bytes 1572864 | tf_op jit(solution)/shard_map/psum | solution.py:138
  44.4 132.2 %copy-start.11 = (bf16[1,768,384]{2,1,0:T(8,128)(2,1)}, bf16[1,768,384]{2,1,0:T(8,128)(2,1)S(1)}, u32[]{:S(2)}) copy-start(bf16[1,768,384]{2,1,0:T(8,128)(2,1)S(1)} %all-gather.1) | copy-start | bytes 1769476
  121.7 53.5 %copy-start.105 = (bf16[6,128,64]{1,2,0:T(8,128)(2,1)}, bf16[6,128,64]{1,2,0:T(8,128)(2,1)S(1)}, u32[]{:S(2)}) copy-start(bf16[6,128,64]{1,2,0:T(8,128)(2,1)S(1)} %get-tuple-element.599) | copy-start | bytes 294916
  177.7 110.3 %all-gather.17.cloned.1.call-start = ((), (), s32[]{:S(2)}) async-start(), calls=%async_computation.24 | async-start | bytes 5898240 | tf_op jit(solution)/shard_map/all_gather | solution.py:304
  182.5 156.5 %all-gather.19.cloned.1.call-start = ((), (), s32[]{:S(2)}) async-start(), calls=%async_computation.25 | async-start | bytes 2949120 | tf_op jit(solution)/shard_map/all_gather | solution.py:305
  183.7 205.5 %all-gather.21.cloned.1.call-start = ((), (), s32[]{:S(2)}) async-start(), calls=%async_computation.26 | async-start | bytes 2211840 | tf_op jit(solution)/shard_map/all_gather | solution.py:302
  184.3 225.9 %all-reduce.47.cloned.1.call-start = ((), (), s32[]{:S(2)}) async-start(), calls=%async_computation.40 | async-start | bytes 1572864 | tf_op jit(solution)/shard_map/psum | solution.py:144
  196.4 213.8 %copy-start.6 = (f32[128,768]{1,0:T(8,128)}, f32[128,768]{1,0:T(8,128)S(1)}, u32[]{:S(2)}) copy-start(f32[128,768]{1,0:T(8,128)S(1)} %get-tuple-element.1451) | copy-start | bytes 1179652
  197.2 213.0 %copy-start.152 = (f32[128]{0:T(128)}, f32[128]{0:T(128)S(1)}, u32[]{:S(2)}) copy-start(f32[128]{0:T(128)S(1)} %fusion.351) | copy-start | bytes 1540
  197.4 94.1 %copy-start.184 = (f32[128]{0:T(128)}, f32[128]{0:T(128)S(1)}, u32[]{:S(2)}) copy-start(f32[128]{0:T(128)S(1)} %multiply_reduce_fusion.23) | copy-start | bytes 1540
  350.9 206.6 %all-gather.23.cloned.1.call-start = ((), (), s32[]{:S(2)}) async-start(), calls=%async_computation.27 | async-start | bytes 5898240 | tf_op jit(solution)/shard_map/all_gather | solution.py:304
  351.6 224.4 %all-reduce.45.cloned.1.call-start = ((), (), s32[]{:S(2)}) async-start(), calls=%async_computation.39 | async-start | bytes 1572864 | tf_op jit(solution)/shard_map/psum | solution.py:138
  411.7 164.4 %copy-start.4 = (f32[128,768]{1,0:T(8,128)}, f32[128,768]{1,0:T(8,128)S(1)}, u32[]{:S(2)}) copy-start(f32[128,768]{1,0:T(8,128)S(1)} %get-tuple-element.1396) | copy-start | bytes 1179652
  411.9 164.2 %copy-start.156 = (f32[128]{0:T(128)}, f32[128]{0:T(128)S(1)}, u32[]{:S(2)}) copy-start(f32[128]{0:T(128)S(1)} %fusion.352) | copy-start | bytes 1540
  412.7 163.4 %copy-start.159 = (f32[128]{0:T(128)}, f32[128]{0:T(128)S(1)}, u32[]{:S(2)}) copy-start(f32[128]{0:T(128)S(1)} %fusion.348) | copy-start | bytes 1540
  556.7 73.3 %all-gather.25.cloned.1.call-start = ((), (), s32[]{:S(2)}) async-start(), calls=%async_computation.28 | async-start | bytes 2949120 | tf_op jit(solution)/shard_map/all_gather | solution.py:305
  557.4 95.9 %all-reduce.43.cloned.1.call-start = ((), (), s32[]{:S(2)}) async-start(), calls=%async_computation.38 | async-start | bytes 1572864 | tf_op jit(solution)/shard_map/psum | solution.py:144
  578.0 114.0 %copy-start.154 = (f32[128]{0:T(128)}, f32[128]{0:T(128)S(1)}, u32[]{:S(2)}) copy-start(f32[128]{0:T(128)S(1)} %fusion.353) | copy-start | bytes 1540
  635.1 54.4 %all-reduce.41.cloned.1.call-start = ((), (), s32[]{:S(2)}) async-start(), calls=%async_computation.37 | async-start | bytes 1572864 | tf_op jit(solution)/shard_map/psum | solution.py:190
  668.9 132.9 %reduce-scatter.31.cloned.1.call-start = ((), (), s32[]{:S(2)}) async-start(), calls=%async_computation.18 | async-start | bytes 983040 | tf_op jit(solution)/shard_map/reduce_scatter | solution.py:233
  749.1 88.1 %copy-start.77 = (bf16[6,128,64]{1,2,0:T(8,128)(2,1)}, bf16[6,128,64]{1,2,0:T(8,128)(2,1)S(1)}, u32[]{:S(2)}) copy-start(bf16[6,128,64]{1,2,0:T(8,128)(2,1)S(1)} %get-tuple-element.610) | copy-start | bytes 294916
  749.1 56.8 %reduce-scatter.29.cloned.1.call-start = ((), (), s32[]{:S(2)}) async-start(), calls=%async_computation.17 | async-start | bytes 983040 | tf_op jit(solution)/shard_map/reduce_scatter | solution.py:232
  752.1 83.5 %reduce-scatter.23.cloned.1.call-start = ((), (), s32[]{:S(2)}) async-start(), calls=%async_computation.14 | async-start | bytes 983040 | tf_op jit(solution)/shard_map/reduce_scatter | solution.py:233
  801.2 64.1 %reduce-scatter.21.cloned.1.call-start = ((), (), s32[]{:S(2)}) async-start(), calls=%async_computation.13 | async-start | bytes 983040 | tf_op jit(solution)/shard_map/reduce_scatter | solution.py:232
  801.8 86.7 %all-reduce.39.cloned.1.call-start = ((), (), s32[]{:S(2)}) async-start(), calls=%async_computation.36 | async-start | bytes 1572864 | tf_op jit(solution)/shard_map/psum | solution.py:244
  802.8 63.5 %copy-start.72 = (bf16[6,128,64]{1,2,0:T(8,128)(2,1)}, bf16[6,128,64]{1,2,0:T(8,128)(2,1)S(1)}, u32[]{:S(2)}) copy-start(bf16[6,128,64]{1,2,0:T(8,128)(2,1)S(1)} %convert_element_type.323) | copy-start | bytes 294916
  806.9 59.3 %copy-start.74 = (bf16[6,128,64]{1,2,0:T(8,128)(2,1)}, bf16[6,128,64]{1,2,0:T(8,128)(2,1)S(1)}, u32[]{:S(2)}) copy-start(bf16[6,128,64]{1,2,0:T(8,128)(2,1)S(1)} %convert_element_type.322) | copy-start | bytes 294916
  869.1 53.4 %all-reduce.37.cloned.1.call-start = ((), (), s32[]{:S(2)}) async-start(), calls=%async_computation.35 | async-start | bytes 1572864 | tf_op jit(solution)/shard_map/psum | solution.py:190
  901.9 139.7 %reduce-scatter.35.cloned.1.call-start = ((), (), s32[]{:S(2)}) async-start(), calls=%async_computation.20 | async-start | bytes 983040 | tf_op jit(solution)/shard_map/reduce_scatter | solution.py:233
  980.4 77.4 %reduce-scatter.27.cloned.1.call-start = ((), (), s32[]{:S(2)}) async-start(), calls=%async_computation.16 | async-start | bytes 983040 | tf_op jit(solution)/shard_map/reduce_scatter | solution.py:233
  1030.4 56.6 %reduce-scatter.25.cloned.1.call-start = ((), (), s32[]{:S(2)}) async-start(), calls=%async_computation.15 | async-start | bytes 983040 | tf_op jit(solution)/shard_map/reduce_scatter | solution.py:232
  1031.2 85.6 %reduce-scatter.33.cloned.1.call-start = ((), (), s32[]{:S(2)}) async-start(), calls=%async_computation.19 | async-start | bytes 983040 | tf_op jit(solution)/shard_map/reduce_scatter | solution.py:232
  1032.0 354.3 %all-reduce.31.cloned.1.call-start = ((), (), s32[]{:S(2)}) async-start(), calls=%async_computation.32 | async-start | bytes 14155776
  1042.6 75.2 %copy-start.93 = (bf16[6,128,64]{1,2,0:T(8,128)(2,1)}, bf16[6,128,64]{1,2,0:T(8,128)(2,1)S(1)}, u32[]{:S(2)}) copy-start(bf16[6,128,64]{1,2,0:T(8,128)(2,1)S(1)} %convert_element_type.330) | copy-start | bytes 294916
  1058.8 61.8 %copy-start.83 = (bf16[6,128,64]{1,2,0:T(8,128)(2,1)}, bf16[6,128,64]{1,2,0:T(8,128)(2,1)S(1)}, u32[]{:S(2)}) copy-start(bf16[6,128,64]{1,2,0:T(8,128)(2,1)S(1)} %convert_element_type.314) | copy-start | bytes 294916
  1058.8 59.0 %copy-start.98 = (bf16[6,128,64]{1,2,0:T(8,128)(2,1)S(1)}, bf16[6,128,64]{1,2,0:T(8,128)(2,1)}, u32[]{:S(2)}) copy-start(bf16[6,128,64]{1,2,0:T(8,128)(2,1)} %copy-done.97) | copy-start | bytes 294916
  1137.9 563.6 %reduce-scatter.41.cloned.1.call-start = ((), (), s32[]{:S(2)}) async-start(), calls=%async_computation.29 | async-start | bytes 23592960
  1219.2 534.1 %reduce-scatter.37.cloned.1.call-start = ((), (), s32[]{:S(2)}) async-start(), calls=%async_computation.21 | async-start | bytes 2949120 | tf_op jit(solution)/shard_map/reduce_scatter | solution.py:343
  1223.5 693.0 %reduce-scatter.39.cloned.1.call-start = ((), (), s32[]{:S(2)}) async-start(), calls=%async_computation.22 | async-start | bytes 11796480 | tf_op jit(solution)/shard_map/reduce_scatter | solution.py:345
  1233.0 726.8 %reduce-scatter.45.cloned.1.call-start = ((), (), s32[]{:S(2)}) async-start(), calls=%async_computation.31 | async-start | bytes 491520
  1242.4 719.6 %reduce-scatter.43.cloned.1.call-start = ((), (), s32[]{:S(2)}) async-start(), calls=%async_computation.30 | async-start | bytes 491520
  1246.1 737.8 %all-reduce.35.cloned.1.call-start = ((), (), s32[]{:S(2)}) async-start(), calls=%async_computation.34 | async-start | bytes 1572864 | tf_op jit(solution)/shard_map/psum | solution.py:244
  1247.4 931.5 %all-reduce.33.cloned.1.call-start = ((), (), s32[]{:S(2)}) async-start(), calls=%async_computation.33 | async-start | bytes 18874368 | tf_op jit(solution)/shard_map/psum | solution.py:349
  1916.6 67.4 %copy-start.37 = (f32[128,768]{1,0:T(8,128)S(1)}, f32[128,768]{1,0:T(8,128)}, u32[]{:S(2)}) copy-start(f32[128,768]{1,0:T(8,128)} %copy-done.36) | copy-start | bytes 1179652
  1916.6 67.4 %copy-start.175 = (f32[128]{0:T(128)S(1)}, f32[128]{0:T(128)}, u32[]{:S(2)}) copy-start(f32[128]{0:T(128)} %copy-done.174) | copy-start | bytes 1540
  1916.6 68.5 %copy-start.177 = (f32[128]{0:T(128)S(1)}, f32[128]{0:T(128)}, u32[]{:S(2)}) copy-start(f32[128]{0:T(128)} %copy-done.176) | copy-start | bytes 1540
  1986.2 195.7 %slice-start.4 = ((bf16[2,192,3,384]{3,1,2,0:T(8,128)(2,1)}), bf16[2,192,2,384]{3,1,2,0:T(8,128)(2,1)S(1)}, s32[]{:S(2)}) async-start(bf16[2,192,3,384]{3,1,2,0:T(8,128)(2,1)} %param.47), calls=%async_computation.46 | async-start | bytes 1179648 | tf_op jit(solution)/shard_map/slice | solution.py:365
  (193 other events, 1467.6 us)
Sparse Core Ops, SparseCore 0:
  10.2 52.7 all-gather.14
  177.8 17.2 all-reduce.48
  197.3 90.5 all-gather.16
  290.0 48.9 all-gather.18
  340.5 48.5 all-gather.20
  392.1 18.1 all-reduce.46
  412.4 90.5 all-gather.22
  556.8 19.2 all-reduce.44
  578.3 51.6 all-gather.24
  635.2 18.0 all-reduce.42
  669.1 20.4 all-reduce.40
  749.2 27.2 reduce-scatter.30
  779.7 26.2 reduce-scatter.28
  809.5 25.9 reduce-scatter.22
  839.1 26.0 reduce-scatter.20
  869.2 19.2 all-reduce.38
  902.0 20.4 all-reduce.36
  980.6 27.2 reduce-scatter.34
  1030.5 27.2 reduce-scatter.26
  1060.8 26.0 reduce-scatter.24
  1090.7 26.0 reduce-scatter.32
  1138.0 248.2 all-reduce.30
  1388.7 312.6 reduce-scatter.40
  1704.2 49.1 reduce-scatter.36
  1755.7 160.7 reduce-scatter.38
  1918.7 21.4 reduce-scatter.44
  1943.0 18.9 reduce-scatter.42
  1964.9 17.5 all-reduce.34
  1987.5 191.4 all-reduce.32
where the time goes:
time: 2210 us; the launch traced here: 2200 us
  waiting for transfers between devices  1300 us (59%)
  matrix products  306 us (14%)
  local copies, waits for them, and re-layouts  232 us (10%)
  blocking collectives  187 us (8%)
  other arithmetic  148 us (7%)
    unnamed x33, waiting for transfers between devices  454 us
    psum x1, waiting for transfers between devices, shards(): lax.psum((shard_grads[0], shard_grads[1], shard_grads[2], shard_grads[3],...  192 us
    reduce_scatter x1, waiting for transfers between devices, shards(): lax.psum_scatter(stacked[3], 'dp', scatter_dimension=1, tiled=True)  163 us
    unnamed x456, local copies, waits for them, and re-layouts  97.2 us
    all_gather x2, waiting for transfers between devices, shards(): lax.all_gather(glu_weight[layer_index], 'dp', axis=0, tiled=True)  90.6 us
    reduce_scatter x4, waiting for transfers between devices, backward_layer(): lax.psum_scatter(key_terms, 'ctx', scatter_dimension=1, tiled=True)  84.7 us
    all_gather x2, waiting for transfers between devices, shards(): lax.all_gather(down_weight[layer_index], 'dp', axis=0, tiled=True)  83.5 us
    all_gather x2, blocking collectives, shards(): lax.all_gather(out_weight[layer_index], 'dp', axis=0, tiled=True)  49.9 us
  transfers between devices with their start and end apart: 29, of which 24 were waited for; matrix products, arithmetic and copies ran while one was open for 19% of the time, Pallas kernels for 0%

commit v1 on v0

v1 whole, which is shorter than its diff:
```python
import functools
import math

import jax
import jax.numpy as jnp
from jax import lax
from jax.experimental import pallas as pl
from jax.experimental.pallas import tpu as pltpu
from jax.sharding import PartitionSpec as P

HEADS = 12
HEAD_DIM = 64


EPSILON = 1e-12
NEGATIVE = -1e30
CLIP_LIMIT = 4.0
STEP_SIZE = 0.0008
VMEM_LIMIT = 48 * 1024 * 1024


def power_slopes(head_count):
    first_slope = 2.0 ** (-8.0 / head_count)
    return [first_slope ** (position + 1) for position in range(head_count)]


def alibi_slopes(head_count):
    closest = 2 ** int(math.floor(math.log2(head_count)))
    slopes = power_slopes(closest)
    slopes = slopes + power_slopes(2 * closest)[0::2][: head_count - closest]
    return slopes


def dot(a, b):
    return jnp.dot(a, b, preferred_element_type=jnp.float32)


def contract_rows(former, latter):
    return lax.dot_general(
        former, latter, (((0,), (0,)), ((), ())), preferred_element_type=jnp.float32
    )


def contract_cols(former, latter):
    return lax.dot_general(
        former, latter, (((1,), (1,)), ((), ())), preferred_element_type=jnp.float32
    )


def norm_forward(z, gain, shift):
    mean = jnp.mean(z, axis=-1, keepdims=True)
    centred = z - mean
    var = jnp.mean(centred * centred, axis=-1, keepdims=True)
    rstd = lax.rsqrt(var + EPSILON)
    n = centred * rstd
    return n * gain + shift, n, rstd


def norm_backward(grad, n, rstd, gain):
    scaled = grad * gain
    mean_one = jnp.mean(scaled, axis=-1, keepdims=True)
    mean_two = jnp.mean(scaled * n, axis=-1, keepdims=True)
    dz = (scaled - mean_one - n * mean_two) * rstd
    return dz, jnp.sum(grad * n, axis=0), jnp.sum(grad, axis=0)


def cdf(x):
    return 0.5 * (1.0 + lax.erf(x * (0.5**0.5)))


def positions_of(shape, axis, rows, part):
    index = lax.broadcasted_iota(jnp.int32, shape, axis)
    shift = rows.bit_length() - 1
    return (((index >> shift) ^ part) << shift) | (index & (rows - 1))


def attend_kernel(rows, info_ref, slope_ref, qkv_ref, mixed_ref, probs_ref, top_ref):
    total = qkv_ref.shape[0]
    cols = qkv_ref.shape[1] // 3
    part = info_ref[0]
    length = info_ref[1]
    key_pos = positions_of((1, total), 1, rows, part)
    key_ok = key_pos < length
    tops = []
    for h in range(cols // HEAD_DIM):
        lo = h * HEAD_DIM
        key = qkv_ref[:, cols + lo : cols + lo + HEAD_DIM]
        value = qkv_ref[:, 2 * cols + lo : 2 * cols + lo + HEAD_DIM]
        slope = slope_ref[h]
        top = jnp.full((1, 1), NEGATIVE, jnp.float32)
        for b in range(total // rows):
            span = slice(b * rows, (b + 1) * rows)
            query = qkv_ref[span, lo : lo + HEAD_DIM] * jnp.bfloat16(HEAD_DIM**-0.5)
            raw = contract_cols(query, key)
            pos = ((b ^ part) * rows) + lax.broadcasted_iota(jnp.int32, (rows, 1), 0)
            masked = jnp.where(key_ok, raw, NEGATIVE)
            block_top = jnp.max(masked, axis=1, keepdims=True)
            block_top = jnp.where(pos < length, block_top, NEGATIVE)
            top = jnp.maximum(top, jnp.max(block_top, axis=0, keepdims=True))
            distance = jnp.abs(pos - key_pos).astype(jnp.float32)
            scores = masked - slope * distance
            row_max = jnp.max(scores, axis=1, keepdims=True)
            exponent = jnp.exp(scores - row_max)
            totals = jnp.sum(exponent, axis=1, keepdims=True)
            probs = (exponent * (1.0 / totals)).astype(jnp.bfloat16)
            probs_ref[h, span, :] = probs
            mixed_ref[span, lo : lo + HEAD_DIM] = dot(probs, value).astype(jnp.bfloat16)
        tops.append(top)
    lane = lax.broadcasted_iota(jnp.int32, (8, 128), 1)
    packed = jnp.full((8, 128), NEGATIVE, jnp.float32)
    for h, top in enumerate(tops):
        packed = jnp.where(lane == h, top, packed)
    top_ref[...] = packed


def attend(info, slopes, qkv, rows):
    total, width = qkv.shape
    cols = width // 3
    heads = cols // HEAD_DIM
    smem = pl.BlockSpec(memory_space=pltpu.SMEM)
    vmem = pl.BlockSpec(memory_space=pltpu.VMEM)
    return pl.pallas_call(
        functools.partial(attend_kernel, rows),
        out_shape=(
            jax.ShapeDtypeStruct((total, cols), jnp.bfloat16),
            jax.ShapeDtypeStruct((heads, total, total), jnp.bfloat16),
            jax.ShapeDtypeStruct((8, 128), jnp.float32),
        ),
        in_specs=[smem, smem, vmem],
        out_specs=(vmem, vmem, vmem),
        compiler_params=pltpu.CompilerParams(vmem_limit_bytes=VMEM_LIMIT),
        cost_estimate=pl.CostEstimate(
            flops=4 * heads * total * total * HEAD_DIM * 4,
            bytes_accessed=total * width * 2 + heads * total * total * 2,
            transcendentals=heads * total * total,
        ),
        name="attend",
    )(info, slopes, qkv)


def attend_back_kernel(rows, qkv_ref, probs_ref, grad_ref, out_ref, gs_ref):
    total = qkv_ref.shape[0]
    cols = qkv_ref.shape[1] // 3
    scale = HEAD_DIM**-0.5
    for h in range(cols // HEAD_DIM):
        lo = h * HEAD_DIM
        query = qkv_ref[:, lo : lo + HEAD_DIM]
        key = qkv_ref[:, cols + lo : cols + lo + HEAD_DIM]
        value = qkv_ref[:, 2 * cols + lo : 2 * cols + lo + HEAD_DIM]
        grad = grad_ref[:, lo : lo + HEAD_DIM]
        for b in range(total // rows):
            span = slice(b * rows, (b + 1) * rows)
            probs = probs_ref[h, span, :].astype(jnp.float32)
            grad_probs = contract_cols(grad_ref[span, lo : lo + HEAD_DIM], value)
            inner = jnp.sum(grad_probs * probs, axis=1, keepdims=True)
            grad_scores = (probs * (grad_probs - inner)).astype(jnp.bfloat16)
            gs_ref[span, :] = grad_scores
            out_ref[span, lo : lo + HEAD_DIM] = (dot(grad_scores, key) * scale).astype(
                jnp.bfloat16
            )
        out_ref[:, cols + lo : cols + lo + HEAD_DIM] = (
            contract_rows(gs_ref[...], query) * scale
        ).astype(jnp.bfloat16)
        out_ref[:, 2 * cols + lo : 2 * cols + lo + HEAD_DIM] = contract_rows(
            probs_ref[h], grad
        ).astype(jnp.bfloat16)


def attend_back(qkv, probs, grad_mixed, rows):
    total, width = qkv.shape
    heads = probs.shape[0]
    vmem = pl.BlockSpec(memory_space=pltpu.VMEM)
    return pl.pallas_call(
        functools.partial(attend_back_kernel, rows),
        out_shape=jax.ShapeDtypeStruct((total, width), jnp.bfloat16),
        in_specs=[vmem, vmem, vmem],
        out_specs=vmem,
        scratch_shapes=[pltpu.VMEM((total, total), jnp.bfloat16)],
        compiler_params=pltpu.CompilerParams(vmem_limit_bytes=VMEM_LIMIT),
        cost_estimate=pl.CostEstimate(
            flops=8 * heads * total * total * HEAD_DIM * 4,
            bytes_accessed=total * width * 4 + heads * total * total * 2,
            transcendentals=0,
        ),
        name="attend_back",
    )(qkv, probs, grad_mixed)


def shards(
    tokens,
    cotangent,
    lengths,
    dealing,
    qkv_weight,
    out_weight,
    glu_weight,
    down_weight,
    biases,
    gains,
):
    slots, rows, width = tokens.shape
    layers = qkv_weight.shape[0]
    parts = lax.axis_size("ctx")
    cores = lax.axis_size("heads")
    groups = lax.axis_size("dp")
    part = lax.axis_index("ctx")
    core = lax.axis_index("heads")
    group = lax.axis_index("dp")
    local_rows = qkv_weight.shape[1]
    half = qkv_weight.shape[3]
    cols = half * cores // parts
    local_heads = cols // HEAD_DIM
    quarter = glu_weight.shape[3] // parts
    per_core = parts // cores
    home = part // per_core == core
    offset = (part % per_core) * cols

    def swap(x):
        return lax.ppermute(x, "heads", [(j, cores - 1 - j) for j in range(cores)])

    def hop(x, k):
        return lax.ppermute(x, "ctx", [(j, j ^ k) for j in range(parts)])

    def gather(x):
        return [x] + [hop(x, k) for k in range(1, parts)]

    def scatter(blocks):
        total = blocks[0]
        for k in range(1, parts):
            total = total + hop(blocks[k].astype(jnp.bfloat16), k).astype(jnp.float32)
        return total

    def weave(x):
        blocks = jnp.stack(gather(x))
        return [
            lax.dynamic_index_in_dim(blocks, part ^ q, 0, keepdims=False) for q in range(parts)
        ]

    query_key = lax.dynamic_slice_in_dim(qkv_weight[:, :, :2, :], offset, cols, 3)
    value_w = lax.dynamic_slice_in_dim(qkv_weight[:, :, 2, :], offset, cols, 2)
    out_w = lax.dynamic_slice_in_dim(out_weight, offset, cols, 2)
    value_out = jnp.concatenate([value_w, out_w], axis=2)
    query_key = jnp.concatenate([query_key[:, :, 0], query_key[:, :, 1]], axis=2)
    attn_shard = jnp.where(home, query_key, swap(value_out))
    glu_part = lax.dynamic_slice_in_dim(glu_weight, part * quarter, quarter, 3)
    down_part = lax.dynamic_slice_in_dim(down_weight, part * quarter, quarter, 2)
    feed_shard = jnp.concatenate([glu_part[:, :, 0], glu_part[:, :, 1], down_part], axis=2)

    attn_full = []
    feed_full = []
    for l in range(layers):
        if l == 0:
            attn_own = lax.all_gather(attn_shard[l], "dp", axis=0, tiled=True)
            feed_own = lax.all_gather(feed_shard[l], "dp", axis=0, tiled=True)
        else:
            both = lax.all_gather(
                jnp.concatenate([attn_shard[l], feed_shard[l]], axis=1), "dp", axis=0, tiled=True
            )
            attn_own = both[:, : 2 * cols]
            feed_own = both[:, 2 * cols :]
        attn_other = swap(attn_own)
        query_key = jnp.where(home, attn_own, attn_other)
        value_out = jnp.where(home, attn_other, attn_own)
        attn_full.append(
            (jnp.concatenate([query_key, value_out[:, :cols]], axis=1), value_out[:, cols:])
        )
        feed_other = swap(feed_own)
        feed_full.append(
            [(w[:, : 2 * quarter], w[:, 2 * quarter :]) for w in (feed_own, feed_other)]
        )

    slot = group * slots + core
    slot_ids = jnp.arange(lengths.shape[0], dtype=jnp.int32)
    sequence = jnp.sum(jnp.where(slot_ids == slot, dealing, 0))
    length = jnp.sum(jnp.where(slot_ids == sequence, lengths, 0))
    info = jnp.stack([part, length]).astype(jnp.int32)
    slopes = lax.dynamic_slice_in_dim(
        jnp.array(alibi_slopes(HEADS), jnp.float32), part * local_heads, local_heads
    )
    row_pos = part * rows + jnp.arange(rows, dtype=jnp.int32)
    row_mask = (row_pos < length).astype(jnp.float32)[:, None]

    def span(x, b):
        return x[b * rows : (b + 1) * rows]

    residual = lax.dynamic_index_in_dim(tokens, core, 0, keepdims=False).astype(jnp.float32)
    saved = []
    tops = []
    for l in range(layers):
        vectors = biases[l]
        qkv_w, out_w = attn_full[l]
        low = gather(residual.astype(jnp.bfloat16))
        bias = jnp.concatenate(
            [
                lax.dynamic_slice_in_dim(vectors[0], part * cols, cols),
                jnp.zeros((cols,), jnp.float32),
                lax.dynamic_slice_in_dim(vectors[1], part * cols, cols),
            ]
        )
        qkv = jnp.concatenate([(dot(b, qkv_w) + bias).astype(jnp.bfloat16) for b in low])
        mixed, probs, top = attend(info, slopes, qkv, rows)
        tops.append(top[0, :local_heads])
        attention = scatter([contract_cols(span(mixed, b), out_w) for b in range(parts)])
        hidden, n_one, r_one = norm_forward(
            residual + attention + vectors[2], gains[l, 0], vectors[4]
        )
        hidden_low = gather(hidden.astype(jnp.bfloat16))
        gates = [[], []]
        acts = [[], []]
        sums = []
        for b in range(parts):
            total = None
            for side, (glu_w, down_w) in enumerate(feed_full[l]):
                packed = dot(hidden_low[b], glu_w)
                gate, up = packed[:, :quarter], packed[:, quarter:]
                act = (gate * cdf(gate) * up).astype(jnp.bfloat16)
                gates[side].append(packed)
                acts[side].append(act)
                term = contract_cols(act, down_w)
                total = term if total is None else total + term
            sums.append(total)
        feed_out = scatter(sums)
        result, n_two, r_two = norm_forward(
            hidden + feed_out + vectors[3], gains[l, 1], vectors[5]
        )
        saved.append((low, qkv, probs, mixed, n_one, r_one, hidden_low, gates, acts, n_two, r_two))
        residual = result

    outputs = (residual * row_mask).astype(jnp.bfloat16)
    grad = lax.dynamic_index_in_dim(cotangent, core, 0, keepdims=False).astype(jnp.float32)
    grad = grad * row_mask

    bias_rows = [None] * layers
    gain_rows = [None] * layers
    attn_parts = [None] * layers
    feed_parts = [None] * layers
    for l in reversed(range(layers)):
        low, qkv, probs, mixed, n_one, r_one, hidden_low, gates, acts, n_two, r_two = saved[l]
        qkv_w, out_w = attn_full[l]
        grad_second, gain_two, shift_two = norm_backward(grad, n_two, r_two, gains[l, 1])
        feed_low = grad_second.astype(jnp.bfloat16)
        feed_grad = gather(feed_low)
        packed_grads = [[], []]
        sums = []
        for b in range(parts):
            total = None
            for side, (glu_w, down_w) in enumerate(feed_full[l]):
                grad_act = dot(feed_grad[b], down_w)
                packed = gates[side][b]
                gate, up = packed[:, :quarter], packed[:, quarter:]
                phi = cdf(gate)
                slope = phi + gate * (jnp.exp(-0.5 * gate * gate) * (2.0 * math.pi) ** -0.5)
                packed_grad = jnp.concatenate(
                    [grad_act * up * slope, grad_act * (gate * phi)], axis=1
                ).astype(jnp.bfloat16)
                packed_grads[side].append(packed_grad)
                term = contract_cols(packed_grad, glu_w)
                total = term if total is None else total + term
            sums.append(total)
        grad_hidden = grad_second + scatter(sums)
        feed_all = jnp.concatenate(feed_grad)
        hidden_all = jnp.concatenate(hidden_low)
        terms = [
            jnp.concatenate(
                [
                    contract_rows(hidden_all, jnp.concatenate(packed_grads[side])),
                    contract_rows(feed_all, jnp.concatenate(acts[side])),
                ],
                axis=1,
            )
            for side in range(2)
        ]
        feed_total = terms[0] + swap(terms[1].astype(jnp.bfloat16)).astype(jnp.float32)
        feed_parts[l] = lax.psum_scatter(
            feed_total.astype(jnp.bfloat16), "dp", scatter_dimension=0, tiled=True
        )

        grad_first, gain_one, shift_one = norm_backward(grad_hidden, n_one, r_one, gains[l, 0])
        attn_low = grad_first.astype(jnp.bfloat16)
        attn_grad = gather(attn_low)
        attn_all = jnp.concatenate(attn_grad)
        grad_mixed = dot(attn_all, out_w).astype(jnp.bfloat16)
        grad_qkv = attend_back(qkv, probs, grad_mixed, rows)
        grad = grad_first + scatter(
            [contract_cols(span(grad_qkv, b), qkv_w) for b in range(parts)]
        )
        low_all = jnp.concatenate(low)
        qkv_term = contract_rows(low_all, grad_qkv)
        out_term = contract_rows(attn_all, mixed)
        qk_term = qkv_term[:, : 2 * cols]
        vo_term = jnp.concatenate([qkv_term[:, 2 * cols :], out_term], axis=1)
        keep = jnp.where(home, qk_term, vo_term)
        give = jnp.where(home, vo_term, qk_term).astype(jnp.bfloat16)
        attn_total = keep + swap(give).astype(jnp.float32)
        attn_parts[l] = lax.psum_scatter(
            attn_total.astype(jnp.bfloat16), "dp", scatter_dimension=0, tiled=True
        )
        column_sums = jnp.sum(grad_qkv.astype(jnp.float32), axis=0)
        empty = jnp.zeros((width,), jnp.float32)
        bias_rows[l] = jnp.stack(
            [
                lax.dynamic_update_slice_in_dim(empty, column_sums[:cols], part * cols, 0),
                lax.dynamic_update_slice_in_dim(empty, column_sums[2 * cols :], part * cols, 0),
                jnp.sum(attn_low.astype(jnp.float32), axis=0),
                jnp.sum(feed_low.astype(jnp.float32), axis=0),
                shift_one,
                shift_two,
            ]
        )
        gain_rows[l] = jnp.stack([gain_one, gain_two])

    def both_slots(x):
        other = swap(x)
        return jnp.where(core == 0, jnp.stack([x, other]), jnp.stack([other, x]))

    out_tokens = both_slots(outputs)
    grad_tokens = both_slots(grad)

    joint = ("ctx", "heads")

    def share(x, k):
        pairs = [
            (j * cores + j // per_core, (j ^ k) * cores + j // per_core) for j in range(parts)
        ]
        return lax.ppermute(x, joint, pairs)

    qkv_out, out_out, glu_out, down_out = [], [], [], []
    for l in range(layers):
        blocks = weave(feed_parts[l])
        glu_out.append(
            jnp.stack(
                [
                    jnp.concatenate([b[:, s * quarter : (s + 1) * quarter] for b in blocks], axis=1)
                    for s in range(2)
                ],
                axis=1,
            ).astype(jnp.float32)
        )
        down_out.append(
            jnp.concatenate([b[:, 2 * quarter :] for b in blocks], axis=1).astype(jnp.float32)
        )
        whole = jnp.concatenate([attn_parts[l], swap(attn_parts[l])], axis=1)
        shared = [share(whole, k) for k in range(1, parts)]
        same = jnp.where(home, whole, shared[1])
        cross = jnp.where(home, shared[0], shared[2])
        even = part % per_core == 0
        first = jnp.where(even, same, cross).reshape(local_rows, 4, cols)
        second = jnp.where(even, cross, same).reshape(local_rows, 4, cols)
        joined = jnp.concatenate([first, second], axis=2).astype(jnp.float32)
        qkv_out.append(joined[:, :3])
        out_out.append(joined[:, 3])
    grad_qkv = jnp.stack(qkv_out)

    small = jnp.concatenate([jnp.stack(bias_rows), jnp.stack(gain_rows)], axis=1)
    small = lax.psum(small, ("dp", "ctx", "heads"))
    small = lax.dynamic_slice_in_dim(small, group * local_rows, local_rows, 2)

    top = jnp.full((layers, HEADS), NEGATIVE, jnp.float32)
    top = lax.dynamic_update_slice_in_dim(top, jnp.stack(tops), part * local_heads, 1)
    top = lax.pmax(top, ("dp", "ctx", "heads"))
    factor = CLIP_LIMIT / jnp.maximum(top, CLIP_LIMIT)
    factor = lax.dynamic_slice_in_dim(factor, core * (HEADS // cores), HEADS // cores, 1)
    factor_cols = jnp.repeat(factor, HEAD_DIM, axis=1)
    clipped_qk = (
        qkv_weight[:, :, :2, :].astype(jnp.float32) - STEP_SIZE * grad_qkv[:, :, :2, :]
    ) * factor_cols[:, None, None, :]
    return (
        out_tokens,
        grad_tokens,
        grad_qkv,
        jnp.stack(out_out),
        jnp.stack(glu_out),
        jnp.stack(down_out),
        small[:, :6],
        small[:, 6:],
        clipped_qk,
    )


def solution(mesh):
    in_specs = (
        P("dp", "ctx", None),
        P("dp", "ctx", None),
        P(),
        P(),
        P(None, "dp", None, "heads"),
        P(None, "dp", "heads"),
        P(None, "dp", None, "heads"),
        P(None, "dp", "heads"),
        P(),
        P(),
    )
    out_specs = (
        P("dp", "ctx", None),
        P("dp", "ctx", None),
        P(None, "dp", None, "heads"),
        P(None, "dp", "heads"),
        P(None, "dp", None, "heads"),
        P(None, "dp", "heads"),
        P(None, None, "dp"),
        P(None, None, "dp"),
        P(None, "dp", None, "heads"),
    )
    return jax.shard_map(shards, mesh=mesh, in_specs=in_specs, out_specs=out_specs, check_vma=False)
```

time: 2210 us -> 553 us (0.25)
  waiting for transfers between devices: 1300 us -> 131 us
  matrix products: 306 us -> 101 us
  local copies, waits for them, and re-layouts: 232 us -> 47.4 us
  other arithmetic: 148 us -> 35.8 us
  starting transfers between devices: 2.9 us -> 88 us
  blocking collectives: 187 us -> 103 us
    unnamed x33 -> x8, waiting for transfers between devices: 454 us -> 0.12 us
    reduce_scatter x10 -> x2, waiting for transfers between devices: 331 us -> 0.04 us  [shards(): lax.psum_scatter(feed_total.astype(jnp.bfloat16), 'dp', scatter_dimension...]
    psum x9 -> x0, waiting for transfers between devices: 311 us -> none  [the longest x1 192 us: shards(): lax.psum((shard_grads[0], shard_grads[1], shard_grads[2], shard_grads[3],...]
    dot_general x184 -> x42, matrix products: 243 us -> 38.5 us  [dot(): return jnp.dot(a, b, preferred_element_type=jnp.float32)]
    all_gather x6 -> x2, waiting for transfers between devices: 206 us -> 28.4 us  [the longest x1 28.4 us: shards(): lax.all_gather(jnp.concatenate([attn_shard[l], feed_shard[l]], axis=1), '...]
    ppermute x0 -> x73, waiting for transfers between devices: none -> 103 us  [the longest x54 93.6 us: hop(): return lax.ppermute(x, 'ctx', [(j, j ^ k) for j in range(parts)])]
    all_gather x10 -> x1, blocking collectives: 125 us -> 23.1 us  [shards(): attn_own = lax.all_gather(attn_shard[l], 'dp', axis=0, tiled=True)]
    ppermute x0 -> x73, starting transfers between devices: none -> 87.2 us  [the longest x54 67.1 us: hop(): return lax.ppermute(x, 'ctx', [(j, j ^ k) for j in range(parts)])]
  transfers between devices with their start and end apart: 29 -> 79, of which waited for: 24 -> 31; matrix products, arithmetic and copies ran while one was open for 19% -> 27% of each run, Pallas kernels for 0% -> 3%
where the time goes in v1:
time: 553 us; the launch traced here: 544 us
  waiting for transfers between devices  131 us (24%)
  blocking collectives  103 us (19%)
  matrix products  101 us (18%)
  starting transfers between devices  88 us (16%)
  local copies, waits for them, and re-layouts  47.4 us (9%)
  other arithmetic  35.8 us (6%)
  Pallas kernels  18.8 us (3%)
  between operations  18.3 us (3%)
    ppermute x54, waiting for transfers between devices, hop(): return lax.ppermute(x, 'ctx', [(j, j ^ k) for j in range(parts)])  93.6 us
    ppermute x54, starting transfers between devices, hop(): return lax.ppermute(x, 'ctx', [(j, j ^ k) for j in range(parts)])  67.1 us
    dot_general x48, matrix products, contract_cols(): lax.dot_general(former, latter, (((1,), (1,)), ((), ())), preferred_eleme...  46.7 us
    psum x1, blocking collectives, shards(): small = lax.psum(small, ('dp', 'ctx', 'heads'))  41.7 us
    pmax x1, blocking collectives, shards(): top = lax.pmax(top, ('dp', 'ctx', 'heads'))  38.7 us
    dot_general x42, matrix products, dot(): return jnp.dot(a, b, preferred_element_type=jnp.float32)  38.5 us
    unnamed x441, local copies, waits for them, and re-layouts  30.1 us
    all_gather x1, waiting for transfers between devices, shards(): lax.all_gather(jnp.concatenate([attn_shard[l], feed_shard[l]], axis=1), '...  28.4 us
  transfers between devices with their start and end apart: 79, of which 31 were waited for; matrix products, arithmetic and copies ran while one was open for 27% of the time, Pallas kernels for 3%

profile of v1, /device:TPU:0, one launch (start us, length us, event | category | flops | bytes accessed | tf_op | source)
XLA Modules:
  0.0 544.2 jit_solution(567951925186673303)
XLA Ops:
  8.3 3.0 collective-permute-start.2
  15.3 2.7 constant_dynamic-slice_fusion.1
  20.3 23.1 %all-gather = bf16[1,768,384]{2,1,0:T(8,128)(2,1)S(1)} all-gather(bf16[1,192,384]{2,1,0:T(8,128)(2,1)S(1)} %get-tuple-element.193), channel_id=2, replica_groups=mesh['dp'=4,'ctx'=4,'heads'=2] {'dp'}, dimensions={1}, use_global_device_ids=true | all-gather | bytes 737280 | tf_op jit(solution)/shard_map/all_gather | solution.py:253
  52.2 5.0 attend.2
  63.9 2.6 collective-permute-done.5
  66.4 5.5 %collective-permute-done.6 = bf16[128,768]{1,0:T(8,128)(2,1)S(1)} collective-permute-done((bf16[128,768]{1,0:T(8,128)(2,1)S(1)}, bf16[128,768]{1,0:T(8,128)(2,1)S(1)}, u32[]{:S(2)}, u32[]{:S(2)}) %collective-permute-start.6) | collective-permute-done | bytes 196640 | tf_op jit(solution)/shard_map/ppermute | solution.py:222
  78.9 2.6 collective-permute-done.9
  81.9 3.0 collective-permute-done.11
  90.0 28.4 %all-gather.5.cloned.1.call-done = bf16[768,1536]{1,0:T(8,128)(2,1)} async-done(((bf16[192,1536]{1,0:T(8,128)(2,1)}), bf16[768,1536]{1,0:T(8,128)(2,1)}) %all-gather.5.cloned.1.call-update) | async-done | bytes 2359312 | tf_op jit(solution)/shard_map/all_gather | solution.py:256
  136.3 4.5 collective-permute-done.14
  143.9 2.4 collective-permute-start.18
  146.7 3.9 collective-permute-done.16
  154.9 5.0 attend.3
  167.9 38.7 %pmax.7 = f32[2,12]{1,0:T(2,128)} all-reduce(f32[2,12]{1,0:T(2,128)S(1)} %dynamic_update_slice.23), channel_id=1, replica_groups=mesh['dp'=4,'ctx'=4,'heads'=2] {'dp','ctx','heads'}, use_global_device_ids=true, to_apply=%region_37.38 | all-reduce | flops 24 | bytes 192 | tf_op jit(solution)/shard_map/pmax | solution.py:460
  209.3 2.3 collective-permute-start.23
  213.9 3.3 collective-permute-done.23
  217.6 3.7 collective-permute-done.25
  237.7 3.4 collective-permute-done.28
  268.6 3.6 collective-permute-done.35
  272.2 2.8 multiply_reduce_fusion
  289.4 4.4 attend_back.2
  301.4 3.2 collective-permute-done.40
  331.1 3.7 collective-permute-done.47
  334.8 2.6 multiply_reduce_fusion.2
  344.8 3.2 collective-permute-done.49
  350.9 4.4 attend_back.3
  360.6 3.0 fusion.151
  363.7 2.2 fusion.105
  371.8 3.0 fusion.1
  374.9 2.2 copy.228
  383.6 2.2 fusion.74
  390.8 3.2 collective-permute-done.51
  394.0 4.7 collective-permute-done.52
  400.3 41.7 %psum.7 = f32[2,8,768]{2,1,0:T(8,128)S(1)} all-reduce(f32[2,8,768]{2,1,0:T(8,128)S(1)} %maximum_maximum_fusion), channel_id=1, replica_groups=mesh['dp'=4,'ctx'=4,'heads'=2] {'dp','ctx','heads'}, use_global_device_ids=true, to_apply=%region_36.37 | all-reduce | flops 12288 | bytes 98304 | tf_op jit(solution)/shard_map/psum | solution.py:455
  447.4 4.9 collective-permute-start.62
  452.4 2.4 collective-permute-start.63
  456.9 2.4 fusion
  459.3 2.2 copy.226
  466.6 5.5 %collective-permute-start.57 = (bf16[192,768]{0,1:T(8,128)(2,1)S(1)}, bf16[192,768]{0,1:T(8,128)(2,1)S(1)}, u32[]{:S(2)}, u32[]{:S(2)}) collective-permute-start(bf16[192,768]{0,1:T(8,128)(2,1)S(1)} %pad_maximum_fusion.20), channel_id=1, source_target_pairs={{0,4},{2,6},{5,1},{7,3},{8,12},{10,14},{13,9},{15,11},{16,20},{18,... | collective-permute-start | bytes 884744 | tf_op jit(solution)/shard_map/ppermute | solution.py:425
  472.0 2.6 collective-permute-start.58
  477.3 4.4 collective-permute-done.58
  481.7 2.4 collective-permute-done.59
  486.5 2.6 collective-permute-start.71
  494.4 4.1 collective-permute-done.70
  498.5 9.1 %collective-permute-done.71 = bf16[192,1152]{1,0:T(8,128)(2,1)S(1)} collective-permute-done((bf16[192,1152]{1,0:T(8,128)(2,1)}, bf16[192,1152]{1,0:T(8,128)(2,1)S(1)}, u32[]{:S(2)}, u32[]{:S(2)}) %collective-permute-start.71) | collective-permute-done | bytes 442400 | tf_op jit(solution)/shard_map/ppermute | solution.py:222
  511.9 9.7 %collective-permute-done.66 = bf16[192,1152]{1,0:T(8,128)(2,1)S(1)} collective-permute-done((bf16[192,1152]{1,0:T(8,128)(2,1)}, bf16[192,1152]{1,0:T(8,128)(2,1)S(1)}, u32[]{:S(2)}, u32[]{:S(2)}) %collective-permute-start.66) | collective-permute-done | bytes 442400 | tf_op jit(solution)/shard_map/ppermute | solution.py:222
  521.7 6.9 %collective-permute-done.67 = bf16[192,1152]{1,0:T(8,128)(2,1)S(1)} collective-permute-done((bf16[192,1152]{1,0:T(8,128)(2,1)}, bf16[192,1152]{1,0:T(8,128)(2,1)S(1)}, u32[]{:S(2)}, u32[]{:S(2)}) %collective-permute-start.67) | collective-permute-done | bytes 442400 | tf_op jit(solution)/shard_map/ppermute | solution.py:222
  529.6 5.8 %copy.203 = f32[2,192,2,1536]{3,2,1,0:T(2,128)} copy(f32[2,192,2,1536]{3,1,2,0:T(8,128)S(1)} %maximum_convert_fusion) | data formatting | bytes 9437184
  (834 shorter events, 227.6 us)
Async XLA Ops:
  7.2 70.0 %all-gather.7.cloned.1.call-start = ((), (), s32[]{:S(2)}) async-start(), calls=%async_computation.5 | async-start | bytes 2211840 | tf_op jit(solution)/shard_map/all_gather | solution.py:254
  8.3 40.6 %collective-permute-start.2 = (bf16[128,768]{1,0:T(8,128)(2,1)S(1)}, bf16[128,768]{1,0:T(8,128)(2,1)S(1)}, u32[]{:S(2)}, u32[]{:S(2)}) collective-permute-start(bf16[128,768]{1,0:T(8,128)(2,1)S(1)} %dynamic-slice_bitcast_fusion.11), channel_id=1, source_target_pairs={{0,2},{2,0},{4,6},{6,4},{1,3},{3,1},{5,7},{7,5},{8,10},{10,8},{12,... | collective-permute-start | bytes 589832 | tf_op jit(solution)/shard_map/ppermute | solution.py:222
  11.3 38.1 %collective-permute-start.3 = (bf16[128,768]{1,0:T(8,128)(2,1)S(1)}, bf16[128,768]{1,0:T(8,128)(2,1)}, u32[]{:S(2)}, u32[]{:S(2)}) collective-permute-start(bf16[128,768]{1,0:T(8,128)(2,1)S(1)} %dynamic-slice_bitcast_fusion.11), channel_id=1, source_target_pairs={{0,4},{2,6},{4,0},{6,2},{1,5},{3,7},{5,1},{7,3},{8,12},{10,14},{12... | collective-permute-start | bytes 589832 | tf_op jit(solution)/shard_map/ppermute | solution.py:222
  12.8 38.0 %collective-permute-start.4 = (bf16[128,768]{1,0:T(8,128)(2,1)S(1)}, bf16[128,768]{1,0:T(8,128)(2,1)}, u32[]{:S(2)}, u32[]{:S(2)}) collective-permute-start(bf16[128,768]{1,0:T(8,128)(2,1)S(1)} %dynamic-slice_bitcast_fusion.11), channel_id=1, source_target_pairs={{0,6},{2,4},{4,2},{6,0},{1,7},{3,5},{5,3},{7,1},{8,14},{10,12},{12... | collective-permute-start | bytes 589832 | tf_op jit(solution)/shard_map/ppermute | solution.py:222
  19.1 99.3 %all-gather.5.cloned.1.call-start = ((), (), s32[]{:S(2)}) async-start(), calls=%async_computation.4 | async-start | bytes 2949120 | tf_op jit(solution)/shard_map/all_gather | solution.py:256
  60.6 11.3 %collective-permute-start.6 = (bf16[128,768]{1,0:T(8,128)(2,1)S(1)}, bf16[128,768]{1,0:T(8,128)(2,1)S(1)}, u32[]{:S(2)}, u32[]{:S(2)}) collective-permute-start(bf16[128,768]{1,0:T(8,128)(2,1)S(1)} %convolution_convert_fusion.8), channel_id=1, source_target_pairs={{0,4},{2,6},{4,0},{6,2},{1,5},{3,7},{5,1},{7,3},{8,12},{10,14},{12... | collective-permute-start | bytes 589832 | tf_op jit(solution)/shard_map/ppermute | solution.py:222
  62.2 9.7 %collective-permute-start.7 = (bf16[128,768]{1,0:T(8,128)(2,1)S(1)}, bf16[128,768]{1,0:T(8,128)(2,1)}, u32[]{:S(2)}, u32[]{:S(2)}) collective-permute-start(bf16[128,768]{1,0:T(8,128)(2,1)S(1)} %convolution_convert_fusion.7), channel_id=1, source_target_pairs={{0,6},{2,4},{4,2},{6,0},{1,7},{3,5},{5,3},{7,1},{8,14},{10,12},{12... | collective-permute-start | bytes 589832 | tf_op jit(solution)/shard_map/ppermute | solution.py:222
  63.6 378.4 %reduce-scatter.15.cloned.1.call-start = ((), (), s32[]{:S(2)}) async-start(), calls=%async_computation.7 | async-start | bytes 737280
  74.5 10.4 %collective-permute-start.11 = (bf16[128,768]{1,0:T(8,128)(2,1)S(1)}, bf16[128,768]{1,0:T(8,128)(2,1)S(1)}, u32[]{:S(2)}, u32[]{:S(2)}) collective-permute-start(bf16[128,768]{1,0:T(8,128)(2,1)S(1)} %fusion.176), channel_id=1, source_target_pairs={{0,4},{2,6},{4,0},{6,2},{1,5},{3,7},{5,1},{7,3},{8,12},{10,14},{12... | collective-permute-start | bytes 589832 | tf_op jit(solution)/shard_map/ppermute | solution.py:222
  75.8 10.2 %collective-permute-start.13 = (bf16[128,768]{1,0:T(8,128)(2,1)S(1)}, bf16[128,768]{1,0:T(8,128)(2,1)S(1)}, u32[]{:S(2)}, u32[]{:S(2)}) collective-permute-start(bf16[128,768]{1,0:T(8,128)(2,1)S(1)} %fusion.176), channel_id=1, source_target_pairs={{0,6},{2,4},{4,2},{6,0},{1,7},{3,5},{5,3},{7,1},{8,14},{10,12},{12... | collective-permute-start | bytes 589832 | tf_op jit(solution)/shard_map/ppermute | solution.py:222
  77.2 42.6 %collective-permute-start.8 = (bf16[768,1152]{1,0:T(8,128)(2,1)}, bf16[768,1152]{1,0:T(8,128)(2,1)}, u32[]{:S(2)}, u32[]{:S(2)}) collective-permute-start(bf16[768,1152]{1,0:T(8,128)(2,1)} %bitcast.178), channel_id=1, source_target_pairs={{0,1},{1,0},{2,3},{3,2},{4,5},{5,4},{6,7},{7,6},{8,9},{9,8},{10,11... | collective-permute-start | bytes 5308424 | tf_op jit(solution)/shard_map/ppermute | solution.py:219
  119.7 14.1 %collective-permute-start.15 = (bf16[768,384]{0,1:T(8,128)(2,1)S(1)}, bf16[768,384]{0,1:T(8,128)(2,1)S(1)}, u32[]{:S(2)}, u32[]{:S(2)}) collective-permute-start(bf16[768,384]{0,1:T(8,128)(2,1)S(1)} %copy.234), channel_id=1, source_target_pairs={{0,1},{1,0},{2,3},{3,2},{4,5},{5,4},{6,7},{7,6},{8,9},{9,8},{10,11... | collective-permute-start | bytes 1769480 | tf_op jit(solution)/shard_map/ppermute | solution.py:219
  123.7 12.6 %collective-permute-start.10 = (bf16[128,768]{1,0:T(8,128)(2,1)S(1)}, bf16[128,768]{1,0:T(8,128)(2,1)S(1)}, u32[]{:S(2)}, u32[]{:S(2)}) collective-permute-start(bf16[128,768]{1,0:T(8,128)(2,1)S(1)} %fusion.44), channel_id=1, source_target_pairs={{0,2},{2,0},{4,6},{6,4},{1,3},{3,1},{5,7},{7,5},{8,10},{10,8},{12,... | collective-permute-start | bytes 589832 | tf_op jit(solution)/shard_map/ppermute | solution.py:222
  143.3 9.7 %collective-permute-start.17 = (bf16[128,768]{1,0:T(8,128)(2,1)S(1)}, bf16[128,768]{1,0:T(8,128)(2,1)S(1)}, u32[]{:S(2)}, u32[]{:S(2)}) collective-permute-start(bf16[128,768]{1,0:T(8,128)(2,1)S(1)} %fusion.177), channel_id=1, source_target_pairs={{0,4},{2,6},{4,0},{6,2},{1,5},{3,7},{5,1},{7,3},{8,12},{10,14},{12... | collective-permute-start | bytes 589832 | tf_op jit(solution)/shard_map/ppermute | solution.py:222
  143.9 9.6 %collective-permute-start.18 = (bf16[128,768]{1,0:T(8,128)(2,1)S(1)}, bf16[128,768]{1,0:T(8,128)(2,1)S(1)}, u32[]{:S(2)}, u32[]{:S(2)}) collective-permute-start(bf16[128,768]{1,0:T(8,128)(2,1)S(1)} %fusion.177), channel_id=1, source_target_pairs={{0,6},{2,4},{4,2},{6,0},{1,7},{3,5},{5,3},{7,1},{8,14},{10,12},{12... | collective-permute-start | bytes 589832 | tf_op jit(solution)/shard_map/ppermute | solution.py:222
  162.1 44.5 %collective-permute-start.19 = (bf16[128,768]{1,0:T(8,128)(2,1)}, bf16[128,768]{1,0:T(8,128)(2,1)S(1)}, u32[]{:S(2)}, u32[]{:S(2)}) collective-permute-start(bf16[128,768]{1,0:T(8,128)(2,1)} %convolution_convert_fusion.6), channel_id=1, source_target_pairs={{0,2},{2,0},{4,6},{6,4},{1,3},{3,1},{5,7},{7,5},{8,10},{10,8},{12,... | collective-permute-start | bytes 589832 | tf_op jit(solution)/shard_map/ppermute | solution.py:222
  163.6 43.0 %collective-permute-start.20 = (bf16[128,768]{1,0:T(8,128)(2,1)}, bf16[128,768]{1,0:T(8,128)(2,1)S(1)}, u32[]{:S(2)}, u32[]{:S(2)}) collective-permute-start(bf16[128,768]{1,0:T(8,128)(2,1)} %convolution_convert_fusion.5), channel_id=1, source_target_pairs={{0,4},{2,6},{4,0},{6,2},{1,5},{3,7},{5,1},{7,3},{8,12},{10,14},{12... | collective-permute-start | bytes 589832 | tf_op jit(solution)/shard_map/ppermute | solution.py:222
  164.3 42.4 %collective-permute-start.21 = (bf16[128,768]{1,0:T(8,128)(2,1)S(1)}, bf16[128,768]{1,0:T(8,128)(2,1)}, u32[]{:S(2)}, u32[]{:S(2)}) collective-permute-start(bf16[128,768]{1,0:T(8,128)(2,1)S(1)} %convolution_convert_fusion.4), channel_id=1, source_target_pairs={{0,6},{2,4},{4,2},{6,0},{1,7},{3,5},{5,3},{7,1},{8,14},{10,12},{12... | collective-permute-start | bytes 589832 | tf_op jit(solution)/shard_map/ppermute | solution.py:222
  167.8 55.3 %collective-permute-start.22 = (bf16[768,1152]{1,0:T(8,128)(2,1)}, bf16[768,1152]{1,0:T(8,128)(2,1)}, u32[]{:S(2)}, u32[]{:S(2)}) collective-permute-start(bf16[768,1152]{1,0:T(8,128)(2,1)} %slice.614), channel_id=1, source_target_pairs={{0,1},{1,0},{2,3},{3,2},{4,5},{5,4},{6,7},{7,6},{8,9},{9,8},{10,11... | collective-permute-start | bytes 5308424 | tf_op jit(solution)/shard_map/ppermute | solution.py:219
  211.6 9.7 %collective-permute-start.25 = (bf16[128,768]{1,0:T(8,128)(2,1)S(1)}, bf16[128,768]{1,0:T(8,128)(2,1)S(1)}, u32[]{:S(2)}, u32[]{:S(2)}) collective-permute-start(bf16[128,768]{1,0:T(8,128)(2,1)S(1)} %fusion.178), channel_id=1, source_target_pairs={{0,4},{2,6},{4,0},{6,2},{1,5},{3,7},{5,1},{7,3},{8,12},{10,14},{12... | collective-permute-start | bytes 589832 | tf_op jit(solution)/shard_map/ppermute | solution.py:222
  226.2 11.5 %collective-permute-start.24 = (bf16[128,768]{1,0:T(8,128)(2,1)S(1)}, bf16[128,768]{1,0:T(8,128)(2,1)S(1)}, u32[]{:S(2)}, u32[]{:S(2)}) collective-permute-start(bf16[128,768]{1,0:T(8,128)(2,1)S(1)} %fusion.47), channel_id=1, source_target_pairs={{0,2},{2,0},{4,6},{6,4},{1,3},{3,1},{5,7},{7,5},{8,10},{10,8},{12,... | collective-permute-start | bytes 589832 | tf_op jit(solution)/shard_map/ppermute | solution.py:222
  246.3 9.8 %collective-permute-start.32 = (bf16[128,768]{1,0:T(8,128)(2,1)S(1)}, bf16[128,768]{1,0:T(8,128)(2,1)S(1)}, u32[]{:S(2)}, u32[]{:S(2)}) collective-permute-start(bf16[128,768]{1,0:T(8,128)(2,1)S(1)} %get-tuple-element.110), channel_id=1, source_target_pairs={{0,4},{2,6},{4,0},{6,2},{1,5},{3,7},{5,1},{7,3},{8,12},{10,14},{12... | collective-permute-start | bytes 589832 | tf_op jit(solution)/shard_map/ppermute | solution.py:222
  247.3 14.1 %collective-permute-start.34 = (bf16[128,768]{1,0:T(8,128)(2,1)S(1)}, bf16[128,768]{1,0:T(8,128)(2,1)S(1)}, u32[]{:S(2)}, u32[]{:S(2)}) collective-permute-start(bf16[128,768]{1,0:T(8,128)(2,1)S(1)} %get-tuple-element.110), channel_id=1, source_target_pairs={{0,6},{2,4},{4,2},{6,0},{1,7},{3,5},{5,3},{7,1},{8,14},{10,12},{12... | collective-permute-start | bytes 589832 | tf_op jit(solution)/shard_map/ppermute | solution.py:222
  255.0 13.5 %collective-permute-start.31 = (bf16[128,768]{1,0:T(8,128)(2,1)S(1)}, bf16[128,768]{1,0:T(8,128)(2,1)S(1)}, u32[]{:S(2)}, u32[]{:S(2)}) collective-permute-start(bf16[128,768]{1,0:T(8,128)(2,1)S(1)} %fusion.38), channel_id=1, source_target_pairs={{0,2},{2,0},{4,6},{6,4},{1,3},{3,1},{5,7},{7,5},{8,10},{10,8},{12,... | collective-permute-start | bytes 589832 | tf_op jit(solution)/shard_map/ppermute | solution.py:222
  281.4 90.4 %collective-permute-start.69 = (bf16[768,1152]{0,1:T(8,128)(2,1)}, bf16[768,1152]{0,1:T(8,128)(2,1)}, u32[]{:S(2)}, u32[]{:S(2)}) collective-permute-start(bf16[768,1152]{0,1:T(8,128)(2,1)} %pad_maximum_fusion.3), channel_id=1, source_target_pairs={{0,1},{1,0},{2,3},{3,2},{4,5},{5,4},{6,7},{7,6},{8,9},{9,8},{10,11... | collective-permute-start | bytes 5308424 | tf_op jit(solution)/shard_map/ppermute | solution.py:219
  299.9 42.7 %collective-permute-start.60 = (bf16[768,384]{0,1:T(8,128)(2,1)S(1)}, bf16[768,384]{0,1:T(8,128)(2,1)S(1)}, u32[]{:S(2)}, u32[]{:S(2)}) collective-permute-start(bf16[768,384]{0,1:T(8,128)(2,1)S(1)} %select_convert_fusion), channel_id=1, source_target_pairs={{0,1},{1,0},{2,3},{3,2},{4,5},{5,4},{6,7},{7,6},{8,9},{9,8},{10,11... | collective-permute-start | bytes 1769480 | tf_op jit(solution)/shard_map/ppermute | solution.py:219
  307.4 10.1 %collective-permute-start.44 = (bf16[128,768]{1,0:T(8,128)(2,1)S(1)}, bf16[128,768]{1,0:T(8,128)(2,1)S(1)}, u32[]{:S(2)}, u32[]{:S(2)}) collective-permute-start(bf16[128,768]{1,0:T(8,128)(2,1)S(1)} %get-tuple-element.104), channel_id=1, source_target_pairs={{0,4},{2,6},{4,0},{6,2},{1,5},{3,7},{5,1},{7,3},{8,12},{10,14},{12... | collective-permute-start | bytes 589832 | tf_op jit(solution)/shard_map/ppermute | solution.py:222
  308.6 15.3 %collective-permute-start.46 = (bf16[128,768]{1,0:T(8,128)(2,1)S(1)}, bf16[128,768]{1,0:T(8,128)(2,1)S(1)}, u32[]{:S(2)}, u32[]{:S(2)}) collective-permute-start(bf16[128,768]{1,0:T(8,128)(2,1)S(1)} %get-tuple-element.104), channel_id=1, source_target_pairs={{0,6},{2,4},{4,2},{6,0},{1,7},{3,5},{5,3},{7,1},{8,14},{10,12},{12... | collective-permute-start | bytes 589832 | tf_op jit(solution)/shard_map/ppermute | solution.py:222
  316.5 14.6 %collective-permute-start.43 = (bf16[128,768]{1,0:T(8,128)(2,1)S(1)}, bf16[128,768]{1,0:T(8,128)(2,1)S(1)}, u32[]{:S(2)}, u32[]{:S(2)}) collective-permute-start(bf16[128,768]{1,0:T(8,128)(2,1)S(1)} %fusion.41), channel_id=1, source_target_pairs={{0,2},{2,0},{4,6},{6,4},{1,3},{3,1},{5,7},{7,5},{8,10},{10,8},{12,... | collective-permute-start | bytes 589832 | tf_op jit(solution)/shard_map/ppermute | solution.py:222
  343.9 117.7 %reduce-scatter.13.cloned.1.call-start = ((), (), s32[]{:S(2)}) async-start(), calls=%async_computation.6 | async-start | bytes 737280
  368.5 116.7 %reduce-scatter.19.cloned.1.call-start = ((), (), s32[]{:S(2)}) async-start(), calls=%async_computation.9 | async-start | bytes 2211840 | tf_op jit(solution)/shard_map/reduce_scatter | solution.py:374
  377.3 131.0 %reduce-scatter.17.cloned.1.call-start = ((), (), s32[]{:S(2)}) async-start(), calls=%async_computation.8 | async-start | bytes 2211840 | tf_op jit(solution)/shard_map/reduce_scatter | solution.py:374
  381.4 75.5 %collective-permute-start.65 = (bf16[768,1152]{0,1:T(8,128)(2,1)}, bf16[768,1152]{0,1:T(8,128)(2,1)S(1)}, u32[]{:S(2)}, u32[]{:S(2)}) collective-permute-start(bf16[768,1152]{0,1:T(8,128)(2,1)} %pad_maximum_fusion.1), channel_id=1, source_target_pairs={{0,1},{1,0},{2,3},{3,2},{4,5},{5,4},{6,7},{7,6},{8,9},{9,8},{10,11... | collective-permute-start | bytes 5308424 | tf_op jit(solution)/shard_map/ppermute | solution.py:219
  387.8 11.0 %collective-permute-start.52 = (bf16[128,768]{1,0:T(8,128)(2,1)S(1)}, bf16[128,768]{1,0:T(8,128)(2,1)S(1)}, u32[]{:S(2)}, u32[]{:S(2)}) collective-permute-start(bf16[128,768]{1,0:T(8,128)(2,1)S(1)} %convolution_convert_fusion.11), channel_id=1, source_target_pairs={{0,4},{2,6},{4,0},{6,2},{1,5},{3,7},{5,1},{7,3},{8,12},{10,14},{12... | collective-permute-start | bytes 589832 | tf_op jit(solution)/shard_map/ppermute | solution.py:222
  389.1 9.7 %collective-permute-start.53 = (bf16[128,768]{1,0:T(8,128)(2,1)S(1)}, bf16[128,768]{1,0:T(8,128)(2,1)S(1)}, u32[]{:S(2)}, u32[]{:S(2)}) collective-permute-start(bf16[128,768]{1,0:T(8,128)(2,1)S(1)} %convolution_convert_fusion.10), channel_id=1, source_target_pairs={{0,6},{2,4},{4,2},{6,0},{1,7},{3,5},{5,3},{7,1},{8,14},{10,12},{12... | collective-permute-start | bytes 589832 | tf_op jit(solution)/shard_map/ppermute | solution.py:222
  399.9 44.6 %collective-permute-start.54 = (f32[128,768]{1,0:T(8,128)}, f32[128,768]{1,0:T(8,128)S(1)}, u32[]{:S(2)}, u32[]{:S(2)}) collective-permute-start(f32[128,768]{1,0:T(8,128)} %fusion.30), channel_id=1, source_target_pairs={{0,1},{1,0},{2,3},{3,2},{4,5},{5,4},{6,7},{7,6},{8,9},{9,8},{10,11... | collective-permute-start | bytes 1179656 | tf_op jit(solution)/shard_map/ppermute | solution.py:219
  447.4 15.3 %collective-permute-start.62 = (bf16[192,768]{0,1:T(8,128)(2,1)}, bf16[192,768]{0,1:T(8,128)(2,1)}, u32[]{:S(2)}, u32[]{:S(2)}) collective-permute-start(bf16[192,768]{0,1:T(8,128)(2,1)} %pad_maximum_fusion.21), channel_id=1, source_target_pairs={{0,4},{2,6},{5,1},{7,3},{8,12},{10,14},{13,9},{15,11},{16,20},{18,... | collective-permute-start | bytes 884744 | tf_op jit(solution)/shard_map/ppermute | solution.py:425
  452.4 10.4 %collective-permute-start.63 = (bf16[192,768]{0,1:T(8,128)(2,1)}, bf16[192,768]{0,1:T(8,128)(2,1)}, u32[]{:S(2)}, u32[]{:S(2)}) collective-permute-start(bf16[192,768]{0,1:T(8,128)(2,1)} %pad_maximum_fusion.21), channel_id=1, source_target_pairs={{0,2},{2,0},{5,7},{7,5},{8,10},{10,8},{13,15},{15,13},{16,18},{18,... | collective-permute-start | bytes 884744 | tf_op jit(solution)/shard_map/ppermute | solution.py:425
  454.8 9.8 %collective-permute-start.64 = (bf16[192,768]{0,1:T(8,128)(2,1)}, bf16[192,768]{0,1:T(8,128)(2,1)}, u32[]{:S(2)}, u32[]{:S(2)}) collective-permute-start(bf16[192,768]{0,1:T(8,128)(2,1)} %pad_maximum_fusion.21), channel_id=1, source_target_pairs={{0,6},{2,4},{5,3},{7,1},{8,14},{10,12},{13,11},{15,9},{16,22},{18,... | collective-permute-start | bytes 884744 | tf_op jit(solution)/shard_map/ppermute | solution.py:425
  466.6 10.7 %collective-permute-start.57 = (bf16[192,768]{0,1:T(8,128)(2,1)S(1)}, bf16[192,768]{0,1:T(8,128)(2,1)S(1)}, u32[]{:S(2)}, u32[]{:S(2)}) collective-permute-start(bf16[192,768]{0,1:T(8,128)(2,1)S(1)} %pad_maximum_fusion.20), channel_id=1, source_target_pairs={{0,4},{2,6},{5,1},{7,3},{8,12},{10,14},{13,9},{15,11},{16,20},{18,... | collective-permute-start | bytes 884744 | tf_op jit(solution)/shard_map/ppermute | solution.py:425
  472.0 9.7 %collective-permute-start.58 = (bf16[192,768]{0,1:T(8,128)(2,1)S(1)}, bf16[192,768]{0,1:T(8,128)(2,1)S(1)}, u32[]{:S(2)}, u32[]{:S(2)}) collective-permute-start(bf16[192,768]{0,1:T(8,128)(2,1)S(1)} %pad_maximum_fusion.20), channel_id=1, source_target_pairs={{0,2},{2,0},{5,7},{7,5},{8,10},{10,8},{13,15},{15,13},{16,18},{18,... | collective-permute-start | bytes 884744 | tf_op jit(solution)/shard_map/ppermute | solution.py:425
  474.6 9.5 %collective-permute-start.59 = (bf16[192,768]{0,1:T(8,128)(2,1)S(1)}, bf16[192,768]{0,1:T(8,128)(2,1)S(1)}, u32[]{:S(2)}, u32[]{:S(2)}) collective-permute-start(bf16[192,768]{0,1:T(8,128)(2,1)S(1)} %pad_maximum_fusion.20), channel_id=1, source_target_pairs={{0,6},{2,4},{5,3},{7,1},{8,14},{10,12},{13,11},{15,9},{16,22},{18,... | collective-permute-start | bytes 884744 | tf_op jit(solution)/shard_map/ppermute | solution.py:425
  485.1 13.4 %collective-permute-start.70 = (bf16[192,1152]{1,0:T(8,128)(2,1)}, bf16[192,1152]{1,0:T(8,128)(2,1)S(1)}, u32[]{:S(2)}, u32[]{:S(2)}) collective-permute-start(bf16[192,1152]{1,0:T(8,128)(2,1)} %reduce-scatter.19.cloned.1.call-done), channel_id=1, source_target_pairs={{0,2},{2,0},{4,6},{6,4},{1,3},{3,1},{5,7},{7,5},{8,10},{10,8},{12,... | collective-permute-start | bytes 1327112 | tf_op jit(solution)/shard_map/ppermute | solution.py:222
  486.5 21.1 %collective-permute-start.71 = (bf16[192,1152]{1,0:T(8,128)(2,1)}, bf16[192,1152]{1,0:T(8,128)(2,1)S(1)}, u32[]{:S(2)}, u32[]{:S(2)}) collective-permute-start(bf16[192,1152]{1,0:T(8,128)(2,1)} %reduce-scatter.19.cloned.1.call-done), channel_id=1, source_target_pairs={{0,4},{2,6},{4,0},{6,2},{1,5},{3,7},{5,1},{7,3},{8,12},{10,14},{12... | collective-permute-start | bytes 1327112 | tf_op jit(solution)/shard_map/ppermute | solution.py:222
  489.1 18.5 %collective-permute-start.72 = (bf16[192,1152]{1,0:T(8,128)(2,1)}, bf16[192,1152]{1,0:T(8,128)(2,1)S(1)}, u32[]{:S(2)}, u32[]{:S(2)}) collective-permute-start(bf16[192,1152]{1,0:T(8,128)(2,1)} %reduce-scatter.19.cloned.1.call-done), channel_id=1, source_target_pairs={{0,6},{2,4},{4,2},{6,0},{1,7},{3,5},{5,3},{7,1},{8,14},{10,12},{12... | collective-permute-start | bytes 1327112 | tf_op jit(solution)/shard_map/ppermute | solution.py:222
  508.3 13.4 %collective-permute-start.66 = (bf16[192,1152]{1,0:T(8,128)(2,1)}, bf16[192,1152]{1,0:T(8,128)(2,1)S(1)}, u32[]{:S(2)}, u32[]{:S(2)}) collective-permute-start(bf16[192,1152]{1,0:T(8,128)(2,1)} %reduce-scatter.17.cloned.1.call-done), channel_id=1, source_target_pairs={{0,2},{2,0},{4,6},{6,4},{1,3},{3,1},{5,7},{7,5},{8,10},{10,8},{12,... | collective-permute-start | bytes 1327112 | tf_op jit(solution)/shard_map/ppermute | solution.py:222
  508.7 19.8 %collective-permute-start.67 = (bf16[192,1152]{1,0:T(8,128)(2,1)}, bf16[192,1152]{1,0:T(8,128)(2,1)S(1)}, u32[]{:S(2)}, u32[]{:S(2)}) collective-permute-start(bf16[192,1152]{1,0:T(8,128)(2,1)} %reduce-scatter.17.cloned.1.call-done), channel_id=1, source_target_pairs={{0,4},{2,6},{4,0},{6,2},{1,5},{3,7},{5,1},{7,3},{8,12},{10,14},{12... | collective-permute-start | bytes 1327112 | tf_op jit(solution)/shard_map/ppermute | solution.py:222
  510.1 18.4 %collective-permute-start.68 = (bf16[192,1152]{1,0:T(8,128)(2,1)}, bf16[192,1152]{1,0:T(8,128)(2,1)S(1)}, u32[]{:S(2)}, u32[]{:S(2)}) collective-permute-start(bf16[192,1152]{1,0:T(8,128)(2,1)} %reduce-scatter.17.cloned.1.call-done), channel_id=1, source_target_pairs={{0,6},{2,4},{4,2},{6,0},{1,7},{3,5},{5,3},{7,1},{8,14},{10,12},{12... | collective-permute-start | bytes 1327112 | tf_op jit(solution)/shard_map/ppermute | solution.py:222
  (247 other events, 1822.4 us)
Sparse Core Ops, SparseCore 0:
  19.2 46.1 all-gather.6
  67.5 50.7 all-gather.4
  344.0 20.9 reduce-scatter.14
  368.6 20.8 reduce-scatter.12
  392.2 37.4 reduce-scatter.18
  461.7 36.6 reduce-scatter.16

commit v2 on v1

v2 whole, which is shorter than its diff:
```python
import functools
import math

import jax
import jax.numpy as jnp
from jax import lax
from jax.experimental import pallas as pl
from jax.experimental.pallas import tpu as pltpu
from jax.sharding import PartitionSpec as P

HEADS = 12
HEAD_DIM = 64


EPSILON = 1e-12
NEGATIVE = -1e30
CLIP_LIMIT = 4.0
STEP_SIZE = 0.0008
MIB = 1024 * 1024


def power_slopes(head_count):
    first_slope = 2.0 ** (-8.0 / head_count)
    return [first_slope ** (position + 1) for position in range(head_count)]


def alibi_slopes(head_count):
    closest = 2 ** int(math.floor(math.log2(head_count)))
    slopes = power_slopes(closest)
    slopes = slopes + power_slopes(2 * closest)[0::2][: head_count - closest]
    return slopes


def dot(a, b):
    return jnp.dot(a, b, preferred_element_type=jnp.float32)


def contract_rows(former, latter):
    return lax.dot_general(
        former, latter, (((0,), (0,)), ((), ())), preferred_element_type=jnp.float32
    )


def contract_cols(former, latter):
    return lax.dot_general(
        former, latter, (((1,), (1,)), ((), ())), preferred_element_type=jnp.float32
    )


def low(x):
    return x.astype(jnp.bfloat16)


def wide(x):
    return x.astype(jnp.float32)


def positions_of(shape, axis, rows, part):
    index = lax.broadcasted_iota(jnp.int32, shape, axis)
    shift = rows.bit_length() - 1
    return (((index >> shift) ^ part) << shift) | (index & (rows - 1))


def join(refs):
    return jnp.concatenate([r[...] for r in refs], axis=0)


def call(body, name, outs, *args, scratch=(), flops=0, exps=0, limit=16, alias=None):
    spaces = {"s": pltpu.SMEM, "h": pltpu.HBM, "d": pl.ANY, "v": pltpu.VMEM}
    args = [a if isinstance(a, tuple) else ("v", a) for a in args]
    outs = [o if len(o) == 3 else (*o, "v") for o in outs]
    values = [
        pltpu.with_memory_space_constraint(a[1], pltpu.HBM) if a[0] == "h" else a[1] for a in args
    ]
    shapes = tuple(
        pltpu.HBM(o[0], o[1]) if o[2] == "h" else jax.ShapeDtypeStruct(o[0], o[1]) for o in outs
    )
    moved = sum(v.size * v.dtype.itemsize for v in values)
    moved += sum(math.prod(o[0]) * jnp.dtype(o[1]).itemsize for o in outs)
    return pl.pallas_call(
        body,
        out_shape=shapes,
        in_specs=[pl.BlockSpec(memory_space=spaces[a[0]]) for a in args],
        out_specs=tuple(pl.BlockSpec(memory_space=spaces[o[2]]) for o in outs),
        scratch_shapes=list(scratch),
        input_output_aliases=alias or {},
        compiler_params=pltpu.CompilerParams(vmem_limit_bytes=limit * MIB),
        cost_estimate=pl.CostEstimate(flops=flops, bytes_accessed=moved, transcendentals=exps),
        name=name,
    )(*values)


def start(source, target, sem):
    copy = pltpu.make_async_copy(source, target, sem)
    copy.start()
    return copy


def bf16(*shape):
    return pltpu.VMEM(shape, jnp.bfloat16)


def f32(*shape):
    return pltpu.VMEM(shape, jnp.float32)


def sems(count):
    return pltpu.SemaphoreType.DMA((count,))


def pick(flag, one, two):
    chosen = jnp.full(one.shape, flag, jnp.int32) == 1
    return jnp.where(chosen, wide(one[...]), wide(two[...])).astype(jnp.bfloat16)


def attend_kernel(count, at, info, slope_ref, x0, x1, x2, x3, own, other, bias, *refs):
    xs_out, qkvm_out, probs_out, w_out, top_ref = refs[:5]
    sends = refs[5:9]
    xs, qkvm, probs_ref, w, own_ref, other_ref, sem = refs[9:]
    columns = slice(at, at + own_ref.shape[1])
    one = start(own.at[:, columns], own_ref, sem.at[10])
    two = start(other.at[:, columns], other_ref, sem.at[11])
    blocks = (x0, x1, x2, x3)
    rows = x0.shape[0]
    total = rows * len(blocks)
    cols = own_ref.shape[1] // 2
    part, length, home = info[0], info[1], info[2]
    for b, ref in enumerate(blocks):
        xs[b * rows : (b + 1) * rows, :] = ref[...]
    copies = [start(xs, xs_out, sem.at[0])]
    height = own_ref.shape[0] // count
    one.wait()
    two.wait()
    for k in range(count):
        span = slice(k * height, (k + 1) * height)
        place = pl.ds(pl.multiple_of((info[3] ^ k) * height, height), height)
        w[place, : 2 * cols] = pick(home, own_ref[span, :], other_ref[span, :])
        w[place, 2 * cols :] = pick(home, other_ref[span, :], own_ref[span, :])
    copies.append(start(w, w_out, sem.at[9]))
    x = xs[...]
    qkvm[:, : 3 * cols] = low(dot(x, w[:, : 3 * cols]) + bias[...])
    out_w = w[:, 3 * cols :]
    key_pos = positions_of((1, total), 1, rows, part)
    key_ok = key_pos < length
    heads = cols // HEAD_DIM
    tops = [jnp.full((1, 1), NEGATIVE, jnp.float32)] * heads
    for b in range(len(blocks)):
        span = slice(b * rows, (b + 1) * rows)
        pos = ((b ^ part) * rows) + lax.broadcasted_iota(jnp.int32, (rows, 1), 0)
        distance = jnp.abs(pos - key_pos).astype(jnp.float32)
        for h in range(heads):
            lo = h * HEAD_DIM
            key = qkvm[:, cols + lo : cols + lo + HEAD_DIM]
            value = qkvm[:, 2 * cols + lo : 2 * cols + lo + HEAD_DIM]
            query = qkvm[span, lo : lo + HEAD_DIM] * jnp.bfloat16(HEAD_DIM**-0.5)
            masked = jnp.where(key_ok, contract_cols(query, key), NEGATIVE)
            block_top = jnp.max(masked, axis=1, keepdims=True)
            block_top = jnp.where(pos < length, block_top, NEGATIVE)
            tops[h] = jnp.maximum(tops[h], jnp.max(block_top, axis=0, keepdims=True))
            scores = masked - slope_ref[h] * distance
            row_max = jnp.max(scores, axis=1, keepdims=True)
            exponent = jnp.exp(scores - row_max)
            totals = jnp.sum(exponent, axis=1, keepdims=True)
            probs = low(exponent * (1.0 / totals))
            probs_ref[h, span, :] = probs
            qkvm[span, 3 * cols + lo : 3 * cols + lo + HEAD_DIM] = low(dot(probs, value))
        copies.append(
            start(probs_ref.at[:, span, :], probs_out.at[:, span, :], sem.at[1 + 2 * b])
        )
        copies.append(start(qkvm.at[span, :], qkvm_out.at[span, :], sem.at[2 + 2 * b]))
        sends[b][...] = low(contract_cols(qkvm[span, 3 * cols :], out_w))
    lane = lax.broadcasted_iota(jnp.int32, (8, 128), 1)
    packed = jnp.full((8, 128), NEGATIVE, jnp.float32)
    for h, top in enumerate(tops):
        packed = jnp.where(lane == h, top, packed)
    top_ref[...] = packed
    for copy in copies:
        copy.wait()


def attend(info, slopes, blocks, own, other, at, bias, count):
    rows, width = blocks[0].shape
    total = rows * len(blocks)
    cols = bias.shape[1] // 3
    heads = cols // HEAD_DIM
    outs = [
        ((total, width), jnp.bfloat16, "h"),
        ((total, 4 * cols), jnp.bfloat16, "h"),
        ((heads, total, total), jnp.bfloat16, "h"),
        ((width, 4 * cols), jnp.bfloat16, "h"),
        ((8, 128), jnp.float32),
    ] + [((rows, width), jnp.bfloat16)] * len(blocks)
    return call(
        functools.partial(attend_kernel, count, at),
        "attend",
        outs,
        ("s", info),
        ("s", slopes),
        *blocks,
        ("h", own),
        ("h", other),
        bias,
        scratch=[
            bf16(total, width),
            bf16(total, 4 * cols),
            bf16(heads, total, total),
            bf16(width, 4 * cols),
            bf16(width, 2 * cols),
            bf16(width, 2 * cols),
            sems(4 + 2 * len(blocks)),
        ],
        flops=16 * heads * total * total * HEAD_DIM + 8 * total * width * cols,
        exps=heads * total * total,
    )


def attend_back_kernel(g0, g1, g2, g3, w_in, qkvm_in, probs_in, *refs):
    out_ref, sum_ref, *sends = refs[-13:-7]
    w, qkvm, probs_ref, gs_ref, gm_ref, sem, sem_w = refs[-7:]
    blocks = (g0, g1, g2, g3)
    rows = g0.shape[0]
    cols = w.shape[1] // 4
    heads = cols // HEAD_DIM
    scale = HEAD_DIM**-0.5
    weights = start(w_in, w, sem_w)
    first = start(qkvm_in, qkvm, sem.at[0])
    rest = [start(probs_in.at[h], probs_ref.at[h], sem.at[1 + h]) for h in range(heads)]
    g = join(blocks)
    weights.wait()
    gm_ref[...] = low(dot(g, w[:, 3 * cols :]))
    first.wait()
    for h in range(heads):
        lo = h * HEAD_DIM
        query = qkvm[:, lo : lo + HEAD_DIM]
        key = qkvm[:, cols + lo : cols + lo + HEAD_DIM]
        value = qkvm[:, 2 * cols + lo : 2 * cols + lo + HEAD_DIM]
        rest[h].wait()
        for b in range(len(blocks)):
            span = slice(b * rows, (b + 1) * rows)
            probs = wide(probs_ref[h, span, :])
            grad_probs = contract_cols(gm_ref[span, lo : lo + HEAD_DIM], value)
            inner = jnp.sum(grad_probs * probs, axis=1, keepdims=True)
            grad_scores = low(probs * (grad_probs - inner))
            gs_ref[span, :] = grad_scores
            out_ref[span, lo : lo + HEAD_DIM] = low(dot(grad_scores, key) * scale)
        out_ref[:, cols + lo : cols + lo + HEAD_DIM] = low(
            contract_rows(gs_ref[...], query) * scale
        )
        out_ref[:, 2 * cols + lo : 2 * cols + lo + HEAD_DIM] = low(
            contract_rows(probs_ref[h], gm_ref[:, lo : lo + HEAD_DIM])
        )
    for b in range(len(blocks)):
        span = slice(b * rows, (b + 1) * rows)
        sends[b][...] = low(contract_cols(out_ref[span, :], w[:, : 3 * cols]))
    sums = jnp.sum(wide(out_ref[...]), axis=0, keepdims=True)
    sum_ref[...] = jnp.broadcast_to(sums, sum_ref.shape)


def attend_back(blocks, w, qkvm, probs, after):
    rows, width = blocks[0].shape
    total = rows * len(blocks)
    cols = w.shape[1] // 4
    heads = cols // HEAD_DIM
    outs = [
        ((total, 3 * cols), jnp.bfloat16),
        ((8, 3 * cols), jnp.float32),
    ] + [((rows, width), jnp.bfloat16)] * len(blocks)
    return call(
        attend_back_kernel,
        "attend_back",
        outs,
        *blocks,
        ("h", w),
        ("h", qkvm),
        ("h", probs),
        *[("d", a) for a in after],
        scratch=[
            bf16(*w.shape),
            bf16(total, 4 * cols),
            bf16(heads, total, total),
            bf16(total, total),
            bf16(total, cols),
            sems(1 + heads),
            pltpu.SemaphoreType.DMA,
        ],
        flops=32 * heads * total * total * HEAD_DIM + 8 * total * width * cols,
    )


def attend_weights_kernel(info, g0, g1, g2, g3, dqkv, xs_in, qkvm_in, give, keep, xs, mixed, sem):
    cols = dqkv.shape[1] // 3
    extra = mixed.shape[1] - cols
    first = start(xs_in, xs, sem.at[0])
    second = start(qkvm_in.at[:, 3 * cols - extra :], mixed, sem.at[1])
    second.wait()
    out = contract_rows(join((g0, g1, g2, g3)), mixed[:, extra:])
    first.wait()
    query_key = contract_rows(xs[...], dqkv[:, : 2 * cols])
    value = contract_rows(xs[...], dqkv[:, 2 * cols :])
    value_out = jnp.concatenate([value, out], axis=1)
    is_home = jnp.full(query_key.shape, info[2], jnp.int32) == 1
    give[...] = low(jnp.where(is_home, value_out, query_key))
    keep[...] = low(jnp.where(is_home, query_key, value_out))


def attend_weights(info, g, dqkv, xs, qkvm):
    total, width = xs.shape
    cols = qkvm.shape[1] // 4
    out = ((width, 2 * cols), jnp.bfloat16)
    return call(
        attend_weights_kernel,
        "attend_weights",
        [out, out],
        ("s", info),
        *g,
        dqkv,
        ("h", xs),
        ("h", qkvm),
        scratch=[bf16(total, width), bf16(total, -(-cols // 128) * 128), sems(2)],
        flops=8 * total * width * cols,
    )


def spread_kernel(count, place, keep, came, *refs):
    extra, outs = refs[:-count], refs[-count:]
    height = keep.shape[0] // count
    for k, out in enumerate(outs):
        to = place[0] ^ k
        span = pl.ds(pl.multiple_of(to * height, height), height)
        out[:height, :] = low(wide(keep[span, :]) + wide(came[span, :]))
        if extra:
            small, sums = extra
            cols = sums.shape[1] // 3
            row = lax.broadcasted_iota(jnp.int32, (small.shape[1], cols), 0)
            mine = jnp.full(row.shape, to, jnp.int32) == place[1]
            query = jnp.where(mine & (row == 0), sums[0:1, :cols], 0.0)
            value = jnp.where(mine & (row == 1), sums[0:1, 2 * cols :], 0.0)
            out[height:, :cols] = low(small[to][:, :cols] + query + value)
            out[height:, cols:] = low(small[to][:, cols:])


def spread(place, keep, came, count, *extra):
    added = extra[0].shape[1] if extra else 0
    out = ((keep.shape[0] // count + added, keep.shape[1]), jnp.bfloat16)
    body = functools.partial(spread_kernel, count)
    return call(body, "spread", [out] * count, ("s", place), keep, came, *extra)


def total_kernel(*refs):
    refs[-1][...] = low(summed(refs[:-1]))


def total_of(blocks):
    return call(total_kernel, "total", [(blocks[0].shape, jnp.bfloat16)], *blocks)[0]


def fetch(weights, scratch, sem, order):
    unit = scratch[0].shape[1] // 3
    cut = (slice(0, 2 * unit), slice(2 * unit, 3 * unit))
    copies = {}
    for i, (side, which) in enumerate(order):
        span = cut[which]
        copies[side, which] = start(
            weights[side].at[:, span], scratch[side].at[:, span], sem.at[i]
        )
    return copies


def feed_kernel(x_ref, own, other, part_ref, saved_out, saved, own_ref, other_ref, sem):
    unit = own_ref.shape[1] // 3
    scratch = (own_ref, other_ref)
    copies = fetch((own, other), scratch, sem, ((0, 0), (1, 0), (0, 1), (1, 1)))
    x = x_ref[...]
    width = x.shape[1]
    first = start(x_ref, saved_out.at[:, :width], sem.at[4])
    for side, w in enumerate(scratch):
        lo = side * unit
        copies[side, 0].wait()
        packed = dot(x, w[:, : 2 * unit])
        gate, up = packed[:, :unit], packed[:, unit:]
        phi = 0.5 + 0.5 * lax.erf(gate * (0.5**0.5))
        bell = jnp.exp(gate * gate * -0.5) * (2.0 * math.pi) ** -0.5
        gelu = gate * phi
        saved[:, lo : lo + unit] = low(gelu * up)
        saved[:, 2 * unit + lo : 3 * unit + lo] = low(up * (phi + gate * bell))
        saved[:, 4 * unit + lo : 5 * unit + lo] = low(gelu)
    second = start(saved, saved_out.at[:, width:], sem.at[5])
    copies[0, 1].wait()
    copies[1, 1].wait()
    part_ref[...] = low(
        contract_cols(saved[:, :unit], own_ref[:, 2 * unit :])
        + contract_cols(saved[:, unit : 2 * unit], other_ref[:, 2 * unit :])
    )
    first.wait()
    second.wait()


def feed(x, own, other, unit):
    rows, width = x.shape
    outs = [
        ((rows, width), jnp.bfloat16),
        ((rows, width + 6 * unit), jnp.bfloat16, "h"),
    ]
    return call(
        feed_kernel,
        "feed",
        outs,
        x,
        ("h", own),
        ("h", other),
        scratch=[
            bf16(rows, 6 * unit),
            bf16(width, 3 * unit),
            bf16(width, 3 * unit),
            sems(6),
        ],
        flops=12 * rows * width * unit,
        exps=4 * rows * unit,
    )


def feed_back_kernel(
    g_ref, own, other, saved_in, part_ref, packed_ref, saved, own_ref, other_ref, sem
):
    scratch = (own_ref, other_ref)
    copies = fetch((own, other), scratch, sem, ((0, 1), (1, 1)))
    g = g_ref[...]
    width = g.shape[1]
    unit = own_ref.shape[1] // 3
    copy = start(saved_in.at[:, width + 2 * unit :], saved, sem.at[4])
    cut = slice(0, 2 * unit)
    for side, w in enumerate((own, other)):
        copies[side, 0] = start(w.at[:, cut], scratch[side].at[:, cut], sem.at[2 + side])
    grads = []
    for side, w in enumerate(scratch):
        copies[side, 1].wait()
        grads.append(dot(g, w[:, 2 * unit :]))
    copy.wait()
    total = None
    for side, w in enumerate(scratch):
        lo = side * unit
        at = 2 * side * unit
        packed_ref[:, at : at + unit] = low(grads[side] * wide(saved[:, lo : lo + unit]))
        packed_ref[:, at + unit : at + 2 * unit] = low(
            grads[side] * wide(saved[:, 2 * unit + lo : 3 * unit + lo])
        )
        copies[side, 0].wait()
        term = contract_cols(packed_ref[:, at : at + 2 * unit], w[:, : 2 * unit])
        total = term if total is None else total + term
    part_ref[...] = low(total)


def feed_back(g, own, other, saved, unit):
    rows, width = g.shape
    outs = [((rows, width), jnp.bfloat16), ((rows, 4 * unit), jnp.bfloat16)]
    return call(
        feed_back_kernel,
        "feed_back",
        outs,
        g,
        ("h", own),
        ("h", other),
        ("h", saved),
        scratch=[
            bf16(rows, 4 * unit),
            bf16(width, 3 * unit),
            bf16(width, 3 * unit),
            sems(5),
        ],
        flops=12 * rows * width * unit,
    )


def feed_weights_kernel(side, *refs):
    saved_in, g, packed = refs[:4], refs[4:8], refs[8:12]
    out, xs, act, sem = refs[-4:]
    rows, width = g[0].shape
    unit = act.shape[1]
    at = width + side * unit
    copies = []
    for b, ref in enumerate(saved_in):
        span = slice(b * rows, (b + 1) * rows)
        copies.append(start(ref.at[:, at : at + unit], act.at[span, :], sem.at[2 * b]))
        copies.append(start(ref.at[:, :width], xs.at[span, :], sem.at[2 * b + 1]))
    g_all = join(g)
    lo = 2 * side * unit
    packed_all = jnp.concatenate([p[:, lo : lo + 2 * unit] for p in packed], axis=0)
    for copy in copies[0::2]:
        copy.wait()
    out[:, 2 * unit :] = low(contract_rows(g_all, act[...]))
    for copy in copies[1::2]:
        copy.wait()
    out[:, : 2 * unit] = low(contract_rows(xs[...], packed_all))


def feed_weights(side, saved, g, packed):
    rows, width = g[0].shape
    unit = packed[0].shape[1] // 4
    return call(
        functools.partial(feed_weights_kernel, side),
        "feed_weights",
        [((width, 3 * unit), jnp.bfloat16)],
        *[("h", x) for x in saved],
        *g,
        *packed,
        scratch=[bf16(4 * rows, width), bf16(4 * rows, unit), sems(8)],
        flops=24 * rows * width * unit,
    )[0]


def small_kernel(place, *refs):
    *given, out = refs
    layers = len(given) // 4
    groups, count, both = out.shape
    cols = both // 2
    row = lax.broadcasted_iota(jnp.int32, (count, cols), 0)
    lane = lax.broadcasted_iota(jnp.int32, (count, cols), 1)
    heads = cols // HEAD_DIM
    high = jnp.zeros((count, cols), jnp.float32)
    for l in range(layers):
        top = given[4 * l + 3]
        for h in range(heads):
            at = (place[0] * layers + l) * heads + h
            high = jnp.where(lane == at, top[0:1, h : h + 1], high)
    whole = wide(low(high))
    tops = jnp.where(row == 0, whole, jnp.where(row == 1, high - whole, 0.0))
    for g in range(groups):
        span = slice(g * cols, (g + 1) * cols)
        mine = jnp.full((1, cols), place[1], jnp.int32) == g
        values = jnp.zeros((count, cols), jnp.float32)
        for l in range(layers):
            one, two, sums = given[4 * l : 4 * l + 3]
            rows = [
                one[2:3, span],
                two[2:3, span],
                one[1:2, span],
                two[1:2, span],
                one[0:1, span],
                two[0:1, span],
            ]
            if l > 0:
                query = jnp.where(mine, sums[0:1, :cols], 0.0)
                rows = [query, jnp.where(mine, sums[0:1, 2 * cols :], 0.0)] + rows
            for i, value in enumerate(reversed(rows)):
                values = jnp.where(row == 8 * l + 7 - i, value, values)
        out[g, :, :cols] = values
        out[g, :, cols:] = tops


def small_rows(place, groups, given, cols):
    shape = (groups, 2 * len(given), 2 * cols)
    return call(small_kernel, "small", [(shape, jnp.float32)], ("s", place), *given)[0]


def finish_feed_kernel(l, place, *refs):
    glu_out, down_out, token, glu, down, sem = refs[-6:]
    parts, _, unit = down.shape
    token[...] = jnp.zeros_like(token)
    near = refs[:parts] if len(refs[0].shape) == 2 else [refs[0].at[k] for k in range(parts)]
    copies = []
    for k, block in enumerate(near):
        span = pl.ds(pl.multiple_of((place[1] ^ k) * unit, 128), unit)
        glu[k, :, 0, :] = wide(block[:, :unit])
        glu[k, :, 1, :] = wide(block[:, unit : 2 * unit])
        copies.append(start(glu.at[k], glu_out.at[l, :, :, span], sem.at[2 * k]))
        down[k] = wide(block[:, 2 * unit :])
        copies.append(start(down.at[k], down_out.at[l, :, span], sem.at[2 * k + 1]))
    for copy in copies:
        copy.wait()


def finish_feed(l, layers, place, near, parts, before):
    rows, width = near[0].shape[-2:]
    unit = width // 3
    outs = [
        ((layers, rows, 2, unit * parts), jnp.float32, "h"),
        ((layers, rows, unit * parts), jnp.float32, "h"),
        ((8, 128), jnp.float32),
    ]
    given = [("s", place), *near]
    alias = {}
    if before is not None:
        alias = {len(given): 0, len(given) + 1: 1}
        given += [("h", x) for x in before]
    return call(
        functools.partial(finish_feed_kernel, l),
        "finish_feed",
        outs,
        *given,
        scratch=[
            pltpu.VMEM((parts, rows, 2, unit), jnp.float32),
            pltpu.VMEM((parts, rows, unit), jnp.float32),
            sems(2 * parts),
        ],
        alias=alias,
    )


def choose_kernel(flags, *refs):
    *blocks, out = refs
    parts = len(blocks)
    pair = parts // 2
    height, _ = blocks[0].shape
    count = (out.shape[0] - pair * height) // parts
    home = jnp.full(blocks[0].shape, flags[0], jnp.int32) == 1
    for i in range(pair):
        out[i * height : (i + 1) * height, :] = low(
            jnp.where(home, wide(blocks[pair + i][...]), wide(blocks[i][...]))
        )
    for k, block in enumerate(blocks):
        at = pair * height + k * count
        out[at : at + count, :] = block[height - count :, :]


def choose(flags, blocks, count):
    parts = len(blocks)
    height, width = blocks[0].shape
    shape = (parts // 2 * height + parts * count, width)
    return call(choose_kernel, "choose", [(shape, jnp.bfloat16)], ("s", flags), *blocks)[0]


def finish_attention_kernel(groups, count, flags, *refs):
    qkv_out, out_out, clip_out, small_out, weights, qkv, out, clip, sem = refs[-9:]
    *blocks, came, weight_in = refs[:-9]
    parts = len(blocks)
    pair = parts // 2
    height, _ = blocks[0].shape
    layers, _, rows, half = qkv.shape
    cols = half // 2
    heads = cols // HEAD_DIM
    fetched = [start(weight_in.at[l, :2], weights.at[l], sem.at[l]) for l in range(layers)]
    total, tops = None, []
    for k, block in enumerate(blocks):
        at = pair * height + k * count
        mine, theirs = wide(block[height - count :, :]), wide(came[at : at + count, :])
        both = mine[:, :cols] + theirs[:, :cols]
        total = both if total is None else total + both
        tops.append(
            jnp.maximum(
                mine[0:1, cols:] + mine[1:2, cols:], theirs[0:1, cols:] + theirs[1:2, cols:]
            )
        )
    small_out[...] = total
    home = jnp.full((rows, half), flags[0], jnp.int32) == 1
    even = jnp.full((rows, half), flags[1], jnp.int32) == 1
    home_row, even_row = home[0:1, :cols], even[0:1, :cols]
    pick_tops = [jnp.where(home_row, tops[i], tops[pair + i]) for i in range(pair)]
    first_top = jnp.where(even_row, pick_tops[0], pick_tops[1])
    second_top = jnp.where(even_row, pick_tops[1], pick_tops[0])
    lane = lax.broadcasted_iota(jnp.int32, (1, half), 1) // HEAD_DIM
    copies = []
    for l in range(layers):
        span = slice(l * rows, (l + 1) * rows)
        near = [wide(b[span, :]) for b in blocks]
        far = [wide(came[i * height + l * rows : i * height + (l + 1) * rows, :]) for i in range(pair)]
        near = [jnp.where(home, near[i], near[pair + i]) for i in range(pair)]
        query_key = [jnp.where(even, near[0], near[1]), jnp.where(even, near[1], near[0])]
        value_out = [jnp.where(even, far[0], far[1]), jnp.where(even, far[1], far[0])]
        for i in range(pair):
            place = slice(i * cols, (i + 1) * cols)
            qkv[l, 0, :, place] = query_key[i][:, :cols]
            qkv[l, 1, :, place] = query_key[i][:, cols:]
            qkv[l, 2, :, place] = value_out[i][:, :cols]
            out[l, :, place] = value_out[i][:, cols:]
        copies.append(start(qkv.at[l], qkv_out.at[l], sem.at[layers + 3 * l]))
        copies.append(start(out.at[l], out_out.at[l], sem.at[layers + 3 * l + 1]))
        top = jnp.zeros((1, half), jnp.float32)
        for i, row in enumerate((first_top, second_top)):
            for h in range(heads):
                best = None
                for g in range(groups):
                    at = (g * layers + l) * heads + h
                    value = row[:, at : at + 1]
                    best = value if best is None else jnp.maximum(best, value)
                top = jnp.where(lane == i * heads + h, best, top)
        factor = CLIP_LIMIT / jnp.maximum(top, CLIP_LIMIT)
        fetched[l].wait()
        for m in range(2):
            clip[l, :, m, :] = (wide(weights[l, m]) - STEP_SIZE * qkv[l, m]) * factor
        copies.append(start(clip.at[l], clip_out.at[l], sem.at[layers + 3 * l + 2]))
    for copy in copies:
        copy.wait()


def finish_attention(groups, count, flags, blocks, came, weight):
    layers, _, rows, half = weight.shape
    outs = [
        ((layers, 3, rows, half), jnp.float32, "h"),
        ((layers, rows, half), jnp.float32, "h"),
        ((layers, rows, 2, half), jnp.float32, "h"),
        ((count, half // 2), jnp.float32),
    ]
    return call(
        functools.partial(finish_attention_kernel, groups, count),
        "finish_attention",
        outs,
        ("s", flags),
        *blocks,
        came,
        ("h", weight),
        scratch=[
            pltpu.VMEM((layers, 2, rows, half), weight.dtype),
            f32(layers, 3, rows, half),
            f32(layers, rows, half),
            f32(layers, rows, 2, half),
            sems(4 * layers),
        ],
    )


def both_kernel(core, own, other, out):
    out[core[0]] = own[...]
    out[1 - core[0]] = other[...]


def both_slots(core, own, other):
    out = ((2, *own.shape), own.dtype)
    return call(both_kernel, "both", [out], ("s", core), own, other)[0]


def normalised(z):
    mean = jnp.mean(z, axis=1, keepdims=True)
    centred = z - mean
    r = lax.rsqrt(jnp.mean(centred * centred, axis=1, keepdims=True) + EPSILON)
    return centred * r, r


def affine(n, vec, gain, shift):
    return n * vec[gain : gain + 1, :] + vec[shift : shift + 1, :]


def summed(refs):
    total = wide(refs[0][...])
    for ref in refs[1:]:
        total = total + wide(ref[...])
    return total


def norm_input(before, bias, parts, prev_in, prev, sem, vec_in, vec):
    copy = start(prev_in, prev, sem.at[0])
    other = start(vec_in, vec, sem.at[2])
    z = summed(parts)
    other.wait()
    z = z + vec[bias : bias + 1, :]
    copy.wait()
    if before is None:
        return z + wide(prev[...])
    return z + affine(normalised(prev[...])[0], vec, *before)


def norm_kernel(
    before, rows_of, p0, p1, p2, p3, prev_in, vec_in, low_ref, z_out, prev, zs, vec, sem
):
    bias, gain, shift = rows_of
    z = norm_input(before, bias, (p0, p1, p2, p3), prev_in, prev, sem, vec_in, vec)
    zs[...] = z
    copy = start(zs, z_out, sem.at[1])
    low_ref[...] = low(affine(normalised(z)[0], vec, gain, shift))
    copy.wait()


def norm(before, rows_of, parts, prev, vec):
    shape = parts[0].shape
    outs = [(shape, jnp.bfloat16), (shape, jnp.float32, "h")]
    return call(
        functools.partial(norm_kernel, before, rows_of),
        "norm",
        outs,
        *parts,
        ("h", prev),
        ("h", vec),
        scratch=[pltpu.VMEM(shape, prev.dtype), f32(*shape), f32(*vec.shape), sems(3)],
        flops=prev.size,
    )


def norm_grad(grad, n, r, gain, dz_out, low_ref, stat_ref, dzs, sem):
    scaled = grad * gain
    one = jnp.mean(scaled, axis=1, keepdims=True)
    two = jnp.mean(scaled * n, axis=1, keepdims=True)
    dz = (scaled - one - n * two) * r
    dz_low = low(dz)
    dzs[...] = dz
    copy = start(dzs, dz_out, sem)
    low_ref[...] = dz_low
    stat_ref[0:1, :] = jnp.sum(grad * n, axis=0, keepdims=True)
    stat_ref[1:2, :] = jnp.sum(grad, axis=0, keepdims=True)
    stat_ref[2:3, :] = jnp.sum(wide(dz_low), axis=0, keepdims=True)
    stat_ref[3:, :] = jnp.zeros((stat_ref.shape[0] - 3, stat_ref.shape[1]), jnp.float32)
    copy.wait()


def norm_back_kernel(gain_row, p0, p1, p2, p3, skip_in, z_in, vec_in, *refs):
    outs, (skip, zs, dzs, vec, sem) = refs[-8:-5], refs[-5:]
    one = start(z_in, zs, sem.at[0])
    two = start(skip_in, skip, sem.at[1])
    three = start(vec_in, vec, sem.at[3])
    grad = summed((p0, p1, p2, p3))
    one.wait()
    n, r = normalised(zs[...])
    two.wait()
    three.wait()
    gain = vec[gain_row : gain_row + 1, :]
    norm_grad(grad + skip[...], n, r, gain, *outs, dzs, sem.at[2])


def grad_outs(shape):
    return [
        (shape, jnp.float32, "h"),
        (shape, jnp.bfloat16),
        ((8, shape[1]), jnp.float32),
    ]


def norm_back(gain_row, parts, skip, z, vec, after):
    shape = skip.shape
    return call(
        functools.partial(norm_back_kernel, gain_row),
        "norm_back",
        grad_outs(shape),
        *parts,
        ("h", skip),
        ("h", z),
        ("h", vec),
        *[("d", a) for a in after],
        scratch=[f32(*shape), f32(*shape), f32(*shape), f32(*vec.shape), sems(4)],
        flops=skip.size,
    )


def turn_kernel(before, rows_of, info, p0, p1, p2, p3, prev_in, vec_in, cot, out_ref, *refs):
    outs, (prev, dzs, vec, sem) = refs[:3], refs[3:]
    bias, gain, shift = rows_of
    z = norm_input(before, bias, (p0, p1, p2, p3), prev_in, prev, sem, vec_in, vec)
    n, r = normalised(z)
    rows = z.shape[0]
    ok = info[0] * rows + lax.broadcasted_iota(jnp.int32, (rows, 1), 0) < info[1]
    out_ref[...] = low(jnp.where(ok, affine(n, vec, gain, shift), 0.0))
    grad = jnp.where(ok, wide(cot[...]), 0.0)
    norm_grad(grad, n, r, vec[gain : gain + 1, :], *outs, dzs, sem.at[1])


def turn(before, rows_of, info, parts, prev, vec, cot):
    shape = prev.shape
    outs = [(shape, jnp.bfloat16)] + grad_outs(shape)
    return call(
        functools.partial(turn_kernel, before, rows_of),
        "turn",
        outs,
        ("s", info),
        *parts,
        ("h", prev),
        ("h", vec),
        cot,
        scratch=[f32(*shape), f32(*shape), f32(*vec.shape), sems(3)],
        flops=prev.size,
    )


def shards(
    tokens,
    cotangent,
    lengths,
    dealing,
    qkv_weight,
    out_weight,
    glu_weight,
    down_weight,
    biases,
    gains,
):
    slots, rows, width = tokens.shape
    layers = qkv_weight.shape[0]
    parts = lax.axis_size("ctx")
    cores = lax.axis_size("heads")
    groups = lax.axis_size("dp")
    part = lax.axis_index("ctx")
    core = lax.axis_index("heads")
    group = lax.axis_index("dp")
    local_rows = qkv_weight.shape[1]
    half = qkv_weight.shape[3]
    cols = half * cores // parts
    local_heads = cols // HEAD_DIM
    quarter = glu_weight.shape[3] // parts
    per_core = parts // cores
    home = part // per_core == core
    offset = (part % per_core) * cols

    def swap(x):
        return lax.ppermute(x, "heads", [(j, cores - 1 - j) for j in range(cores)])

    def hop(x, k):
        return lax.ppermute(x, "ctx", [(j, j ^ k) for j in range(parts)])

    def hops(blocks):
        return [blocks[0]] + [hop(blocks[k], k) for k in range(1, parts)]

    def own_first(work, blocks, extras):
        done = [work(blocks[0], extras[0])]
        for block, extra in zip(blocks[1:], extras[1:]):
            block, _ = lax.optimization_barrier((block, done[0][0]))
            done.append(work(block, extra))
        return zip(*done)

    def gather(x):
        return hops([x] * parts)

    def tie(x, *others):
        return lax.optimization_barrier((x, *others))[0]

    value_out = jnp.concatenate(
        [
            lax.dynamic_slice_in_dim(qkv_weight[:, :, 2, :], offset, cols, 2),
            lax.dynamic_slice_in_dim(out_weight, offset, cols, 2),
        ],
        axis=2,
    )
    query_key = jnp.concatenate(
        [
            lax.dynamic_slice_in_dim(qkv_weight[:, :, 0, :], offset, cols, 2),
            lax.dynamic_slice_in_dim(qkv_weight[:, :, 1, :], offset, cols, 2),
        ],
        axis=2,
    )
    attn_shard = jnp.where(home, query_key, swap(value_out))
    attn_first, attn_shard_later = attn_shard[0], [attn_shard[l] for l in range(1, layers)]
    glu_part = lax.dynamic_slice_in_dim(glu_weight, part * quarter, quarter, 3)
    down_part = lax.dynamic_slice_in_dim(down_weight, part * quarter, quarter, 2)

    def over_dp(x):
        return lax.all_gather(x, "dp", axis=0, tiled=True)

    direct = groups <= 4 and local_rows == cols
    place = jnp.stack([group, part]).astype(jnp.int32)

    def hop_dp(x, k):
        return lax.ppermute(x, "dp", [(j, j ^ k) for j in range(groups)])

    feed_full = [None] * layers
    attn_full = [None] * layers
    tokens_own = lax.dynamic_index_in_dim(tokens, core, 0, keepdims=False)
    feed_shard = [
        jnp.concatenate([glu_part[l, :, 0], glu_part[l, :, 1], down_part[l]], axis=1)
        for l in range(layers)
    ]
    early = over_dp(jnp.concatenate([feed_shard[0]] + attn_shard_later, axis=1))
    if direct:
        own = jnp.concatenate([attn_first] + [hop_dp(attn_first, k) for k in range(1, groups)])
    else:
        own = over_dp(attn_first)
    low_zero = gather(tokens_own)
    attn_full[0] = (own, swap(own), 0)
    late = [over_dp(lax.optimization_barrier((x, own))[0]) for x in feed_shard[1:]]

    slot = group * slots + core
    slot_ids = jnp.arange(lengths.shape[0], dtype=jnp.int32)
    sequence = jnp.sum(jnp.where(slot_ids == slot, dealing, 0))
    length = jnp.sum(jnp.where(slot_ids == sequence, lengths, 0))
    info = [
        jnp.stack([part, length, home, group if direct and l == 0 else jnp.int32(0)]).astype(
            jnp.int32
        )
        for l in range(layers)
    ]
    slopes = lax.dynamic_slice_in_dim(
        jnp.array(alibi_slopes(HEADS), jnp.float32), part * local_heads, local_heads
    )
    vec = jnp.concatenate([biases, gains], axis=1).reshape(layers * 8, width)
    qv = lax.dynamic_slice_in_dim(biases[:, :2], part * cols, cols, 2)
    qkv_bias = jnp.concatenate([qv[:, :1], jnp.zeros_like(qv[:, :1]), qv[:, 1:]], axis=2)

    prev, before = tokens_own, None
    low_own = tokens_own
    saved = []
    tops = []
    for l in range(layers):
        v = 8 * l
        x_low = low_zero if l == 0 else gather(low_own)
        xs, qkvm, probs, attn_w, top, *sends = attend(
            info[l],
            slopes,
            x_low,
            *attn_full[l],
            qkv_bias[l],
            groups if direct and l == 0 else 1,
        )
        tops.append(top)
        hidden_low, z_one = norm(before, (v + 2, v + 6, v + 4), hops(sends), prev, vec)
        feed_own = tie(early if l == 0 else late[l - 1], hidden_low if l == 0 else top)
        feed_full[l] = (feed_own, swap(feed_own))
        if l == 0:
            for n in range(1, layers):
                attn_full[n] = (*feed_full[0], 3 * quarter + 2 * cols * (n - 1))
        h_low = gather(hidden_low)
        sends, kept = own_first(lambda h, _: feed(h, *feed_full[l], quarter), h_low, h_low)
        arrived = hops(sends)
        rows_of = (v + 3, v + 7, v + 5)
        if l + 1 < layers:
            low_own, z_two = norm((v + 6, v + 4), rows_of, arrived, z_one, vec)
            prev, before = z_two, (v + 7, v + 5)
        else:
            cot = lax.dynamic_index_in_dim(cotangent, core, 0, keepdims=False)
            outputs, grad_two, low_two, stats_two = turn(
                (v + 6, v + 4), rows_of, info[l], arrived, z_one, vec, cot
            )
            z_two = None
        saved.append((xs, qkvm, probs, attn_w, z_one, kept, z_two))

    feed_parts = [None] * layers
    attn_parts = [None] * layers
    carried = None
    woven = [None] * layers
    def over_dp_sum(x):
        return lax.psum_scatter(x, "dp", scatter_dimension=0, tiled=True)

    stats = [[None] * 3 for _ in range(layers)]
    for l in reversed(range(layers)):
        v = 8 * l
        x_low, qkvm, probs, attn_w, z_one, kept, _ = saved[l]
        above = l + 1 < layers
        stats[l][1] = stats_two
        g_low = gather(low_two)
        sends, packed = own_first(
            lambda g, k: feed_back(g, *feed_full[l], k, quarter), g_low, kept
        )
        arrived = hops(sends)
        packed = list(packed)
        packed[0], arrived[3] = lax.optimization_barrier((packed[0], arrived[3]))
        give = feed_weights(1, kept, g_low, packed)
        packed[0], arrived[2], give = lax.optimization_barrier((packed[0], arrived[2], give))
        keep = feed_weights(0, kept, g_low, packed)
        total = wide(keep) + wide(swap(give))
        if above:
            total = jnp.concatenate([total, carried], axis=1)
        total = low(total)
        arrived[0] = tie(arrived[0], total)
        if above:
            arrived[0], feed_parts[l + 1] = lax.optimization_barrier(
                (arrived[0], feed_parts[l + 1])
            )
        grad_one, low_one, stats[l][0] = norm_back(v + 6, arrived, grad_two, z_one, vec, [])
        feed_parts[l] = over_dp_sum(total)
        if above:
            attn_parts[l + 1] = feed_parts[l][:, 3 * quarter :]
            feed_parts[l] = feed_parts[l][:, : 3 * quarter]
        a_low = gather(low_one)
        if above:
            near = tie(feed_parts[l + 1], *a_low)
            near = [near] + [hop(near, k) for k in (1, 2)]
        dqkv, sums, *sends = attend_back(a_low, attn_w, qkvm, probs, [])
        if above:
            tied = lax.optimization_barrier((*sends, *near))
            sends, woven[l + 1] = list(tied[:parts]), list(tied[parts:])
            woven[l + 1] += [hop(woven[l + 1][0], k) for k in range(3, parts)]
        stats[l][2] = sums
        arrived = hops(sends)
        give, keep = attend_weights(info[l], a_low, dqkv, x_low, qkvm)
        came = swap(give)
        if l > 0:
            arrived[0] = tie(arrived[0], keep)
            carried = wide(keep) + wide(came)
            grad_two, low_two, stats_two = norm_back(
                v - 8 + 7, arrived, grad_one, saved[l - 1][6], vec, []
            )

    count = layers * local_heads
    if direct:
        given = []
        for l in range(layers):
            given += [stats[l][0], stats[l][1], stats[l][2] if l else stats[l][0], tops[l]]
        small = small_rows(place, groups, given, cols)
        terms = list(spread(place, keep, came, groups, small, sums))
        terms[1:] = [hop_dp(terms[k], k) for k in range(1, groups)]
        last = total_of(terms)
        near = [x for l in range(1, layers) for x in woven[l]]
        tied = lax.optimization_barrier((*arrived, *near, *terms))
        arrived, near = list(tied[:parts]), list(tied[parts : parts + len(near)])
        last = tie(last, *arrived, *near)
        for l in range(1, layers):
            woven[l] = near[(l - 1) * parts : l * parts]
        grad = grad_one + sum(wide(a) for a in arrived)
    else:
        grad = grad_one + sum(wide(a) for a in arrived)
        empty = jnp.zeros((width,), jnp.float32)
        small = []
        for l in range(layers):
            one, two, sums = stats[l]
            small += [
                lax.dynamic_update_slice_in_dim(empty, sums[0, lo : lo + cols], part * cols, 0)
                for lo in (0, 2 * cols)
            ]
            small += [one[2], two[2], one[1], two[1], one[0], two[0]]
        small = jnp.stack(small).reshape(layers * 8, groups, local_rows).transpose(1, 0, 2)
        small = jnp.pad(small, ((0, 0), (0, 0), (0, cols - local_rows)))
        own_tops = jnp.stack([t[0, :local_heads] for t in tops]).reshape(-1)
        high = wide(low(own_tops))
        pair = jnp.stack([high, own_tops - high])
        slots_of = jnp.zeros((layers * 8, cols), jnp.float32)
        slots_of = lax.dynamic_update_slice(slots_of, pair, (0, group * count))
        slots_of = jnp.broadcast_to(slots_of[None], (groups,) + slots_of.shape)
        small = jnp.concatenate([small, slots_of], axis=2)
        total = wide(keep) + wide(came)
        payload = jnp.concatenate([total.reshape(groups, local_rows, 2 * cols), small], axis=1)
        last = lax.psum_scatter(low(payload), "dp", scatter_dimension=0, tiled=False)
    core_ref = core.astype(jnp.int32)[None]
    out_tokens = both_slots(core_ref, outputs, swap(outputs))
    grad_tokens = both_slots(core_ref, grad, swap(grad))
    result = None
    for l in reversed(range(1, layers)):
        *result, _ = finish_feed(l, layers, place, woven[l], parts, result)
    flags = jnp.stack([home, part % per_core == 0]).astype(jnp.int32)
    small_count = layers * 8
    stacked = [last[:local_rows]] + attn_parts[1:] + [last[local_rows:]]
    shared = gather(jnp.concatenate(stacked))
    near = gather(tie(feed_parts[0], shared[0]))
    tied = lax.optimization_barrier((*shared, *near))
    shared, near = list(tied[:parts]), list(tied[parts:])
    given = choose(flags, shared, small_count)
    arrived = swap(given)

    grad_qkv, grad_out, clipped_qk, small_sum = finish_attention(
        groups, small_count, flags, shared, arrived, qkv_weight.transpose(0, 2, 1, 3)
    )
    small_sum = small_sum[:, :local_rows].reshape(layers, 8, local_rows)
    grad_glu, grad_down, _ = finish_feed(0, layers, place, near, parts, result)
    return (
        out_tokens,
        grad_tokens,
        grad_qkv.transpose(0, 2, 1, 3),
        grad_out,
        grad_glu,
        grad_down,
        small_sum[:, :6],
        small_sum[:, 6:],
        clipped_qk,
    )


def solution(mesh):
    in_specs = (
        P("dp", "ctx", None),
        P("dp", "ctx", None),
        P(),
        P(),
        P(None, "dp", None, "heads"),
        P(None, "dp", "heads"),
        P(None, "dp", None, "heads"),
        P(None, "dp", "heads"),
        P(),
        P(),
    )
    out_specs = (
        P("dp", "ctx", None),
        P("dp", "ctx", None),
        P(None, "dp", None, "heads"),
        P(None, "dp", "heads"),
        P(None, "dp", None, "heads"),
        P(None, "dp", "heads"),
        P(None, None, "dp"),
        P(None, None, "dp"),
        P(None, "dp", None, "heads"),
    )
    return jax.shard_map(shards, mesh=mesh, in_specs=in_specs, out_specs=out_specs, check_vma=False)
```

time: 553 us -> 405 us (0.73)
  Pallas kernels: 18.8 us -> 136 us
  blocking collectives: 103 us -> 0 us
  matrix products: 101 us -> 0 us
  local copies, waits for them, and re-layouts: 47.4 us -> 17.1 us
  other arithmetic: 35.8 us -> 8.93 us
    pallas_call x4 -> x42, Pallas kernels: 18.8 us -> 136 us  [call(): pl.pallas_call(body, out_shape=shapes, in_specs=[pl.BlockSpec(memory_spac...]
    dot_general x102 -> x0, matrix products: 101 us -> none  [the longest x48 46.7 us: contract_cols(): lax.dot_general(former, latter, (((1,), (1,)), ((), ())), preferred_eleme...]
    psum x1 -> x0, blocking collectives: 41.7 us -> none  [shards(): small = lax.psum(small, ('dp', 'ctx', 'heads'))]
    pmax x1 -> x0, blocking collectives: 38.7 us -> none  [shards(): top = lax.pmax(top, ('dp', 'ctx', 'heads'))]
    unnamed x441 -> x54, local copies, waits for them, and re-layouts: 30.1 us -> 6.32 us
    all_gather x1 -> x0, blocking collectives: 23.1 us -> none  [shards(): attn_own = lax.all_gather(attn_shard[l], 'dp', axis=0, tiled=True)]
    all_gather x2, waiting for transfers between devices: 28.4 us -> 9.38 us  [over_dp(): return lax.all_gather(x, 'dp', axis=0, tiled=True)]
    ppermute x6, waiting for transfers between devices: 8.95 us -> 18.7 us  [hop_dp(): return lax.ppermute(x, 'dp', [(j, j ^ k) for j in range(groups)])]
  transfers between devices with their start and end apart: 79 -> 78, of which waited for: 31 -> 35; matrix products, arithmetic and copies ran while one was open for 27% -> 4% of each run, Pallas kernels for 3% -> 32%
where the time goes in v2:
time: 405 us; the launch traced here: 397 us
  Pallas kernels  136 us (34%)
  waiting for transfers between devices  132 us (33%)
  starting transfers between devices  88.7 us (22%)
  local copies, waits for them, and re-layouts  17.1 us (4%)
  between operations  15.2 us (4%)
  other arithmetic  8.93 us (2%)
    pallas_call x42, Pallas kernels, call(): pl.pallas_call(body, out_shape=shapes, in_specs=[pl.BlockSpec(memory_spac...  136 us
    ppermute x57, waiting for transfers between devices, hop(): return lax.ppermute(x, 'ctx', [(j, j ^ k) for j in range(parts)])  99.4 us
    ppermute x57, starting transfers between devices, hop(): return lax.ppermute(x, 'ctx', [(j, j ^ k) for j in range(parts)])  69.4 us
    ppermute x6, waiting for transfers between devices, hop_dp(): return lax.ppermute(x, 'dp', [(j, j ^ k) for j in range(groups)])  18.7 us
    ppermute x6, starting transfers between devices, hop_dp(): return lax.ppermute(x, 'dp', [(j, j ^ k) for j in range(groups)])  16.8 us
    all_gather x2, waiting for transfers between devices, over_dp(): return lax.all_gather(x, 'dp', axis=0, tiled=True)  9.38 us
  transfers between devices with their start and end apart: 78, of which 35 were waited for; matrix products, arithmetic and copies ran while one was open for 4% of the time, Pallas kernels for 32%

profile of v2, /device:TPU:0, one launch (start us, length us, event | category | flops | bytes accessed | tf_op | source)
XLA Modules:
  0.0 397.1 jit_solution(13965172893131591597)
XLA Ops:
  9.7 3.4 constant_dynamic-slice_fusion.1
  27.7 12.0 %collective-permute-done.5 = bf16[192,384]{1,0:T(8,128)(2,1)S(1)} collective-permute-done((bf16[192,384]{1,0:T(8,128)(2,1)S(1)}, bf16[192,384]{1,0:T(8,128)(2,1)S(1)}, u32[]{:S(2)}, u32[]{:S(2)}) %collective-permute-start.5) | collective-permute-done | bytes 147488 | tf_op jit(solution)/shard_map/ppermute | solution.py:937
  42.7 9.6 %attend.2 = (bf16[512,768]{1,0:T(8,128)(2,1)}, bf16[512,768]{1,0:T(8,128)(2,1)}, bf16[3,512,512]{2,1,0:T(8,128)(2,1)}, bf16[768,768]{1,0:T(8,128)(2,1)}, f32[8,1...) custom-call(s32[4]{0:T(128)S(1)} %get-tuple-element.324.info, ...), custom_call_target="tpu_custom_call" | custom-call | flops 1409286144 | bytes 7084316 | tf_op jit(solution)/shard_map/attend/pallas_call | solution.py:80
  56.5 4.5 %collective-permute-done.10.p3 = bf16[128,768]{1,0:T(8,128)(2,1)S(1)} collective-permute-done((bf16[128,768]{1,0:T(8,128)(2,1)S(1)}, bf16[128,768]{1,0:T(8,128)(2,1)S(1)}, u32[]{:S(2)}, u32[]{:S(2)}) %collective-permute-start.10) | collective-permute-done | bytes 196640 | tf_op jit(solution)/shard_map/ppermute | solution.py:893
  66.2 9.4 %all-gather.3.cloned.1.call-done.own = bf16[768,1536]{1,0:T(8,128)(2,1)} async-done(((bf16[192,1536]{1,0:T(8,128)(2,1)}), bf16[768,1536]{1,0:T(8,128)(2,1)}) %all-gather.3.cloned.1.call-update) | async-done | bytes 2359312 | tf_op jit(solution)/shard_map/all_gather | solution.py:931
  82.7 2.9 feed.8
  86.5 3.1 feed.11
  90.0 3.0 feed.10
  94.7 3.0 feed.9
  109.1 3.6 collective-permute-done.18.x1
  112.7 3.1 collective-permute-done.19.x2
  115.8 9.8 %attend.3 = (bf16[512,768]{1,0:T(8,128)(2,1)}, bf16[512,768]{1,0:T(8,128)(2,1)}, bf16[3,512,512]{2,1,0:T(8,128)(2,1)}, bf16[768,768]{1,0:T(8,128)(2,1)}, f32[8,1...) custom-call(s32[4]{0:T(128)S(1)} %pad_add_fusion.info, ...), custom_call_target="tpu_custom_call" | custom-call | flops 1409286144 | bytes 10623260 | tf_op jit(solution)/shard_map/attend/pallas_call | solution.py:80
  129.2 4.2 %collective-permute-done.21.p1 = bf16[128,768]{1,0:T(8,128)(2,1)S(1)} collective-permute-done((bf16[128,768]{1,0:T(8,128)(2,1)S(1)}, bf16[128,768]{1,0:T(8,128)(2,1)S(1)}, u32[]{:S(2)}, u32[]{:S(2)}) %collective-permute-start.21) | collective-permute-done | bytes 196640 | tf_op jit(solution)/shard_map/ppermute | solution.py:893
  133.5 4.1 %collective-permute-done.22.p2 = bf16[128,768]{1,0:T(8,128)(2,1)S(1)} collective-permute-done((bf16[128,768]{1,0:T(8,128)(2,1)S(1)}, bf16[128,768]{1,0:T(8,128)(2,1)S(1)}, u32[]{:S(2)}, u32[]{:S(2)}) %collective-permute-start.22) | collective-permute-done | bytes 196640 | tf_op jit(solution)/shard_map/ppermute | solution.py:893
  144.4 3.1 feed.12
  148.4 3.0 feed.15
  153.1 2.9 feed.14
  157.4 3.0 feed.13
  162.2 3.8 collective-permute-done.26.p1
  173.2 3.1 feed_back.8
  176.3 3.1 feed_back.9
  180.7 3.1 feed_back.10
  184.9 3.1 feed_back.11
  188.0 3.2 feed_weights.4
  192.5 3.1 feed_weights.5
  204.6 4.2 %collective-permute-done.39.g1 = bf16[128,768]{1,0:T(8,128)(2,1)S(1)} collective-permute-done((bf16[128,768]{1,0:T(8,128)(2,1)S(1)}, bf16[128,768]{1,0:T(8,128)(2,1)S(1)}, u32[]{:S(2)}, u32[]{:S(2)}) %collective-permute-start.39) | collective-permute-done | bytes 196640 | tf_op jit(solution)/shard_map/ppermute | solution.py:893
  208.9 3.8 collective-permute-done.40.g2
  212.6 9.0 %attend_back.2 = (bf16[512,576]{1,0:T(8,128)(2,1)S(1)}, f32[8,576]{1,0:T(8,128)S(1)}, bf16[128,768]{1,0:T(8,128)(2,1)S(1)}, bf16[128,768]{1,0:T(8,128)(2,1)S(1)}...) custom-call(bf16[128,768]{1,0:T(8,128)(2,1)S(1)} %get-tuple-element.218.g0, ...), custom_call_target="tpu_custom_call" | custom-call | flops 2214592512 | bytes 5720064 | tf_op jit(solution)/shard_map/attend_back/pallas_call | solution.py:80
  225.2 3.4 attend_weights.2
  237.3 3.1 feed_back.12
  240.8 3.1 feed_back.13
  245.7 3.1 feed_back.14
  250.1 3.1 feed_back.15
  253.2 3.4 feed_weights.6
  257.1 3.1 feed_weights.7
  264.0 6.4 %collective-permute-done.52.p1 = bf16[128,768]{1,0:T(8,128)(2,1)S(1)} collective-permute-done((bf16[128,768]{1,0:T(8,128)(2,1)S(1)}, bf16[128,768]{1,0:T(8,128)(2,1)S(1)}, u32[]{:S(2)}, u32[]{:S(2)}) %collective-permute-start.52) | collective-permute-done | bytes 196640 | tf_op jit(solution)/shard_map/ppermute | solution.py:893
  276.2 4.3 %collective-permute-done.53.g1 = bf16[128,768]{1,0:T(8,128)(2,1)S(1)} collective-permute-done((bf16[128,768]{1,0:T(8,128)(2,1)S(1)}, bf16[128,768]{1,0:T(8,128)(2,1)S(1)}, u32[]{:S(2)}, u32[]{:S(2)}) %collective-permute-start.53) | collective-permute-done | bytes 196640 | tf_op jit(solution)/shard_map/ppermute | solution.py:893
  283.3 8.7 %attend_back.3 = (bf16[512,576]{1,0:T(8,128)(2,1)S(1)}, f32[8,576]{1,0:T(8,128)S(1)}, bf16[128,768]{1,0:T(8,128)(2,1)S(1)}, bf16[128,768]{1,0:T(8,128)(2,1)S(1)}...) custom-call(bf16[128,768]{1,0:T(8,128)(2,1)S(1)} %get-tuple-element.257.g0, ...), custom_call_target="tpu_custom_call" | custom-call | flops 2214592512 | bytes 5720064 | tf_op jit(solution)/shard_map/attend_back/pallas_call | solution.py:80
  292.0 3.4 attend_weights.3
  297.9 10.2 %collective-permute-done.56.refs_1_ = bf16[192,1152]{1,0:T(8,128)(2,1)S(1)} collective-permute-done((bf16[192,1152]{1,0:T(8,128)(2,1)S(1)}, bf16[192,1152]{1,0:T(8,128)(2,1)S(1)}, u32[]{:S(2)}, u32[]{:S(2)}) %collective-permute-start.56) | collective-permute-done | bytes 442400 | tf_op jit(solution)/shard_map/ppermute | solution.py:893
  314.2 4.0 %collective-permute-start.64 = (bf16[208,384]{1,0:T(8,128)(2,1)S(1)}, bf16[208,384]{1,0:T(8,128)(2,1)S(1)}, u32[]{:S(2)}, u32[]{:S(2)}) collective-permute-start(bf16[208,384]{1,0:T(8,128)(2,1)S(1)} %get-tuple-element.287), channel_id=1, source_target_pairs={{0,16},{8,24},{16,0},{24,8},{1,17},{9,25},{17,1},{25,9},{2,18},{10... | collective-permute-start | bytes 479240 | tf_op jit(solution)/shard_map/ppermute | solution.py:937
  322.5 6.2 %collective-permute-start.65 = (bf16[208,384]{1,0:T(8,128)(2,1)S(1)}, bf16[208,384]{1,0:T(8,128)(2,1)S(1)}, u32[]{:S(2)}, u32[]{:S(2)}) collective-permute-start(bf16[208,384]{1,0:T(8,128)(2,1)S(1)} %get-tuple-element.288), channel_id=1, source_target_pairs={{0,24},{8,16},{16,8},{24,0},{1,25},{9,17},{17,9},{25,1},{2,26},{10... | collective-permute-start | bytes 479240 | tf_op jit(solution)/shard_map/ppermute | solution.py:937
  328.6 4.4 %collective-permute-done.65.refs_3_ = bf16[208,384]{1,0:T(8,128)(2,1)S(1)} collective-permute-done((bf16[208,384]{1,0:T(8,128)(2,1)S(1)}, bf16[208,384]{1,0:T(8,128)(2,1)S(1)}, u32[]{:S(2)}, u32[]{:S(2)}) %collective-permute-start.65) | collective-permute-done | bytes 159776 | tf_op jit(solution)/shard_map/ppermute | solution.py:937
  342.8 3.3 collective-permute-done.67.refs_1_
  347.9 24.7 %collective-permute-done.68.refs_2_ = bf16[400,384]{1,0:T(8,128)(2,1)S(1)} collective-permute-done((bf16[400,384]{1,0:T(8,128)(2,1)S(1)}, bf16[400,384]{1,0:T(8,128)(2,1)S(1)}, u32[]{:S(2)}, u32[]{:S(2)}) %collective-permute-start.68) | collective-permute-done | bytes 307232 | tf_op jit(solution)/shard_map/ppermute | solution.py:893
  377.1 3.4 finish_feed.2
  381.4 3.9 finish_feed.3
  385.4 3.5 finish_attention.1
  (251 shorter events, 146.2 us)
Async XLA Ops:
  7.2 68.3 %all-gather.3.cloned.1.call-start = ((), (), s32[]{:S(2)}) async-start(), calls=%async_computation.2 | async-start | bytes 2949120 | tf_op jit(solution)/shard_map/all_gather | solution.py:931
  15.3 110.3 %all-gather.5.cloned.1.call-start = ((), (), s32[]{:S(2)}) async-start(), calls=%async_computation.3 | async-start | bytes 2211840 | tf_op jit(solution)/shard_map/all_gather | solution.py:931
  15.4 25.4 %collective-permute-start = (bf16[128,768]{1,0:T(8,128)(2,1)S(1)}, bf16[128,768]{1,0:T(8,128)(2,1)S(1)}, u32[]{:S(2)}, u32[]{:S(2)}) collective-permute-start(bf16[128,768]{1,0:T(8,128)(2,1)S(1)} %dynamic-slice_bitcast_fusion.4.x0.prev_in), channel_id=1, source_target_pairs={{0,2},{2,0},{4,6},{6,4},{1,3},{3,1},{5,7},{7,5},{8,10},{10,8},{12,... | collective-permute-start | bytes 589832 | tf_op jit(solution)/shard_map/ppermute | solution.py:893
  18.0 22.9 %collective-permute-start.1 = (bf16[128,768]{1,0:T(8,128)(2,1)S(1)}, bf16[128,768]{1,0:T(8,128)(2,1)S(1)}, u32[]{:S(2)}, u32[]{:S(2)}) collective-permute-start(bf16[128,768]{1,0:T(8,128)(2,1)S(1)} %dynamic-slice_bitcast_fusion.4.x0.prev_in), channel_id=1, source_target_pairs={{0,4},{2,6},{4,0},{6,2},{1,5},{3,7},{5,1},{7,3},{8,12},{10,14},{12... | collective-permute-start | bytes 589832 | tf_op jit(solution)/shard_map/ppermute | solution.py:893
  21.2 18.5 %collective-permute-start.5 = (bf16[192,384]{1,0:T(8,128)(2,1)S(1)}, bf16[192,384]{1,0:T(8,128)(2,1)S(1)}, u32[]{:S(2)}, u32[]{:S(2)}) collective-permute-start(bf16[192,384]{1,0:T(8,128)(2,1)S(1)} %get-tuple-element.336), channel_id=1, source_target_pairs={{0,16},{8,24},{16,0},{24,8},{1,17},{9,25},{17,1},{25,9},{2,18},{10... | collective-permute-start | bytes 442376 | tf_op jit(solution)/shard_map/ppermute | solution.py:937
  23.8 15.9 %collective-permute-start.6 = (bf16[192,384]{1,0:T(8,128)(2,1)S(1)}, bf16[192,384]{1,0:T(8,128)(2,1)S(1)}, u32[]{:S(2)}, u32[]{:S(2)}) collective-permute-start(bf16[192,384]{1,0:T(8,128)(2,1)S(1)} %get-tuple-element.336), channel_id=1, source_target_pairs={{0,24},{8,16},{16,8},{24,0},{1,25},{9,17},{17,9},{25,1},{2,26},{10... | collective-permute-start | bytes 442376 | tf_op jit(solution)/shard_map/ppermute | solution.py:937
  27.5 13.4 %collective-permute-start.2 = (bf16[128,768]{1,0:T(8,128)(2,1)S(1)}, bf16[128,768]{1,0:T(8,128)(2,1)S(1)}, u32[]{:S(2)}, u32[]{:S(2)}) collective-permute-start(bf16[128,768]{1,0:T(8,128)(2,1)S(1)} %dynamic-slice_bitcast_fusion.4.x0.prev_in), channel_id=1, source_target_pairs={{0,6},{2,4},{4,2},{6,0},{1,7},{3,5},{5,3},{7,1},{8,14},{10,12},{12... | collective-permute-start | bytes 589832 | tf_op jit(solution)/shard_map/ppermute | solution.py:893
  52.3 8.8 %collective-permute-start.10 = (bf16[128,768]{1,0:T(8,128)(2,1)S(1)}, bf16[128,768]{1,0:T(8,128)(2,1)S(1)}, u32[]{:S(2)}, u32[]{:S(2)}) collective-permute-start(bf16[128,768]{1,0:T(8,128)(2,1)S(1)} %get-tuple-element.165), channel_id=1, source_target_pairs={{0,6},{2,4},{4,2},{6,0},{1,7},{3,5},{5,3},{7,1},{8,14},{10,12},{12... | collective-permute-start | bytes 589832 | tf_op jit(solution)/shard_map/ppermute | solution.py:893
  52.7 10.6 %collective-permute-start.8 = (bf16[128,768]{1,0:T(8,128)(2,1)S(1)}, bf16[128,768]{1,0:T(8,128)(2,1)S(1)}, u32[]{:S(2)}, u32[]{:S(2)}) collective-permute-start(bf16[128,768]{1,0:T(8,128)(2,1)S(1)} %get-tuple-element.163), channel_id=1, source_target_pairs={{0,2},{2,0},{4,6},{6,4},{1,3},{3,1},{5,7},{7,5},{8,10},{10,8},{12,... | collective-permute-start | bytes 589832 | tf_op jit(solution)/shard_map/ppermute | solution.py:893
  54.2 10.2 %collective-permute-start.9 = (bf16[128,768]{1,0:T(8,128)(2,1)S(1)}, bf16[128,768]{1,0:T(8,128)(2,1)S(1)}, u32[]{:S(2)}, u32[]{:S(2)}) collective-permute-start(bf16[128,768]{1,0:T(8,128)(2,1)S(1)} %get-tuple-element.164), channel_id=1, source_target_pairs={{0,4},{2,6},{4,0},{6,2},{1,5},{3,7},{5,1},{7,3},{8,12},{10,14},{12... | collective-permute-start | bytes 589832 | tf_op jit(solution)/shard_map/ppermute | solution.py:893
  77.5 186.5 %reduce-scatter.3.cloned.1.call-start = ((), (), s32[]{:S(2)}) async-start(), calls=%async_computation.4 | async-start | bytes 2211840 | tf_op jit(solution)/shard_map/reduce_scatter | solution.py:1014
  77.8 8.7 %collective-permute-start.16 = (bf16[128,768]{1,0:T(8,128)(2,1)S(1)}, bf16[128,768]{1,0:T(8,128)(2,1)S(1)}, u32[]{:S(2)}, u32[]{:S(2)}) collective-permute-start(bf16[128,768]{1,0:T(8,128)(2,1)S(1)} %get-tuple-element.166.x_ref), channel_id=1, source_target_pairs={{0,6},{2,4},{4,2},{6,0},{1,7},{3,5},{5,3},{7,1},{8,14},{10,12},{12... | collective-permute-start | bytes 589832 | tf_op jit(solution)/shard_map/ppermute | solution.py:893
  78.2 11.8 %collective-permute-start.14 = (bf16[128,768]{1,0:T(8,128)(2,1)S(1)}, bf16[128,768]{1,0:T(8,128)(2,1)S(1)}, u32[]{:S(2)}, u32[]{:S(2)}) collective-permute-start(bf16[128,768]{1,0:T(8,128)(2,1)S(1)} %get-tuple-element.166.x_ref), channel_id=1, source_target_pairs={{0,4},{2,6},{4,0},{6,2},{1,5},{3,7},{5,1},{7,3},{8,12},{10,14},{12... | collective-permute-start | bytes 589832 | tf_op jit(solution)/shard_map/ppermute | solution.py:893
  79.8 14.9 %collective-permute-start.12 = (bf16[128,768]{1,0:T(8,128)(2,1)S(1)}, bf16[128,768]{1,0:T(8,128)(2,1)S(1)}, u32[]{:S(2)}, u32[]{:S(2)}) collective-permute-start(bf16[128,768]{1,0:T(8,128)(2,1)S(1)} %get-tuple-element.166.x_ref), channel_id=1, source_target_pairs={{0,2},{2,0},{4,6},{6,4},{1,3},{3,1},{5,7},{7,5},{8,10},{10,8},{12,... | collective-permute-start | bytes 589832 | tf_op jit(solution)/shard_map/ppermute | solution.py:893
  89.6 9.7 %collective-permute-start.17 = (bf16[128,768]{1,0:T(8,128)(2,1)S(1)}, bf16[128,768]{1,0:T(8,128)(2,1)S(1)}, u32[]{:S(2)}, u32[]{:S(2)}) collective-permute-start(bf16[128,768]{1,0:T(8,128)(2,1)S(1)} %get-tuple-element.174), channel_id=1, source_target_pairs={{0,6},{2,4},{4,2},{6,0},{1,7},{3,5},{5,3},{7,1},{8,14},{10,12},{12... | collective-permute-start | bytes 589832 | tf_op jit(solution)/shard_map/ppermute | solution.py:893
  107.1 8.7 %collective-permute-start.19 = (bf16[128,768]{1,0:T(8,128)(2,1)S(1)}, bf16[128,768]{1,0:T(8,128)(2,1)S(1)}, u32[]{:S(2)}, u32[]{:S(2)}) collective-permute-start(bf16[128,768]{1,0:T(8,128)(2,1)S(1)} %get-tuple-element.176.x0), channel_id=1, source_target_pairs={{0,4},{2,6},{4,0},{6,2},{1,5},{3,7},{5,1},{7,3},{8,12},{10,14},{12... | collective-permute-start | bytes 589832 | tf_op jit(solution)/shard_map/ppermute | solution.py:893
  125.6 17.5 %collective-permute-start.24 = (bf16[768,1152]{1,0:T(8,128)(2,1)}, bf16[768,1152]{1,0:T(8,128)(2,1)S(1)}, u32[]{:S(2)}, u32[]{:S(2)}) collective-permute-start(bf16[768,1152]{1,0:T(8,128)(2,1)} %all-gather.5.cloned.1.call-done.own), channel_id=1, source_target_pairs={{0,1},{1,0},{2,3},{3,2},{4,5},{5,4},{6,7},{7,6},{8,9},{9,8},{10,11... | collective-permute-start | bytes 5308424 | tf_op jit(solution)/shard_map/ppermute | solution.py:890
  126.4 11.2 %collective-permute-start.22 = (bf16[128,768]{1,0:T(8,128)(2,1)S(1)}, bf16[128,768]{1,0:T(8,128)(2,1)S(1)}, u32[]{:S(2)}, u32[]{:S(2)}) collective-permute-start(bf16[128,768]{1,0:T(8,128)(2,1)S(1)} %get-tuple-element.179), channel_id=1, source_target_pairs={{0,4},{2,6},{4,0},{6,2},{1,5},{3,7},{5,1},{7,3},{8,12},{10,14},{12... | collective-permute-start | bytes 589832 | tf_op jit(solution)/shard_map/ppermute | solution.py:893
  127.5 10.1 %collective-permute-start.23 = (bf16[128,768]{1,0:T(8,128)(2,1)S(1)}, bf16[128,768]{1,0:T(8,128)(2,1)S(1)}, u32[]{:S(2)}, u32[]{:S(2)}) collective-permute-start(bf16[128,768]{1,0:T(8,128)(2,1)S(1)} %get-tuple-element.180), channel_id=1, source_target_pairs={{0,6},{2,4},{4,2},{6,0},{1,7},{3,5},{5,3},{7,1},{8,14},{10,12},{12... | collective-permute-start | bytes 589832 | tf_op jit(solution)/shard_map/ppermute | solution.py:893
  139.6 8.8 %collective-permute-start.29 = (bf16[128,768]{1,0:T(8,128)(2,1)S(1)}, bf16[128,768]{1,0:T(8,128)(2,1)S(1)}, u32[]{:S(2)}, u32[]{:S(2)}) collective-permute-start(bf16[128,768]{1,0:T(8,128)(2,1)S(1)} %get-tuple-element.182.x_ref), channel_id=1, source_target_pairs={{0,6},{2,4},{4,2},{6,0},{1,7},{3,5},{5,3},{7,1},{8,14},{10,12},{12... | collective-permute-start | bytes 589832 | tf_op jit(solution)/shard_map/ppermute | solution.py:893
  141.3 11.8 %collective-permute-start.27 = (bf16[128,768]{1,0:T(8,128)(2,1)S(1)}, bf16[128,768]{1,0:T(8,128)(2,1)S(1)}, u32[]{:S(2)}, u32[]{:S(2)}) collective-permute-start(bf16[128,768]{1,0:T(8,128)(2,1)S(1)} %get-tuple-element.182.x_ref), channel_id=1, source_target_pairs={{0,4},{2,6},{4,0},{6,2},{1,5},{3,7},{5,1},{7,3},{8,12},{10,14},{12... | collective-permute-start | bytes 589832 | tf_op jit(solution)/shard_map/ppermute | solution.py:893
  142.5 14.9 %collective-permute-start.25 = (bf16[128,768]{1,0:T(8,128)(2,1)S(1)}, bf16[128,768]{1,0:T(8,128)(2,1)S(1)}, u32[]{:S(2)}, u32[]{:S(2)}) collective-permute-start(bf16[128,768]{1,0:T(8,128)(2,1)S(1)} %get-tuple-element.182.x_ref), channel_id=1, source_target_pairs={{0,2},{2,0},{4,6},{6,4},{1,3},{3,1},{5,7},{7,5},{8,10},{10,8},{12,... | collective-permute-start | bytes 589832 | tf_op jit(solution)/shard_map/ppermute | solution.py:893
  151.4 9.6 %collective-permute-start.30 = (bf16[128,768]{1,0:T(8,128)(2,1)S(1)}, bf16[128,768]{1,0:T(8,128)(2,1)S(1)}, u32[]{:S(2)}, u32[]{:S(2)}) collective-permute-start(bf16[128,768]{1,0:T(8,128)(2,1)S(1)} %get-tuple-element.192), channel_id=1, source_target_pairs={{0,6},{2,4},{4,2},{6,0},{1,7},{3,5},{5,3},{7,1},{8,14},{10,12},{12... | collective-permute-start | bytes 589832 | tf_op jit(solution)/shard_map/ppermute | solution.py:893
  170.8 9.8 %collective-permute-start.33 = (bf16[128,768]{1,0:T(8,128)(2,1)S(1)}, bf16[128,768]{1,0:T(8,128)(2,1)S(1)}, u32[]{:S(2)}, u32[]{:S(2)}) collective-permute-start(bf16[128,768]{1,0:T(8,128)(2,1)S(1)} %get-tuple-element.195.g_ref.refs_4_), channel_id=1, source_target_pairs={{0,4},{2,6},{4,0},{6,2},{1,5},{3,7},{5,1},{7,3},{8,12},{10,14},{12... | collective-permute-start | bytes 589832 | tf_op jit(solution)/shard_map/ppermute | solution.py:893
  171.7 13.2 %collective-permute-start.32 = (bf16[128,768]{1,0:T(8,128)(2,1)S(1)}, bf16[128,768]{1,0:T(8,128)(2,1)S(1)}, u32[]{:S(2)}, u32[]{:S(2)}) collective-permute-start(bf16[128,768]{1,0:T(8,128)(2,1)S(1)} %get-tuple-element.195.g_ref.refs_4_), channel_id=1, source_target_pairs={{0,2},{2,0},{4,6},{6,4},{1,3},{3,1},{5,7},{7,5},{8,10},{10,8},{12,... | collective-permute-start | bytes 589832 | tf_op jit(solution)/shard_map/ppermute | solution.py:893
  202.2 10.4 %collective-permute-start.40 = (bf16[128,768]{1,0:T(8,128)(2,1)S(1)}, bf16[128,768]{1,0:T(8,128)(2,1)S(1)}, u32[]{:S(2)}, u32[]{:S(2)}) collective-permute-start(bf16[128,768]{1,0:T(8,128)(2,1)S(1)} %get-tuple-element.218.g0), channel_id=1, source_target_pairs={{0,4},{2,6},{4,0},{6,2},{1,5},{3,7},{5,1},{7,3},{8,12},{10,14},{12... | collective-permute-start | bytes 589832 | tf_op jit(solution)/shard_map/ppermute | solution.py:893
  203.0 9.6 %collective-permute-start.41 = (bf16[128,768]{1,0:T(8,128)(2,1)S(1)}, bf16[128,768]{1,0:T(8,128)(2,1)S(1)}, u32[]{:S(2)}, u32[]{:S(2)}) collective-permute-start(bf16[128,768]{1,0:T(8,128)(2,1)S(1)} %get-tuple-element.218.g0), channel_id=1, source_target_pairs={{0,6},{2,4},{4,2},{6,0},{1,7},{3,5},{5,3},{7,1},{8,14},{10,12},{12... | collective-permute-start | bytes 589832 | tf_op jit(solution)/shard_map/ppermute | solution.py:893
  204.6 130.2 %reduce-scatter.5.cloned.1.call-start = ((), (), s32[]{:S(2)}) async-start(), calls=%async_computation.5 | async-start | bytes 2949120 | tf_op jit(solution)/shard_map/reduce_scatter | solution.py:1014
  222.3 9.2 %collective-permute-start.43 = (bf16[128,768]{1,0:T(8,128)(2,1)S(1)}, bf16[128,768]{1,0:T(8,128)(2,1)S(1)}, u32[]{:S(2)}, u32[]{:S(2)}) collective-permute-start(bf16[128,768]{1,0:T(8,128)(2,1)S(1)} %get-tuple-element.228), channel_id=1, source_target_pairs={{0,4},{2,6},{4,0},{6,2},{1,5},{3,7},{5,1},{7,3},{8,12},{10,14},{12... | collective-permute-start | bytes 589832 | tf_op jit(solution)/shard_map/ppermute | solution.py:893
  235.3 10.4 %collective-permute-start.46 = (bf16[128,768]{1,0:T(8,128)(2,1)S(1)}, bf16[128,768]{1,0:T(8,128)(2,1)S(1)}, u32[]{:S(2)}, u32[]{:S(2)}) collective-permute-start(bf16[128,768]{1,0:T(8,128)(2,1)S(1)} %get-tuple-element.231.g_ref.refs_4_), channel_id=1, source_target_pairs={{0,4},{2,6},{4,0},{6,2},{1,5},{3,7},{5,1},{7,3},{8,12},{10,14},{12... | collective-permute-start | bytes 589832 | tf_op jit(solution)/shard_map/ppermute | solution.py:893
  236.7 13.4 %collective-permute-start.45 = (bf16[128,768]{1,0:T(8,128)(2,1)S(1)}, bf16[128,768]{1,0:T(8,128)(2,1)S(1)}, u32[]{:S(2)}, u32[]{:S(2)}) collective-permute-start(bf16[128,768]{1,0:T(8,128)(2,1)S(1)} %get-tuple-element.231.g_ref.refs_4_), channel_id=1, source_target_pairs={{0,2},{2,0},{4,6},{6,4},{1,3},{3,1},{5,7},{7,5},{8,10},{10,8},{12,... | collective-permute-start | bytes 589832 | tf_op jit(solution)/shard_map/ppermute | solution.py:893
  243.9 9.2 %collective-permute-start.48 = (bf16[128,768]{1,0:T(8,128)(2,1)S(1)}, bf16[128,768]{1,0:T(8,128)(2,1)S(1)}, u32[]{:S(2)}, u32[]{:S(2)}) collective-permute-start(bf16[128,768]{1,0:T(8,128)(2,1)S(1)} %get-tuple-element.239), channel_id=1, source_target_pairs={{0,6},{2,4},{4,2},{6,0},{1,7},{3,5},{5,3},{7,1},{8,14},{10,12},{12... | collective-permute-start | bytes 589832 | tf_op jit(solution)/shard_map/ppermute | solution.py:893
  274.1 9.2 %collective-permute-start.55 = (bf16[128,768]{1,0:T(8,128)(2,1)S(1)}, bf16[128,768]{1,0:T(8,128)(2,1)S(1)}, u32[]{:S(2)}, u32[]{:S(2)}) collective-permute-start(bf16[128,768]{1,0:T(8,128)(2,1)S(1)} %get-tuple-element.257.g0), channel_id=1, source_target_pairs={{0,6},{2,4},{4,2},{6,0},{1,7},{3,5},{5,3},{7,1},{8,14},{10,12},{12... | collective-permute-start | bytes 589832 | tf_op jit(solution)/shard_map/ppermute | solution.py:893
  295.4 15.8 %collective-permute-start.62 = (bf16[768,384]{1,0:T(8,128)(2,1)S(1)}, bf16[768,384]{1,0:T(8,128)(2,1)S(1)}, u32[]{:S(2)}, u32[]{:S(2)}) collective-permute-start(bf16[768,384]{1,0:T(8,128)(2,1)S(1)} %get-tuple-element.277), channel_id=1, source_target_pairs={{0,1},{1,0},{2,3},{3,2},{4,5},{5,4},{6,7},{7,6},{8,9},{9,8},{10,11... | collective-permute-start | bytes 1769480 | tf_op jit(solution)/shard_map/ppermute | solution.py:890
  295.5 12.6 %collective-permute-start.56 = (bf16[192,1152]{1,0:T(8,128)(2,1)S(1)}, bf16[192,1152]{1,0:T(8,128)(2,1)S(1)}, u32[]{:S(2)}, u32[]{:S(2)}) collective-permute-start(bf16[192,1152]{1,0:T(8,128)(2,1)S(1)} %copy-done.3), channel_id=1, source_target_pairs={{0,2},{2,0},{4,6},{6,4},{1,3},{3,1},{5,7},{7,5},{8,10},{10,8},{12,... | collective-permute-start | bytes 1327112 | tf_op jit(solution)/shard_map/ppermute | solution.py:893
  297.1 12.2 %collective-permute-start.57 = (bf16[192,1152]{1,0:T(8,128)(2,1)S(1)}, bf16[192,1152]{1,0:T(8,128)(2,1)S(1)}, u32[]{:S(2)}, u32[]{:S(2)}) collective-permute-start(bf16[192,1152]{1,0:T(8,128)(2,1)S(1)} %copy-done.3), channel_id=1, source_target_pairs={{0,4},{2,6},{4,0},{6,2},{1,5},{3,7},{5,1},{7,3},{8,12},{10,14},{12... | collective-permute-start | bytes 1327112 | tf_op jit(solution)/shard_map/ppermute | solution.py:893
  309.3 23.9 %collective-permute-start.61 = (bf16[192,1152]{1,0:T(8,128)(2,1)S(1)}, bf16[192,1152]{1,0:T(8,128)(2,1)S(1)}, u32[]{:S(2)}, u32[]{:S(2)}) collective-permute-start(bf16[192,1152]{1,0:T(8,128)(2,1)S(1)} %copy-done.3), channel_id=1, source_target_pairs={{0,6},{2,4},{4,2},{6,0},{1,7},{3,5},{5,3},{7,1},{8,14},{10,12},{12... | collective-permute-start | bytes 1327112 | tf_op jit(solution)/shard_map/ppermute | solution.py:893
  318.3 14.9 %collective-permute-start.58 = (bf16[128,768]{1,0:T(8,128)(2,1)S(1)}, bf16[128,768]{1,0:T(8,128)(2,1)S(1)}, u32[]{:S(2)}, u32[]{:S(2)}) collective-permute-start(bf16[128,768]{1,0:T(8,128)(2,1)S(1)} %get-tuple-element.268), channel_id=1, source_target_pairs={{0,2},{2,0},{4,6},{6,4},{1,3},{3,1},{5,7},{7,5},{8,10},{10,8},{12,... | collective-permute-start | bytes 589832 | tf_op jit(solution)/shard_map/ppermute | solution.py:893
  319.1 14.0 %collective-permute-start.59 = (bf16[128,768]{1,0:T(8,128)(2,1)S(1)}, bf16[128,768]{1,0:T(8,128)(2,1)S(1)}, u32[]{:S(2)}, u32[]{:S(2)}) collective-permute-start(bf16[128,768]{1,0:T(8,128)(2,1)S(1)} %get-tuple-element.269), channel_id=1, source_target_pairs={{0,4},{2,6},{4,0},{6,2},{1,5},{3,7},{5,1},{7,3},{8,12},{10,14},{12... | collective-permute-start | bytes 589832 | tf_op jit(solution)/shard_map/ppermute | solution.py:893
  320.6 12.6 %collective-permute-start.60 = (bf16[128,768]{1,0:T(8,128)(2,1)S(1)}, bf16[128,768]{1,0:T(8,128)(2,1)S(1)}, u32[]{:S(2)}, u32[]{:S(2)}) collective-permute-start(bf16[128,768]{1,0:T(8,128)(2,1)S(1)} %get-tuple-element.270), channel_id=1, source_target_pairs={{0,6},{2,4},{4,2},{6,0},{1,7},{3,5},{5,3},{7,1},{8,14},{10,12},{12... | collective-permute-start | bytes 589832 | tf_op jit(solution)/shard_map/ppermute | solution.py:893
  322.5 10.6 %collective-permute-start.65 = (bf16[208,384]{1,0:T(8,128)(2,1)S(1)}, bf16[208,384]{1,0:T(8,128)(2,1)S(1)}, u32[]{:S(2)}, u32[]{:S(2)}) collective-permute-start(bf16[208,384]{1,0:T(8,128)(2,1)S(1)} %get-tuple-element.288), channel_id=1, source_target_pairs={{0,24},{8,16},{16,8},{24,0},{1,25},{9,17},{17,9},{25,1},{2,26},{10... | collective-permute-start | bytes 479240 | tf_op jit(solution)/shard_map/ppermute | solution.py:937
  335.8 10.3 %collective-permute-start.67 = (bf16[400,384]{1,0:T(8,128)(2,1)S(1)}, bf16[400,384]{1,0:T(8,128)(2,1)S(1)}, u32[]{:S(2)}, u32[]{:S(2)}) collective-permute-start(bf16[400,384]{1,0:T(8,128)(2,1)S(1)} %pad_maximum_fusion.4.refs_0_), channel_id=1, source_target_pairs={{0,2},{2,0},{4,6},{6,4},{1,3},{3,1},{5,7},{7,5},{8,10},{10,8},{12,... | collective-permute-start | bytes 921608 | tf_op jit(solution)/shard_map/ppermute | solution.py:893
  337.7 34.8 %collective-permute-start.70 = (bf16[192,1152]{1,0:T(8,128)(2,1)S(1)}, bf16[192,1152]{1,0:T(8,128)(2,1)}, u32[]{:S(2)}, u32[]{:S(2)}) collective-permute-start(bf16[192,1152]{1,0:T(8,128)(2,1)S(1)} %slice.93.refs_0_), channel_id=1, source_target_pairs={{0,2},{2,0},{4,6},{6,4},{1,3},{3,1},{5,7},{7,5},{8,10},{10,8},{12,... | collective-permute-start | bytes 1327112 | tf_op jit(solution)/shard_map/ppermute | solution.py:893
  339.0 33.6 %collective-permute-start.71 = (bf16[192,1152]{1,0:T(8,128)(2,1)S(1)}, bf16[192,1152]{1,0:T(8,128)(2,1)}, u32[]{:S(2)}, u32[]{:S(2)}) collective-permute-start(bf16[192,1152]{1,0:T(8,128)(2,1)S(1)} %slice.93.refs_0_), channel_id=1, source_target_pairs={{0,4},{2,6},{4,0},{6,2},{1,5},{3,7},{5,1},{7,3},{8,12},{10,14},{12... | collective-permute-start | bytes 1327112 | tf_op jit(solution)/shard_map/ppermute | solution.py:893
  340.2 32.4 %collective-permute-start.72 = (bf16[192,1152]{1,0:T(8,128)(2,1)S(1)}, bf16[192,1152]{1,0:T(8,128)(2,1)}, u32[]{:S(2)}, u32[]{:S(2)}) collective-permute-start(bf16[192,1152]{1,0:T(8,128)(2,1)S(1)} %slice.93.refs_0_), channel_id=1, source_target_pairs={{0,6},{2,4},{4,2},{6,0},{1,7},{3,5},{5,3},{7,1},{8,14},{10,12},{12... | collective-permute-start | bytes 1327112 | tf_op jit(solution)/shard_map/ppermute | solution.py:893
  341.3 31.3 %collective-permute-start.68 = (bf16[400,384]{1,0:T(8,128)(2,1)S(1)}, bf16[400,384]{1,0:T(8,128)(2,1)S(1)}, u32[]{:S(2)}, u32[]{:S(2)}) collective-permute-start(bf16[400,384]{1,0:T(8,128)(2,1)S(1)} %pad_maximum_fusion.4.refs_0_), channel_id=1, source_target_pairs={{0,4},{2,6},{4,0},{6,2},{1,5},{3,7},{5,1},{7,3},{8,12},{10,14},{12... | collective-permute-start | bytes 921608 | tf_op jit(solution)/shard_map/ppermute | solution.py:893
  346.0 26.5 %collective-permute-start.69 = (bf16[400,384]{1,0:T(8,128)(2,1)S(1)}, bf16[400,384]{1,0:T(8,128)(2,1)S(1)}, u32[]{:S(2)}, u32[]{:S(2)}) collective-permute-start(bf16[400,384]{1,0:T(8,128)(2,1)S(1)} %pad_maximum_fusion.4.refs_0_), channel_id=1, source_target_pairs={{0,6},{2,4},{4,2},{6,0},{1,7},{3,5},{5,3},{7,1},{8,14},{10,12},{12... | collective-permute-start | bytes 921608 | tf_op jit(solution)/shard_map/ppermute | solution.py:893
  373.3 12.1 %collective-permute-start.73 = (bf16[864,384]{1,0:T(8,128)(2,1)S(1)}, bf16[864,384]{1,0:T(8,128)(2,1)S(1)}, u32[]{:S(2)}, u32[]{:S(2)}) collective-permute-start(bf16[864,384]{1,0:T(8,128)(2,1)S(1)} %choose.1), channel_id=1, source_target_pairs={{0,1},{1,0},{2,3},{3,2},{4,5},{5,4},{6,7},{7,6},{8,9},{9,8},{10,11... | collective-permute-start | bytes 1990664 | tf_op jit(solution)/shard_map/ppermute | solution.py:890
  (57 other events, 542.9 us)
Sparse Core Ops, SparseCore 0:
  15.5 60.0 all-gather.2
  77.7 42.3 all-gather.4
  204.7 41.2 reduce-scatter.2
  263.5 50.3 reduce-scatter.4

commit v3 on v2

--- a/solution.py
+++ b/solution.py
@@ -111,6 +111,28 @@
 def pick(flag, one, two):
     chosen = jnp.full(one.shape, flag, jnp.int32) == 1
     return jnp.where(chosen, wide(one[...]), wide(two[...])).astype(jnp.bfloat16)
+
+
+def stage_kernel(*refs):
+    *refs, sem = refs
+    count = len(refs) // 2
+    copies = []
+    for i, (source, target) in enumerate(zip(refs[:count], refs[count:])):
+        if source.shape != target.shape:
+            source = source.at[:, : target.shape[1]]
+        copies.append(start(source, target, sem.at[i]))
+    for copy in copies:
+        copy.wait()
+
+
+def stage(arrays, columns=None):
+    outs = [
+        ((a.shape[0], columns) if columns and a.shape[0] > columns // 2 else a.shape, a.dtype)
+        for a in arrays
+    ]
+    return call(
+        stage_kernel, "stage", outs, *[("h", a) for a in arrays], scratch=[sems(len(arrays))], limit=4
+    )
 
 
 def attend_kernel(count, at, info, slope_ref, x0, x1, x2, x3, own, other, bias, *refs):
@@ -214,27 +236,19 @@
     )
 
 
-def attend_back_kernel(g0, g1, g2, g3, w_in, qkvm_in, probs_in, *refs):
-    out_ref, sum_ref, *sends = refs[-13:-7]
-    w, qkvm, probs_ref, gs_ref, gm_ref, sem, sem_w = refs[-7:]
+def attend_back_kernel(g0, g1, g2, g3, w, qkvm, probs_ref, *refs):
+    out_ref, sum_ref, *sends, gs_ref, gm_ref = refs
     blocks = (g0, g1, g2, g3)
     rows = g0.shape[0]
     cols = w.shape[1] // 4
     heads = cols // HEAD_DIM
     scale = HEAD_DIM**-0.5
-    weights = start(w_in, w, sem_w)
-    first = start(qkvm_in, qkvm, sem.at[0])
-    rest = [start(probs_in.at[h], probs_ref.at[h], sem.at[1 + h]) for h in range(heads)]
-    g = join(blocks)
-    weights.wait()
-    gm_ref[...] = low(dot(g, w[:, 3 * cols :]))
-    first.wait()
+    gm_ref[...] = low(dot(join(blocks), w[:, 3 * cols :]))
     for h in range(heads):
         lo = h * HEAD_DIM
         query = qkvm[:, lo : lo + HEAD_DIM]
         key = qkvm[:, cols + lo : cols + lo + HEAD_DIM]
         value = qkvm[:, 2 * cols + lo : 2 * cols + lo + HEAD_DIM]
-        rest[h].wait()
         for b in range(len(blocks)):
             span = slice(b * rows, (b + 1) * rows)
             probs = wide(probs_ref[h, span, :])
@@ -256,7 +270,7 @@
     sum_ref[...] = jnp.broadcast_to(sums, sum_ref.shape)
 
 
-def attend_back(blocks, w, qkvm, probs, after):
+def attend_back(blocks, w, qkvm, probs):
     rows, width = blocks[0].shape
     total = rows * len(blocks)
     cols = w.shape[1] // 4
@@ -270,31 +284,17 @@
         "attend_back",
         outs,
         *blocks,
-        ("h", w),
-        ("h", qkvm),
-        ("h", probs),
-        *[("d", a) for a in after],
-        scratch=[
-            bf16(*w.shape),
-            bf16(total, 4 * cols),
-            bf16(heads, total, total),
-            bf16(total, total),
-            bf16(total, cols),
-            sems(1 + heads),
-            pltpu.SemaphoreType.DMA,
-        ],
+        w,
+        qkvm,
+        probs,
+        scratch=[bf16(total, total), bf16(total, cols)],
         flops=32 * heads * total * total * HEAD_DIM + 8 * total * width * cols,
     )
 
 
-def attend_weights_kernel(info, g0, g1, g2, g3, dqkv, xs_in, qkvm_in, give, keep, xs, mixed, sem):
+def attend_weights_kernel(info, g0, g1, g2, g3, dqkv, xs, qkvm, give, keep):
     cols = dqkv.shape[1] // 3
-    extra = mixed.shape[1] - cols
-    first = start(xs_in, xs, sem.at[0])
-    second = start(qkvm_in.at[:, 3 * cols - extra :], mixed, sem.at[1])
-    second.wait()
-    out = contract_rows(join((g0, g1, g2, g3)), mixed[:, extra:])
-    first.wait()
+    out = contract_rows(join((g0, g1, g2, g3)), qkvm[:, 3 * cols :])
     query_key = contract_rows(xs[...], dqkv[:, : 2 * cols])
     value = contract_rows(xs[...], dqkv[:, 2 * cols :])
     value_out = jnp.concatenate([value, out], axis=1)
@@ -314,9 +314,8 @@
         ("s", info),
         *g,
         dqkv,
-        ("h", xs),
-        ("h", qkvm),
-        scratch=[bf16(total, width), bf16(total, -(-cols // 128) * 128), sems(2)],
+        xs,
+        qkvm,
         flops=8 * total * width * cols,
     )
 
@@ -354,28 +353,13 @@
     return call(total_kernel, "total", [(blocks[0].shape, jnp.bfloat16)], *blocks)[0]
 
 
-def fetch(weights, scratch, sem, order):
-    unit = scratch[0].shape[1] // 3
-    cut = (slice(0, 2 * unit), slice(2 * unit, 3 * unit))
-    copies = {}
-    for i, (side, which) in enumerate(order):
-        span = cut[which]
-        copies[side, which] = start(
-            weights[side].at[:, span], scratch[side].at[:, span], sem.at[i]
-        )
-    return copies
-
-
-def feed_kernel(x_ref, own, other, part_ref, saved_out, saved, own_ref, other_ref, sem):
-    unit = own_ref.shape[1] // 3
-    scratch = (own_ref, other_ref)
-    copies = fetch((own, other), scratch, sem, ((0, 0), (1, 0), (0, 1), (1, 1)))
+def feed_kernel(x_ref, own, other, part_ref, saved_out, saved, sem):
+    unit = own.shape[1] // 3
     x = x_ref[...]
     width = x.shape[1]
-    first = start(x_ref, saved_out.at[:, :width], sem.at[4])
-    for side, w in enumerate(scratch):
+    first = start(x_ref, saved_out.at[:, :width], sem.at[0])
+    for side, w in enumerate((own, other)):
         lo = side * unit
-        copies[side, 0].wait()
         packed = dot(x, w[:, : 2 * unit])
         gate, up = packed[:, :unit], packed[:, unit:]
         phi = 0.5 + 0.5 * lax.erf(gate * (0.5**0.5))
@@ -384,19 +368,18 @@
         saved[:, lo : lo + unit] = low(gelu * up)
         saved[:, 2 * unit + lo : 3 * unit + lo] = low(up * (phi + gate * bell))
         saved[:, 4 * unit + lo : 5 * unit + lo] = low(gelu)
-    second = start(saved, saved_out.at[:, width:], sem.at[5])
-    copies[0, 1].wait()
-    copies[1, 1].wait()
+    second = start(saved, saved_out.at[:, width:], sem.at[1])
     part_ref[...] = low(
-        contract_cols(saved[:, :unit], own_ref[:, 2 * unit :])
-        + contract_cols(saved[:, unit : 2 * unit], other_ref[:, 2 * unit :])
+        contract_cols(saved[:, :unit], own[:, 2 * unit :])
+        + contract_cols(saved[:, unit : 2 * unit], other[:, 2 * unit :])
     )
     first.wait()
     second.wait()
 
 
-def feed(x, own, other, unit):
+def feed(x, own, other):
     rows, width = x.shape
+    unit = own.shape[1] // 3
     outs = [
         ((rows, width), jnp.bfloat16),
         ((rows, width + 6 * unit), jnp.bfloat16, "h"),
@@ -406,91 +389,60 @@
         "feed",
         outs,
         x,
-        ("h", own),
-        ("h", other),
-        scratch=[
-            bf16(rows, 6 * unit),
-            bf16(width, 3 * unit),
-            bf16(width, 3 * unit),
-            sems(6),
-        ],
+        own,
+        other,
+        scratch=[bf16(rows, 6 * unit), sems(2)],
         flops=12 * rows * width * unit,
         exps=4 * rows * unit,
-    )
-
-
-def feed_back_kernel(
-    g_ref, own, other, saved_in, part_ref, packed_ref, saved, own_ref, other_ref, sem
-):
-    scratch = (own_ref, other_ref)
-    copies = fetch((own, other), scratch, sem, ((0, 1), (1, 1)))
+        limit=8,
+    )
+
+
+def feed_back_kernel(g_ref, own, other, saved, part_ref, packed_ref):
     g = g_ref[...]
-    width = g.shape[1]
-    unit = own_ref.shape[1] // 3
-    copy = start(saved_in.at[:, width + 2 * unit :], saved, sem.at[4])
-    cut = slice(0, 2 * unit)
+    unit = own.shape[1] // 3
+    total = None
     for side, w in enumerate((own, other)):
-        copies[side, 0] = start(w.at[:, cut], scratch[side].at[:, cut], sem.at[2 + side])
-    grads = []
-    for side, w in enumerate(scratch):
-        copies[side, 1].wait()
-        grads.append(dot(g, w[:, 2 * unit :]))
-    copy.wait()
-    total = None
-    for side, w in enumerate(scratch):
-        lo = side * unit
+        lo = g.shape[1] + (2 + side) * unit
         at = 2 * side * unit
-        packed_ref[:, at : at + unit] = low(grads[side] * wide(saved[:, lo : lo + unit]))
+        grad = dot(g, w[:, 2 * unit :])
+        packed_ref[:, at : at + unit] = low(grad * wide(saved[:, lo : lo + unit]))
         packed_ref[:, at + unit : at + 2 * unit] = low(
-            grads[side] * wide(saved[:, 2 * unit + lo : 3 * unit + lo])
+            grad * wide(saved[:, 2 * unit + lo : 3 * unit + lo])
         )
-        copies[side, 0].wait()
         term = contract_cols(packed_ref[:, at : at + 2 * unit], w[:, : 2 * unit])
         total = term if total is None else total + term
     part_ref[...] = low(total)
 
 
-def feed_back(g, own, other, saved, unit):
+def feed_back(g, own, other, saved):
     rows, width = g.shape
+    unit = own.shape[1] // 3
     outs = [((rows, width), jnp.bfloat16), ((rows, 4 * unit), jnp.bfloat16)]
     return call(
         feed_back_kernel,
         "feed_back",
         outs,
         g,
-        ("h", own),
-        ("h", other),
-        ("h", saved),
-        scratch=[
-            bf16(rows, 4 * unit),
-            bf16(width, 3 * unit),
-            bf16(width, 3 * unit),
-            sems(5),
-        ],
+        own,
+        other,
+        saved,
         flops=12 * rows * width * unit,
+        limit=8,
     )
 
 
 def feed_weights_kernel(side, *refs):
-    saved_in, g, packed = refs[:4], refs[4:8], refs[8:12]
-    out, xs, act, sem = refs[-4:]
-    rows, width = g[0].shape
-    unit = act.shape[1]
+    saved, g, packed, out = refs[:4], refs[4:8], refs[8:12], refs[12]
+    width = g[0].shape[1]
+    unit = out.shape[1] // 3
+    lo = 2 * side * unit
     at = width + side * unit
-    copies = []
-    for b, ref in enumerate(saved_in):
-        span = slice(b * rows, (b + 1) * rows)
-        copies.append(start(ref.at[:, at : at + unit], act.at[span, :], sem.at[2 * b]))
-        copies.append(start(ref.at[:, :width], xs.at[span, :], sem.at[2 * b + 1]))
-    g_all = join(g)
-    lo = 2 * side * unit
+    act = jnp.concatenate([s[:, at : at + unit] for s in saved], axis=0)
+    out[:, 2 * unit :] = low(contract_rows(join(g), act))
+    x = jnp.concatenate([s[:, :width] for s in saved], axis=0)
     packed_all = jnp.concatenate([p[:, lo : lo + 2 * unit] for p in packed], axis=0)
-    for copy in copies[0::2]:
-        copy.wait()
-    out[:, 2 * unit :] = low(contract_rows(g_all, act[...]))
-    for copy in copies[1::2]:
-        copy.wait()
-    out[:, : 2 * unit] = low(contract_rows(xs[...], packed_all))
+    out[:, : 2 * unit] = low(contract_rows(x, packed_all))
 
 
 def feed_weights(side, saved, g, packed):
@@ -500,10 +452,9 @@
         functools.partial(feed_weights_kernel, side),
         "feed_weights",
         [((width, 3 * unit), jnp.bfloat16)],
-        *[("h", x) for x in saved],
+        *saved,
         *g,
         *packed,
-        scratch=[bf16(4 * rows, width), bf16(4 * rows, unit), sems(8)],
         flops=24 * rows * width * unit,
     )[0]
 
@@ -556,22 +507,21 @@
     glu_out, down_out, token, glu, down, sem = refs[-6:]
     parts, _, unit = down.shape
     token[...] = jnp.zeros_like(token)
-    near = refs[:parts] if len(refs[0].shape) == 2 else [refs[0].at[k] for k in range(parts)]
+    near = refs[:parts]
     copies = []
     for k, block in enumerate(near):
         span = pl.ds(pl.multiple_of((place[1] ^ k) * unit, 128), unit)
         glu[k, :, 0, :] = wide(block[:, :unit])
         glu[k, :, 1, :] = wide(block[:, unit : 2 * unit])
         copies.append(start(glu.at[k], glu_out.at[l, :, :, span], sem.at[2 * k]))
-        down[k] = wide(block[:, 2 * unit :])
+        down[k] = wide(block[:, 2 * unit : 3 * unit])
         copies.append(start(down.at[k], down_out.at[l, :, span], sem.at[2 * k + 1]))
     for copy in copies:
         copy.wait()
 
 
-def finish_feed(l, layers, place, near, parts, before):
-    rows, width = near[0].shape[-2:]
-    unit = width // 3
+def finish_feed(l, layers, place, near, unit, before):
+    rows, parts = near[0].shape[0], len(near)
     outs = [
         ((layers, rows, 2, unit * parts), jnp.float32, "h"),
         ((layers, rows, unit * parts), jnp.float32, "h"),
@@ -596,33 +546,37 @@
     )
 
 
-def choose_kernel(flags, *refs):
+def choose_kernel(parts, count, at, flags, *refs):
     *blocks, out = refs
+    pair = parts // 2
+    row = 0
+    for i in range(0, len(blocks), parts):
+        for k in range(pair):
+            near, far = blocks[i + k], blocks[i + pair + k]
+            columns = slice(at if i else 0, None)
+            near, far = wide(near[:, columns]), wide(far[:, columns])
+            home = jnp.full(near.shape, flags[0], jnp.int32) == 1
+            out[row : row + near.shape[0], :] = low(jnp.where(home, far, near))
+            row += near.shape[0]
+    for block in blocks[:parts]:
+        height, _ = block.shape
+        out[row : row + count, :] = block[height - count :, :]
+        row += count
+
+
+def choose(flags, blocks, others, count, at):
     parts = len(blocks)
-    pair = parts // 2
-    height, _ = blocks[0].shape
-    count = (out.shape[0] - pair * height) // parts
-    home = jnp.full(blocks[0].shape, flags[0], jnp.int32) == 1
-    for i in range(pair):
-        out[i * height : (i + 1) * height, :] = low(
-            jnp.where(home, wide(blocks[pair + i][...]), wide(blocks[i][...]))
-        )
-    for k, block in enumerate(blocks):
-        at = pair * height + k * count
-        out[at : at + count, :] = block[height - count :, :]
-
-
-def choose(flags, blocks, count):
-    parts = len(blocks)
-    height, width = blocks[0].shape
-    shape = (parts // 2 * height + parts * count, width)
-    return call(choose_kernel, "choose", [(shape, jnp.bfloat16)], ("s", flags), *blocks)[0]
-
-
-def finish_attention_kernel(groups, count, flags, *refs):
+    rows = sum(b[0].shape[0] for b in [blocks] + others) * (parts // 2) + parts * count
+    body = functools.partial(choose_kernel, parts, count, at)
+    given = [x for b in [blocks] + others for x in b]
+    out = ((rows, blocks[0].shape[1]), jnp.bfloat16)
+    return call(body, "choose", [out], ("s", flags), *given)[0]
+
+
+def finish_attention_kernel(groups, parts, count, from_col, flags, *refs):
     qkv_out, out_out, clip_out, small_out, weights, qkv, out, clip, sem = refs[-9:]
-    *blocks, came, weight_in = refs[:-9]
-    parts = len(blocks)
+    *given, came, weight_in = refs[:-9]
+    blocks = given[:parts]
     pair = parts // 2
     height, _ = blocks[0].shape
     layers, _, rows, half = qkv.shape
@@ -631,7 +585,7 @@
     fetched = [start(weight_in.at[l, :2], weights.at[l], sem.at[l]) for l in range(layers)]
     total, tops = None, []
     for k, block in enumerate(blocks):
-        at = pair * height + k * count
+        at = came.shape[0] - (parts - k) * count
         mine, theirs = wide(block[height - count :, :]), wide(came[at : at + count, :])
         both = mine[:, :cols] + theirs[:, :cols]
         total = both if total is None else total + both
@@ -650,9 +604,10 @@
     lane = lax.broadcasted_iota(jnp.int32, (1, half), 1) // HEAD_DIM
     copies = []
     for l in range(layers):
-        span = slice(l * rows, (l + 1) * rows)
-        near = [wide(b[span, :]) for b in blocks]
-        far = [wide(came[i * height + l * rows : i * height + (l + 1) * rows, :]) for i in range(pair)]
+        columns = slice(from_col if l else 0, None)
+        near = [wide(b[:rows, columns]) for b in given[l * parts : (l + 1) * parts]]
+        at, step = (pair * (height + (l - 1) * rows), rows) if l else (0, height)
+        far = [wide(came[at + i * step : at + i * step + rows, :]) for i in range(pair)]
         near = [jnp.where(home, near[i], near[pair + i]) for i in range(pair)]
         query_key = [jnp.where(even, near[0], near[1]), jnp.where(even, near[1], near[0])]
         value_out = [jnp.where(even, far[0], far[1]), jnp.where(even, far[1], far[0])]
@@ -682,7 +637,7 @@
         copy.wait()
 
 
-def finish_attention(groups, count, flags, blocks, came, weight):
+def finish_attention(groups, count, at, flags, blocks, others, came, weight):
     layers, _, rows, half = weight.shape
     outs = [
         ((layers, 3, rows, half), jnp.float32, "h"),
@@ -691,11 +646,11 @@
         ((count, half // 2), jnp.float32),
     ]
     return call(
-        functools.partial(finish_attention_kernel, groups, count),
+        functools.partial(finish_attention_kernel, groups, len(blocks), count, at),
         "finish_attention",
         outs,
         ("s", flags),
-        *blocks,
+        *[x for b in [blocks] + others for x in b],
         came,
         ("h", weight),
         scratch=[
@@ -736,25 +691,18 @@
     return total
 
 
-def norm_input(before, bias, parts, prev_in, prev, sem, vec_in, vec):
-    copy = start(prev_in, prev, sem.at[0])
-    other = start(vec_in, vec, sem.at[2])
-    z = summed(parts)
-    other.wait()
-    z = z + vec[bias : bias + 1, :]
-    copy.wait()
+def norm_input(before, bias, parts, prev, vec):
+    z = summed(parts) + vec[bias : bias + 1, :]
     if before is None:
         return z + wide(prev[...])
     return z + affine(normalised(prev[...])[0], vec, *before)
 
 
-def norm_kernel(
-    before, rows_of, p0, p1, p2, p3, prev_in, vec_in, low_ref, z_out, prev, zs, vec, sem
-):
+def norm_kernel(before, rows_of, p0, p1, p2, p3, prev, vec, low_ref, z_out, zs, sem):
     bias, gain, shift = rows_of
-    z = norm_input(before, bias, (p0, p1, p2, p3), prev_in, prev, sem, vec_in, vec)
+    z = norm_input(before, bias, (p0, p1, p2, p3), prev, vec)
     zs[...] = z
-    copy = start(zs, z_out, sem.at[1])
+    copy = start(zs, z_out, sem.at[0])
     low_ref[...] = low(affine(normalised(z)[0], vec, gain, shift))
     copy.wait()
 
@@ -767,9 +715,9 @@
         "norm",
         outs,
         *parts,
-        ("h", prev),
-        ("h", vec),
-        scratch=[pltpu.VMEM(shape, prev.dtype), f32(*shape), f32(*vec.shape), sems(3)],
+        prev,
+        vec,
+        scratch=[f32(*shape), sems(1)],
         flops=prev.size,
     )
 
@@ -790,18 +738,11 @@
     copy.wait()
 
 
-def norm_back_kernel(gain_row, p0, p1, p2, p3, skip_in, z_in, vec_in, *refs):
-    outs, (skip, zs, dzs, vec, sem) = refs[-8:-5], refs[-5:]
-    one = start(z_in, zs, sem.at[0])
-    two = start(skip_in, skip, sem.at[1])
-    three = start(vec_in, vec, sem.at[3])
-    grad = summed((p0, p1, p2, p3))
-    one.wait()
-    n, r = normalised(zs[...])
-    two.wait()
-    three.wait()
-    gain = vec[gain_row : gain_row + 1, :]
-    norm_grad(grad + skip[...], n, r, gain, *outs, dzs, sem.at[2])
+def norm_back_kernel(gain_row, p0, p1, p2, p3, skip, z, vec, *refs):
+    *outs, dzs, sem = refs
+    grad = summed((p0, p1, p2, p3)) + skip[...]
+    n, r = normalised(z[...])
+    norm_grad(grad, n, r, vec[gain_row : gain_row + 1, :], *outs, dzs, sem.at[0])
 
 
 def grad_outs(shape):
@@ -812,32 +753,31 @@
     ]
 
 
-def norm_back(gain_row, parts, skip, z, vec, after):
+def norm_back(gain_row, parts, skip, z, vec):
     shape = skip.shape
     return call(
         functools.partial(norm_back_kernel, gain_row),
         "norm_back",
         grad_outs(shape),
         *parts,
-        ("h", skip),
-        ("h", z),
-        ("h", vec),
-        *[("d", a) for a in after],
-        scratch=[f32(*shape), f32(*shape), f32(*shape), f32(*vec.shape), sems(4)],
+        skip,
+        z,
+        vec,
+        scratch=[f32(*shape), sems(1)],
         flops=skip.size,
     )
 
 
-def turn_kernel(before, rows_of, info, p0, p1, p2, p3, prev_in, vec_in, cot, out_ref, *refs):
-    outs, (prev, dzs, vec, sem) = refs[:3], refs[3:]
+def turn_kernel(before, rows_of, info, p0, p1, p2, p3, prev, vec, cot, out_ref, *refs):
+    *outs, dzs, sem = refs
     bias, gain, shift = rows_of
-    z = norm_input(before, bias, (p0, p1, p2, p3), prev_in, prev, sem, vec_in, vec)
+    z = norm_input(before, bias, (p0, p1, p2, p3), prev, vec)
     n, r = normalised(z)
     rows = z.shape[0]
     ok = info[0] * rows + lax.broadcasted_iota(jnp.int32, (rows, 1), 0) < info[1]
     out_ref[...] = low(jnp.where(ok, affine(n, vec, gain, shift), 0.0))
     grad = jnp.where(ok, wide(cot[...]), 0.0)
-    norm_grad(grad, n, r, vec[gain : gain + 1, :], *outs, dzs, sem.at[1])
+    norm_grad(grad, n, r, vec[gain : gain + 1, :], *outs, dzs, sem.at[0])
 
 
 def turn(before, rows_of, info, parts, prev, vec, cot):
@@ -849,10 +789,10 @@
         outs,
         ("s", info),
         *parts,
-        ("h", prev),
-        ("h", vec),
+        prev,
+        vec,
         cot,
-        scratch=[f32(*shape), f32(*shape), f32(*vec.shape), sems(3)],
+        scratch=[f32(*shape), sems(1)],
         flops=prev.size,
     )
 
@@ -898,9 +838,12 @@
     def own_first(work, blocks, extras):
         done = [work(blocks[0], extras[0])]
         for block, extra in zip(blocks[1:], extras[1:]):
-            block, _ = lax.optimization_barrier((block, done[0][0]))
+            block, _ = lax.optimization_barrier((block, done[-1][0]))
             done.append(work(block, extra))
         return zip(*done)
+
+    def behind(blocks, staged):
+        return [tie(blocks[0], staged[0])] + blocks[1:]
 
     def gather(x):
         return hops([x] * parts)
@@ -945,10 +888,11 @@
     ]
     early = over_dp(jnp.concatenate([feed_shard[0]] + attn_shard_later, axis=1))
     if direct:
-        own = jnp.concatenate([attn_first] + [hop_dp(attn_first, k) for k in range(1, groups)])
+        low_zero = gather(tokens_own)
+        own = lax.all_gather(attn_first, "dp", axis=0, tiled=True)
     else:
         own = over_dp(attn_first)
-    low_zero = gather(tokens_own)
+        low_zero = gather(tokens_own)
     attn_full[0] = (own, swap(own), 0)
     late = [over_dp(lax.optimization_barrier((x, own))[0]) for x in feed_shard[1:]]
 
@@ -957,7 +901,7 @@
     sequence = jnp.sum(jnp.where(slot_ids == slot, dealing, 0))
     length = jnp.sum(jnp.where(slot_ids == sequence, lengths, 0))
     info = [
-        jnp.stack([part, length, home, group if direct and l == 0 else jnp.int32(0)]).astype(
+        jnp.stack([part, length, home, jnp.int32(0)]).astype(
             jnp.int32
         )
         for l in range(layers)
@@ -982,34 +926,38 @@
             x_low,
             *attn_full[l],
             qkv_bias[l],
-            groups if direct and l == 0 else 1,
+            1,
         )
         tops.append(top)
-        hidden_low, z_one = norm(before, (v + 2, v + 6, v + 4), hops(sends), prev, vec)
+        near = stage([tie(prev, sends[0]), vec])
+        hidden_low, z_one = norm(before, (v + 2, v + 6, v + 4), behind(hops(sends), near), *near)
         feed_own = tie(early if l == 0 else late[l - 1], hidden_low if l == 0 else top)
         feed_full[l] = (feed_own, swap(feed_own))
         if l == 0:
             for n in range(1, layers):
                 attn_full[n] = (*feed_full[0], 3 * quarter + 2 * cols * (n - 1))
         h_low = gather(hidden_low)
-        sends, kept = own_first(lambda h, _: feed(h, *feed_full[l], quarter), h_low, h_low)
+        near = stage([tie(w, hidden_low) for w in feed_full[l]], 3 * quarter)
+        sends, kept = own_first(lambda h, _: feed(h, *near), h_low, h_low)
         arrived = hops(sends)
         rows_of = (v + 3, v + 7, v + 5)
+        near = stage([tie(z_one, sends[0]), vec])
+        arrived = behind(arrived, near)
         if l + 1 < layers:
-            low_own, z_two = norm((v + 6, v + 4), rows_of, arrived, z_one, vec)
+            low_own, z_two = norm((v + 6, v + 4), rows_of, arrived, *near)
             prev, before = z_two, (v + 7, v + 5)
         else:
             cot = lax.dynamic_index_in_dim(cotangent, core, 0, keepdims=False)
             outputs, grad_two, low_two, stats_two = turn(
-                (v + 6, v + 4), rows_of, info[l], arrived, z_one, vec, cot
+                (v + 6, v + 4), rows_of, info[l], arrived, *near, cot
             )
             z_two = None
         saved.append((xs, qkvm, probs, attn_w, z_one, kept, z_two))
 
     feed_parts = [None] * layers
-    attn_parts = [None] * layers
     carried = None
     woven = [None] * layers
+
     def over_dp_sum(x):
         return lax.psum_scatter(x, "dp", scatter_dimension=0, tiled=True)
 
@@ -1020,38 +968,31 @@
         above = l + 1 < layers
         stats[l][1] = stats_two
         g_low = gather(low_two)
-        sends, packed = own_first(
-            lambda g, k: feed_back(g, *feed_full[l], k, quarter), g_low, kept
+        *near, k0, k1, k2, k3 = stage(
+            [tie(w, low_two) for w in (*feed_full[l], *kept)], 3 * quarter
         )
+        kept = [k0, k1, k2, k3]
+        sends, packed = own_first(lambda g, k: feed_back(g, *near, k), g_low, kept)
         arrived = hops(sends)
         packed = list(packed)
-        packed[0], arrived[3] = lax.optimization_barrier((packed[0], arrived[3]))
+        packed[0], arrived[1] = lax.optimization_barrier((packed[0], arrived[1]))
         give = feed_weights(1, kept, g_low, packed)
         packed[0], arrived[2], give = lax.optimization_barrier((packed[0], arrived[2], give))
         keep = feed_weights(0, kept, g_low, packed)
-        total = wide(keep) + wide(swap(give))
+        came = tie(swap(give), arrived[3])
+        total = wide(keep) + wide(came)
         if above:
             total = jnp.concatenate([total, carried], axis=1)
         total = low(total)
         arrived[0] = tie(arrived[0], total)
+        near = stage([tie(grad_two, sends[0]), z_one, vec])
+        grad_one, low_one, stats[l][0] = norm_back(v + 6, behind(arrived, near), *near)
+        feed_parts[l] = over_dp_sum(total)
+        a_low = gather(low_one)
+        attn_w, qkvm, probs, x_low = stage([tie(attn_w, low_one), qkvm, probs, x_low])
+        dqkv, sums, *sends = attend_back(a_low, attn_w, qkvm, probs)
         if above:
-            arrived[0], feed_parts[l + 1] = lax.optimization_barrier(
-                (arrived[0], feed_parts[l + 1])
-            )
-        grad_one, low_one, stats[l][0] = norm_back(v + 6, arrived, grad_two, z_one, vec, [])
-        feed_parts[l] = over_dp_sum(total)
-        if above:
-            attn_parts[l + 1] = feed_parts[l][:, 3 * quarter :]
-            feed_parts[l] = feed_parts[l][:, : 3 * quarter]
-        a_low = gather(low_one)
-        if above:
-            near = tie(feed_parts[l + 1], *a_low)
-            near = [near] + [hop(near, k) for k in (1, 2)]
-        dqkv, sums, *sends = attend_back(a_low, attn_w, qkvm, probs, [])
-        if above:
-            tied = lax.optimization_barrier((*sends, *near))
-            sends, woven[l + 1] = list(tied[:parts]), list(tied[parts:])
-            woven[l + 1] += [hop(woven[l + 1][0], k) for k in range(3, parts)]
+            woven[l + 1] = gather(tie(feed_parts[l + 1], *a_low))
         stats[l][2] = sums
         arrived = hops(sends)
         give, keep = attend_weights(info[l], a_low, dqkv, x_low, qkvm)
@@ -1059,9 +1000,8 @@
         if l > 0:
             arrived[0] = tie(arrived[0], keep)
             carried = wide(keep) + wide(came)
-            grad_two, low_two, stats_two = norm_back(
-                v - 8 + 7, arrived, grad_one, saved[l - 1][6], vec, []
-            )
+            near = stage([tie(grad_one, sends[0]), saved[l - 1][6], vec])
+            grad_two, low_two, stats_two = norm_back(v - 8 + 7, behind(arrived, near), *near)
 
     count = layers * local_heads
     if direct:
@@ -1105,24 +1045,33 @@
     core_ref = core.astype(jnp.int32)[None]
     out_tokens = both_slots(core_ref, outputs, swap(outputs))
     grad_tokens = both_slots(core_ref, grad, swap(grad))
-    result = None
+    shared = gather(last)
+    near = gather(tie(feed_parts[0], last))
+    result, tokens = None, []
     for l in reversed(range(1, layers)):
-        *result, _ = finish_feed(l, layers, place, woven[l], parts, result)
+        *result, token = finish_feed(l, layers, place, woven[l], quarter, result)
+        tokens.append(token)
+    tied = lax.optimization_barrier((*shared, *near, out_tokens, grad_tokens, *tokens))
+    shared, near = list(tied[:parts]), list(tied[parts : 2 * parts])
+    out_tokens, grad_tokens = tied[2 * parts : 2 * parts + 2]
+    woven[0] = near
     flags = jnp.stack([home, part % per_core == 0]).astype(jnp.int32)
     small_count = layers * 8
-    stacked = [last[:local_rows]] + attn_parts[1:] + [last[local_rows:]]
-    shared = gather(jnp.concatenate(stacked))
-    near = gather(tie(feed_parts[0], shared[0]))
-    tied = lax.optimization_barrier((*shared, *near))
-    shared, near = list(tied[:parts]), list(tied[parts:])
-    given = choose(flags, shared, small_count)
-    arrived = swap(given)
+    others = woven[: layers - 1]
+    arrived = swap(choose(flags, shared, others, small_count, 3 * quarter))
 
     grad_qkv, grad_out, clipped_qk, small_sum = finish_attention(
-        groups, small_count, flags, shared, arrived, qkv_weight.transpose(0, 2, 1, 3)
+        groups,
+        small_count,
+        3 * quarter,
+        flags,
+        shared,
+        others,
+        arrived,
+        qkv_weight.transpose(0, 2, 1, 3),
     )
     small_sum = small_sum[:, :local_rows].reshape(layers, 8, local_rows)
-    grad_glu, grad_down, _ = finish_feed(0, layers, place, near, parts, result)
+    grad_glu, grad_down, _ = finish_feed(0, layers, place, near, quarter, result)
     return (
         out_tokens,
         grad_tokens,

time: 405 us -> 386 us (0.953)
  the two profiles are of different devices: /device:TPU:0 before, /device:TPU:9 now
where the time goes in v3:
time: 386 us; the launch traced here: 378 us
  waiting for transfers between devices  130 us (34%)
  Pallas kernels  107 us (28%)
  starting transfers between devices  77.5 us (20%)
  blocking collectives  22.5 us (6%)
  local copies, waits for them, and re-layouts  15.6 us (4%)
  between operations  15.1 us (4%)
  other arithmetic  10.2 us (3%)
    pallas_call x55, Pallas kernels, call(): pl.pallas_call(body, out_shape=shapes, in_specs=[pl.BlockSpec(memory_spac...  107 us
    ppermute x57, waiting for transfers between devices, hop(): return lax.ppermute(x, 'ctx', [(j, j ^ k) for j in range(parts)])  94 us
    ppermute x57, starting transfers between devices, hop(): return lax.ppermute(x, 'ctx', [(j, j ^ k) for j in range(parts)])  55.1 us
    ppermute x3, waiting for transfers between devices, hop_dp(): return lax.ppermute(x, 'dp', [(j, j ^ k) for j in range(groups)])  27 us
    all_gather x1, blocking collectives, shards(): own = lax.all_gather(attn_first, 'dp', axis=0, tiled=True)  22.5 us
    ppermute x11, starting transfers between devices, swap(): return lax.ppermute(x, 'heads', [(j, cores - 1 - j) for j in range(cores)])  19.2 us
    unnamed x58, local copies, waits for them, and re-layouts  8.55 us
  transfers between devices with their start and end apart: 75, of which 38 were waited for; matrix products, arithmetic and copies ran while one was open for 3% of the time, Pallas kernels for 26%

profile of v3, /device:TPU:9, one launch (start us, length us, event | category | flops | bytes accessed | tf_op | source)
XLA Modules:
  0.0 377.9 jit_solution(16873014469142200193)
XLA Ops:
  9.9 2.7 constant_dynamic-slice_fusion.1
  14.9 2.3 collective-permute-start.2
  19.6 22.5 %all-gather = bf16[1,768,384]{2,1,0:T(8,128)(2,1)S(1)} all-gather(bf16[1,192,384]{2,1,0:T(8,128)(2,1)S(1)} %get-tuple-element.470), channel_id=2, replica_groups=mesh['dp'=4,'ctx'=4,'heads'=2] {'dp'}, dimensions={1}, use_global_device_ids=true | all-gather | bytes 737280 | tf_op jit(solution)/shard_map/all_gather | solution.py:892
  42.1 2.0 collective-permute-start.4
  46.5 9.8 %attend.2 = (bf16[512,768]{1,0:T(8,128)(2,1)}, bf16[512,768]{1,0:T(8,128)(2,1)}, bf16[3,512,512]{2,1,0:T(8,128)(2,1)}, bf16[768,768]{1,0:T(8,128)(2,1)}, f32[8,1...) custom-call(s32[4]{0:T(128)S(1)} %pad_add_fusion.1.info, ...), custom_call_target="tpu_custom_call" | custom-call | flops 1409286144 | bytes 7084316 | tf_op jit(solution)/shard_map/attend/pallas_call | solution.py:80
  60.7 1.9 collective-permute-done.5.p1
  63.5 4.2 %collective-permute-done.7.p3 = bf16[128,768]{1,0:T(8,128)(2,1)S(1)} collective-permute-done((bf16[128,768]{1,0:T(8,128)(2,1)S(1)}, bf16[128,768]{1,0:T(8,128)(2,1)S(1)}, u32[]{:S(2)}, u32[]{:S(2)}) %collective-permute-start.7) | collective-permute-done | bytes 196640 | tf_op jit(solution)/shard_map/ppermute | solution.py:833
  68.6 4.4 %all-gather.4.cloned.1.call-done.refs_0_.own = bf16[768,1536]{1,0:T(8,128)(2,1)} async-done(((bf16[192,1536]{1,0:T(8,128)(2,1)}), bf16[768,1536]{1,0:T(8,128)(2,1)}) %all-gather.4.cloned.1.call-update) | async-done | bytes 2359312 | tf_op jit(solution)/shard_map/all_gather | solution.py:874
  78.0 2.0 stage.14
  92.0 2.1 collective-permute-done.14.p3
  94.1 5.8 %collective-permute-done.12.p2 = bf16[128,768]{1,0:T(8,128)(2,1)S(1)} collective-permute-done((bf16[128,768]{1,0:T(8,128)(2,1)S(1)}, bf16[128,768]{1,0:T(8,128)(2,1)S(1)}, u32[]{:S(2)}, u32[]{:S(2)}) %collective-permute-start.12) | collective-permute-done | bytes 196640 | tf_op jit(solution)/shard_map/ppermute | solution.py:833
  101.8 2.3 collective-permute-start.16
  104.1 3.5 collective-permute-done.17.x3
  107.5 5.5 %collective-permute-done.16.x2 = bf16[128,768]{1,0:T(8,128)(2,1)S(1)} collective-permute-done((bf16[128,768]{1,0:T(8,128)(2,1)S(1)}, bf16[128,768]{1,0:T(8,128)(2,1)S(1)}, u32[]{:S(2)}, u32[]{:S(2)}) %collective-permute-start.16) | collective-permute-done | bytes 196640 | tf_op jit(solution)/shard_map/ppermute | solution.py:833
  113.1 9.8 %attend.3 = (bf16[512,768]{1,0:T(8,128)(2,1)}, bf16[512,768]{1,0:T(8,128)(2,1)}, bf16[3,512,512]{2,1,0:T(8,128)(2,1)}, bf16[768,768]{1,0:T(8,128)(2,1)}, f32[8,1...) custom-call(s32[4]{0:T(128)S(1)} %pad_add_fusion.1.info, ...), custom_call_target="tpu_custom_call" | custom-call | flops 1409286144 | bytes 10623260 | tf_op jit(solution)/shard_map/attend/pallas_call | solution.py:80
  127.2 2.8 collective-permute-done.18.p1
  131.4 3.5 collective-permute-done.20.p3
  140.0 2.0 stage.17
  151.8 3.1 collective-permute-done.27.p3
  154.9 5.4 %collective-permute-done.25.p2 = bf16[128,768]{1,0:T(8,128)(2,1)S(1)} collective-permute-done((bf16[128,768]{1,0:T(8,128)(2,1)S(1)}, bf16[128,768]{1,0:T(8,128)(2,1)S(1)}, u32[]{:S(2)}, u32[]{:S(2)}) %collective-permute-start.25) | collective-permute-done | bytes 196640 | tf_op jit(solution)/shard_map/ppermute | solution.py:833
  160.2 1.9 turn.1
  164.9 2.9 stage.19
  177.1 4.4 %collective-permute-start.33 = (bf16[768,1152]{1,0:T(8,128)(2,1)S(1)}, bf16[768,1152]{1,0:T(8,128)(2,1)S(1)}, u32[]{:S(2)}, u32[]{:S(2)}) collective-permute-start(bf16[768,1152]{1,0:T(8,128)(2,1)S(1)} %feed_weights.4), channel_id=1, source_target_pairs={{0,1},{1,0},{2,3},{3,2},{4,5},{5,4},{6,7},{7,6},{8,9},{9,8},{10,11... | collective-permute-start | bytes 5308424 | tf_op jit(solution)/shard_map/ppermute | solution.py:830
  184.5 4.4 %collective-permute-done.34.p3 = bf16[128,768]{1,0:T(8,128)(2,1)S(1)} collective-permute-done((bf16[128,768]{1,0:T(8,128)(2,1)S(1)}, bf16[128,768]{1,0:T(8,128)(2,1)S(1)}, u32[]{:S(2)}, u32[]{:S(2)}) %collective-permute-start.34) | collective-permute-done | bytes 196640 | tf_op jit(solution)/shard_map/ppermute | solution.py:833
  194.8 2.2 stage.21
  198.5 4.8 %collective-permute-done.36.g2 = bf16[128,768]{1,0:T(8,128)(2,1)S(1)} collective-permute-done((bf16[128,768]{1,0:T(8,128)(2,1)S(1)}, bf16[128,768]{1,0:T(8,128)(2,1)S(1)}, u32[]{:S(2)}, u32[]{:S(2)}) %collective-permute-start.36) | collective-permute-done | bytes 196640 | tf_op jit(solution)/shard_map/ppermute | solution.py:833
  203.3 6.1 %attend_back.2 = (bf16[512,576]{1,0:T(8,128)(2,1)S(1)}, f32[8,576]{1,0:T(8,128)S(1)}, bf16[128,768]{1,0:T(8,128)(2,1)S(1)}, bf16[128,768]{1,0:T(8,128)(2,1)S(1)}...) custom-call(bf16[128,768]{1,0:T(8,128)(2,1)S(1)} %get-tuple-element.327.g0, ...), custom_call_target="tpu_custom_call" | custom-call | flops 2214592512 | bytes 5720064 | tf_op jit(solution)/shard_map/attend_back/pallas_call | solution.py:80
  216.2 4.2 %collective-permute-done.40.p3 = bf16[128,768]{1,0:T(8,128)(2,1)S(1)} collective-permute-done((bf16[128,768]{1,0:T(8,128)(2,1)S(1)}, bf16[128,768]{1,0:T(8,128)(2,1)S(1)}, u32[]{:S(2)}, u32[]{:S(2)}) %collective-permute-start.40) | collective-permute-done | bytes 196640 | tf_op jit(solution)/shard_map/ppermute | solution.py:833
  224.2 3.0 stage.23
  236.5 4.3 %collective-permute-start.46 = (bf16[768,1152]{1,0:T(8,128)(2,1)S(1)}, bf16[768,1152]{1,0:T(8,128)(2,1)S(1)}, u32[]{:S(2)}, u32[]{:S(2)}) collective-permute-start(bf16[768,1152]{1,0:T(8,128)(2,1)S(1)} %feed_weights.6), channel_id=1, source_target_pairs={{0,1},{1,0},{2,3},{3,2},{4,5},{5,4},{6,7},{7,6},{8,9},{9,8},{10,11... | collective-permute-start | bytes 5308424 | tf_op jit(solution)/shard_map/ppermute | solution.py:830
  243.1 1.9 collective-permute-done.48
  245.1 2.5 collective-permute-done.47.p3
  255.1 2.6 stage.25
  258.4 6.0 %collective-permute-done.50.g2 = bf16[128,768]{1,0:T(8,128)(2,1)S(1)} collective-permute-done((bf16[128,768]{1,0:T(8,128)(2,1)S(1)}, bf16[128,768]{1,0:T(8,128)(2,1)S(1)}, u32[]{:S(2)}, u32[]{:S(2)}) %collective-permute-start.50) | collective-permute-done | bytes 196640 | tf_op jit(solution)/shard_map/ppermute | solution.py:833
  264.5 6.1 %attend_back.3 = (bf16[512,576]{1,0:T(8,128)(2,1)S(1)}, f32[8,576]{1,0:T(8,128)S(1)}, bf16[128,768]{1,0:T(8,128)(2,1)S(1)}, bf16[128,768]{1,0:T(8,128)(2,1)S(1)}...) custom-call(bf16[128,768]{1,0:T(8,128)(2,1)S(1)} %get-tuple-element.392.g0, ...), custom_call_target="tpu_custom_call" | custom-call | flops 2214592512 | bytes 5720064 | tf_op jit(solution)/shard_map/attend_back/pallas_call | solution.py:80
  279.9 5.8 %collective-permute-done.53.refs_1_ = bf16[208,384]{1,0:T(8,128)(2,1)S(1)} collective-permute-done((bf16[208,384]{1,0:T(8,128)(2,1)S(1)}, bf16[208,384]{1,0:T(8,128)(2,1)S(1)}, u32[]{:S(2)}, u32[]{:S(2)}) %collective-permute-start.53) | collective-permute-done | bytes 159776 | tf_op jit(solution)/shard_map/ppermute | solution.py:880
  287.3 9.9 %collective-permute-done.54.refs_2_ = bf16[208,384]{1,0:T(8,128)(2,1)S(1)} collective-permute-done((bf16[208,384]{1,0:T(8,128)(2,1)S(1)}, bf16[208,384]{1,0:T(8,128)(2,1)S(1)}, u32[]{:S(2)}, u32[]{:S(2)}) %collective-permute-start.54) | collective-permute-done | bytes 159776 | tf_op jit(solution)/shard_map/ppermute | solution.py:880
  297.2 11.3 %collective-permute-done.55.refs_3_ = bf16[208,384]{1,0:T(8,128)(2,1)S(1)} collective-permute-done((bf16[208,384]{1,0:T(8,128)(2,1)S(1)}, bf16[208,384]{1,0:T(8,128)(2,1)S(1)}, u32[]{:S(2)}, u32[]{:S(2)}) %collective-permute-start.55) | collective-permute-done | bytes 159776 | tf_op jit(solution)/shard_map/ppermute | solution.py:880
  308.5 2.3 collective-permute-start.58
  310.9 3.8 %collective-permute-done.58 = bf16[128,768]{1,0:T(8,128)(2,1)S(1)} collective-permute-done((bf16[128,768]{1,0:T(8,128)(2,1)S(1)}, bf16[128,768]{1,0:T(8,128)(2,1)S(1)}, u32[]{:S(2)}, u32[]{:S(2)}) %collective-permute-start.58) | collective-permute-done | bytes 196640 | tf_op jit(solution)/shard_map/ppermute | solution.py:833
  316.3 2.5 collective-permute-start.67
  320.5 2.7 collective-permute-start.69
  325.7 2.3 collective-permute-start.64
  328.0 18.3 %collective-permute-done.64.refs_3_ = bf16[208,384]{1,0:T(8,128)(2,1)S(1)} collective-permute-done((bf16[208,384]{1,0:T(8,128)(2,1)S(1)}, bf16[208,384]{1,0:T(8,128)(2,1)S(1)}, u32[]{:S(2)}, u32[]{:S(2)}) %collective-permute-start.64) | collective-permute-done | bytes 159776 | tf_op jit(solution)/shard_map/ppermute | solution.py:833
  355.8 3.6 collective-permute-start.70
  359.4 3.1 finish_feed.2
  362.5 3.1 finish_feed.3
  365.7 4.1 %finish_attention.1 = (f32[2,3,192,384]{3,2,1,0:T(8,128)}, f32[2,192,384]{2,1,0:T(8,128)}, f32[2,192,2,384]{3,2,1,0:T(2,128)}, f32[16,192]{1,0:T(8,128)S(1)}) custom-call(s32[2]{0:T(128)S(1)} %add_convert_fusion.3.flags, bf16[208,384]{1,0:T(8,128)(2,1)S(1)} %total.1.refs_0_, bf16[208,384]{1,0:T(8,128)(2,1)} %collective-permute-done.62.refs_1_, ...), custom_call_target="tpu_custom_call" | custom-call | bytes 8097800 | tf_op jit(solution)/shard_map/finish_attention/pallas_call | solution.py:80
  (256 shorter events, 134.6 us)
Async XLA Ops:
  7.2 65.8 %all-gather.4.cloned.1.call-start = ((), (), s32[]{:S(2)}) async-start(), calls=%async_computation.2 | async-start | bytes 2949120 | tf_op jit(solution)/shard_map/all_gather | solution.py:874
  14.8 108.1 %all-gather.6.cloned.1.call-start = ((), (), s32[]{:S(2)}) async-start(), calls=%async_computation.3 | async-start | bytes 2211840 | tf_op jit(solution)/shard_map/all_gather | solution.py:874
  14.9 30.1 %collective-permute-start.2 = (bf16[128,768]{1,0:T(8,128)(2,1)S(1)}, bf16[128,768]{1,0:T(8,128)(2,1)S(1)}, u32[]{:S(2)}, u32[]{:S(2)}) collective-permute-start(bf16[128,768]{1,0:T(8,128)(2,1)S(1)} %dynamic-slice_bitcast_fusion.4.x0.refs_0_), channel_id=1, source_target_pairs={{0,6},{2,4},{4,2},{6,0},{1,7},{3,5},{5,3},{7,1},{8,14},{10,12},{12... | collective-permute-start | bytes 589832 | tf_op jit(solution)/shard_map/ppermute | solution.py:833
  17.3 27.8 %collective-permute-start.1 = (bf16[128,768]{1,0:T(8,128)(2,1)S(1)}, bf16[128,768]{1,0:T(8,128)(2,1)S(1)}, u32[]{:S(2)}, u32[]{:S(2)}) collective-permute-start(bf16[128,768]{1,0:T(8,128)(2,1)S(1)} %dynamic-slice_bitcast_fusion.4.x0.refs_0_), channel_id=1, source_target_pairs={{0,4},{2,6},{4,0},{6,2},{1,5},{3,7},{5,1},{7,3},{8,12},{10,14},{12... | collective-permute-start | bytes 589832 | tf_op jit(solution)/shard_map/ppermute | solution.py:833
  17.4 27.7 %collective-permute-start = (bf16[128,768]{1,0:T(8,128)(2,1)S(1)}, bf16[128,768]{1,0:T(8,128)(2,1)S(1)}, u32[]{:S(2)}, u32[]{:S(2)}) collective-permute-start(bf16[128,768]{1,0:T(8,128)(2,1)S(1)} %dynamic-slice_bitcast_fusion.4.x0.refs_0_), channel_id=1, source_target_pairs={{0,2},{2,0},{4,6},{6,4},{1,3},{3,1},{5,7},{7,5},{8,10},{10,8},{12,... | collective-permute-start | bytes 589832 | tf_op jit(solution)/shard_map/ppermute | solution.py:833
  58.9 8.8 %collective-permute-start.7 = (bf16[128,768]{1,0:T(8,128)(2,1)S(1)}, bf16[128,768]{1,0:T(8,128)(2,1)S(1)}, u32[]{:S(2)}, u32[]{:S(2)}) collective-permute-start(bf16[128,768]{1,0:T(8,128)(2,1)S(1)} %get-tuple-element.236), channel_id=1, source_target_pairs={{0,6},{2,4},{4,2},{6,0},{1,7},{3,5},{5,3},{7,1},{8,14},{10,12},{12... | collective-permute-start | bytes 589832 | tf_op jit(solution)/shard_map/ppermute | solution.py:833
  74.4 200.8 %reduce-scatter.3.cloned.1.call-start = ((), (), s32[]{:S(2)}) async-start(), calls=%async_computation.4 | async-start | bytes 2211840 | tf_op jit(solution)/shard_map/reduce_scatter | solution.py:962
  76.1 9.3 %collective-permute-start.11 = (bf16[128,768]{1,0:T(8,128)(2,1)S(1)}, bf16[128,768]{1,0:T(8,128)(2,1)S(1)}, u32[]{:S(2)}, u32[]{:S(2)}) collective-permute-start(bf16[128,768]{1,0:T(8,128)(2,1)S(1)} %get-tuple-element.238.x_ref), channel_id=1, source_target_pairs={{0,4},{2,6},{4,0},{6,2},{1,5},{3,7},{5,1},{7,3},{8,12},{10,14},{12... | collective-permute-start | bytes 589832 | tf_op jit(solution)/shard_map/ppermute | solution.py:833
  77.5 9.3 %collective-permute-start.13 = (bf16[128,768]{1,0:T(8,128)(2,1)S(1)}, bf16[128,768]{1,0:T(8,128)(2,1)S(1)}, u32[]{:S(2)}, u32[]{:S(2)}) collective-permute-start(bf16[128,768]{1,0:T(8,128)(2,1)S(1)} %get-tuple-element.238.x_ref), channel_id=1, source_target_pairs={{0,6},{2,4},{4,2},{6,0},{1,7},{3,5},{5,3},{7,1},{8,14},{10,12},{12... | collective-permute-start | bytes 589832 | tf_op jit(solution)/shard_map/ppermute | solution.py:833
  82.9 9.1 %collective-permute-start.10 = (bf16[128,768]{1,0:T(8,128)(2,1)S(1)}, bf16[128,768]{1,0:T(8,128)(2,1)S(1)}, u32[]{:S(2)}, u32[]{:S(2)}) collective-permute-start(bf16[128,768]{1,0:T(8,128)(2,1)S(1)} %get-tuple-element.250), channel_id=1, source_target_pairs={{0,2},{2,0},{4,6},{6,4},{1,3},{3,1},{5,7},{7,5},{8,10},{10,8},{12,... | collective-permute-start | bytes 589832 | tf_op jit(solution)/shard_map/ppermute | solution.py:833
  89.2 10.6 %collective-permute-start.12 = (bf16[128,768]{1,0:T(8,128)(2,1)S(1)}, bf16[128,768]{1,0:T(8,128)(2,1)S(1)}, u32[]{:S(2)}, u32[]{:S(2)}) collective-permute-start(bf16[128,768]{1,0:T(8,128)(2,1)S(1)} %get-tuple-element.252), channel_id=1, source_target_pairs={{0,4},{2,6},{4,0},{6,2},{1,5},{3,7},{5,1},{7,3},{8,12},{10,14},{12... | collective-permute-start | bytes 589832 | tf_op jit(solution)/shard_map/ppermute | solution.py:833
  101.8 11.3 %collective-permute-start.16 = (bf16[128,768]{1,0:T(8,128)(2,1)S(1)}, bf16[128,768]{1,0:T(8,128)(2,1)S(1)}, u32[]{:S(2)}, u32[]{:S(2)}) collective-permute-start(bf16[128,768]{1,0:T(8,128)(2,1)S(1)} %get-tuple-element.256.x0), channel_id=1, source_target_pairs={{0,4},{2,6},{4,0},{6,2},{1,5},{3,7},{5,1},{7,3},{8,12},{10,14},{12... | collective-permute-start | bytes 589832 | tf_op jit(solution)/shard_map/ppermute | solution.py:833
  104.1 9.0 %collective-permute-start.15 = (bf16[128,768]{1,0:T(8,128)(2,1)S(1)}, bf16[128,768]{1,0:T(8,128)(2,1)S(1)}, u32[]{:S(2)}, u32[]{:S(2)}) collective-permute-start(bf16[128,768]{1,0:T(8,128)(2,1)S(1)} %get-tuple-element.256.x0), channel_id=1, source_target_pairs={{0,2},{2,0},{4,6},{6,4},{1,3},{3,1},{5,7},{7,5},{8,10},{10,8},{12,... | collective-permute-start | bytes 589832 | tf_op jit(solution)/shard_map/ppermute | solution.py:833
  122.9 15.8 %collective-permute-start.21 = (bf16[768,1152]{1,0:T(8,128)(2,1)}, bf16[768,1152]{1,0:T(8,128)(2,1)S(1)}, u32[]{:S(2)}, u32[]{:S(2)}) collective-permute-start(bf16[768,1152]{1,0:T(8,128)(2,1)} %all-gather.6.cloned.1.call-done.refs_0_), channel_id=1, source_target_pairs={{0,1},{1,0},{2,3},{3,2},{4,5},{5,4},{6,7},{7,6},{8,9},{9,8},{10,11... | collective-permute-start | bytes 5308424 | tf_op jit(solution)/shard_map/ppermute | solution.py:830
  125.6 9.4 %collective-permute-start.20 = (bf16[128,768]{1,0:T(8,128)(2,1)S(1)}, bf16[128,768]{1,0:T(8,128)(2,1)S(1)}, u32[]{:S(2)}, u32[]{:S(2)}) collective-permute-start(bf16[128,768]{1,0:T(8,128)(2,1)S(1)} %get-tuple-element.264), channel_id=1, source_target_pairs={{0,6},{2,4},{4,2},{6,0},{1,7},{3,5},{5,3},{7,1},{8,14},{10,12},{12... | collective-permute-start | bytes 589832 | tf_op jit(solution)/shard_map/ppermute | solution.py:833
  136.1 7.4 %collective-permute-start.22 = (bf16[128,768]{1,0:T(8,128)(2,1)S(1)}, bf16[128,768]{1,0:T(8,128)(2,1)S(1)}, u32[]{:S(2)}, u32[]{:S(2)}) collective-permute-start(bf16[128,768]{1,0:T(8,128)(2,1)S(1)} %get-tuple-element.266.x_ref), channel_id=1, source_target_pairs={{0,2},{2,0},{4,6},{6,4},{1,3},{3,1},{5,7},{7,5},{8,10},{10,8},{12,... | collective-permute-start | bytes 589832 | tf_op jit(solution)/shard_map/ppermute | solution.py:833
  137.1 8.8 %collective-permute-start.24 = (bf16[128,768]{1,0:T(8,128)(2,1)S(1)}, bf16[128,768]{1,0:T(8,128)(2,1)S(1)}, u32[]{:S(2)}, u32[]{:S(2)}) collective-permute-start(bf16[128,768]{1,0:T(8,128)(2,1)S(1)} %get-tuple-element.266.x_ref), channel_id=1, source_target_pairs={{0,4},{2,6},{4,0},{6,2},{1,5},{3,7},{5,1},{7,3},{8,12},{10,14},{12... | collective-permute-start | bytes 589832 | tf_op jit(solution)/shard_map/ppermute | solution.py:833
  137.9 9.6 %collective-permute-start.26 = (bf16[128,768]{1,0:T(8,128)(2,1)S(1)}, bf16[128,768]{1,0:T(8,128)(2,1)S(1)}, u32[]{:S(2)}, u32[]{:S(2)}) collective-permute-start(bf16[128,768]{1,0:T(8,128)(2,1)S(1)} %get-tuple-element.266.x_ref), channel_id=1, source_target_pairs={{0,6},{2,4},{4,2},{6,0},{1,7},{3,5},{5,3},{7,1},{8,14},{10,12},{12... | collective-permute-start | bytes 589832 | tf_op jit(solution)/shard_map/ppermute | solution.py:833
  144.9 6.9 %collective-permute-start.23 = (bf16[128,768]{1,0:T(8,128)(2,1)S(1)}, bf16[128,768]{1,0:T(8,128)(2,1)S(1)}, u32[]{:S(2)}, u32[]{:S(2)}) collective-permute-start(bf16[128,768]{1,0:T(8,128)(2,1)S(1)} %get-tuple-element.280), channel_id=1, source_target_pairs={{0,2},{2,0},{4,6},{6,4},{1,3},{3,1},{5,7},{7,5},{8,10},{10,8},{12,... | collective-permute-start | bytes 589832 | tf_op jit(solution)/shard_map/ppermute | solution.py:833
  150.2 10.0 %collective-permute-start.25 = (bf16[128,768]{1,0:T(8,128)(2,1)S(1)}, bf16[128,768]{1,0:T(8,128)(2,1)S(1)}, u32[]{:S(2)}, u32[]{:S(2)}) collective-permute-start(bf16[128,768]{1,0:T(8,128)(2,1)S(1)} %get-tuple-element.282), channel_id=1, source_target_pairs={{0,4},{2,6},{4,0},{6,2},{1,5},{3,7},{5,1},{7,3},{8,12},{10,14},{12... | collective-permute-start | bytes 589832 | tf_op jit(solution)/shard_map/ppermute | solution.py:833
  163.1 8.0 %collective-permute-start.29 = (bf16[128,768]{1,0:T(8,128)(2,1)S(1)}, bf16[128,768]{1,0:T(8,128)(2,1)S(1)}, u32[]{:S(2)}, u32[]{:S(2)}) collective-permute-start(bf16[128,768]{1,0:T(8,128)(2,1)S(1)} %get-tuple-element.286.g_ref.refs_4_), channel_id=1, source_target_pairs={{0,4},{2,6},{4,0},{6,2},{1,5},{3,7},{5,1},{7,3},{8,12},{10,14},{12... | collective-permute-start | bytes 589832 | tf_op jit(solution)/shard_map/ppermute | solution.py:833
  163.4 9.2 %collective-permute-start.30 = (bf16[128,768]{1,0:T(8,128)(2,1)S(1)}, bf16[128,768]{1,0:T(8,128)(2,1)S(1)}, u32[]{:S(2)}, u32[]{:S(2)}) collective-permute-start(bf16[128,768]{1,0:T(8,128)(2,1)S(1)} %get-tuple-element.286.g_ref.refs_4_), channel_id=1, source_target_pairs={{0,6},{2,4},{4,2},{6,0},{1,7},{3,5},{5,3},{7,1},{8,14},{10,12},{12... | collective-permute-start | bytes 589832 | tf_op jit(solution)/shard_map/ppermute | solution.py:833
  177.1 11.8 %collective-permute-start.33 = (bf16[768,1152]{1,0:T(8,128)(2,1)S(1)}, bf16[768,1152]{1,0:T(8,128)(2,1)S(1)}, u32[]{:S(2)}, u32[]{:S(2)}) collective-permute-start(bf16[768,1152]{1,0:T(8,128)(2,1)S(1)} %feed_weights.4), channel_id=1, source_target_pairs={{0,1},{1,0},{2,3},{3,2},{4,5},{5,4},{6,7},{7,6},{8,9},{9,8},{10,11... | collective-permute-start | bytes 5308424 | tf_op jit(solution)/shard_map/ppermute | solution.py:830
  181.5 7.4 %collective-permute-start.34 = (bf16[128,768]{1,0:T(8,128)(2,1)S(1)}, bf16[128,768]{1,0:T(8,128)(2,1)S(1)}, u32[]{:S(2)}, u32[]{:S(2)}) collective-permute-start(bf16[128,768]{1,0:T(8,128)(2,1)S(1)} %get-tuple-element.316), channel_id=1, source_target_pairs={{0,6},{2,4},{4,2},{6,0},{1,7},{3,5},{5,3},{7,1},{8,14},{10,12},{12... | collective-permute-start | bytes 589832 | tf_op jit(solution)/shard_map/ppermute | solution.py:833
  192.5 10.8 %collective-permute-start.36 = (bf16[128,768]{1,0:T(8,128)(2,1)S(1)}, bf16[128,768]{1,0:T(8,128)(2,1)S(1)}, u32[]{:S(2)}, u32[]{:S(2)}) collective-permute-start(bf16[128,768]{1,0:T(8,128)(2,1)S(1)} %get-tuple-element.327.g0), channel_id=1, source_target_pairs={{0,4},{2,6},{4,0},{6,2},{1,5},{3,7},{5,1},{7,3},{8,12},{10,14},{12... | collective-permute-start | bytes 589832 | tf_op jit(solution)/shard_map/ppermute | solution.py:833
  193.7 9.6 %collective-permute-start.35 = (bf16[128,768]{1,0:T(8,128)(2,1)S(1)}, bf16[128,768]{1,0:T(8,128)(2,1)S(1)}, u32[]{:S(2)}, u32[]{:S(2)}) collective-permute-start(bf16[128,768]{1,0:T(8,128)(2,1)S(1)} %get-tuple-element.327.g0), channel_id=1, source_target_pairs={{0,2},{2,0},{4,6},{6,4},{1,3},{3,1},{5,7},{7,5},{8,10},{10,8},{12,... | collective-permute-start | bytes 589832 | tf_op jit(solution)/shard_map/ppermute | solution.py:833
  194.5 121.7 %reduce-scatter.5.cloned.1.call-start = ((), (), s32[]{:S(2)}) async-start(), calls=%async_computation.5 | async-start | bytes 2949120 | tf_op jit(solution)/shard_map/reduce_scatter | solution.py:962
  211.1 9.2 %collective-permute-start.40 = (bf16[128,768]{1,0:T(8,128)(2,1)S(1)}, bf16[128,768]{1,0:T(8,128)(2,1)S(1)}, u32[]{:S(2)}, u32[]{:S(2)}) collective-permute-start(bf16[128,768]{1,0:T(8,128)(2,1)S(1)} %get-tuple-element.347), channel_id=1, source_target_pairs={{0,6},{2,4},{4,2},{6,0},{1,7},{3,5},{5,3},{7,1},{8,14},{10,12},{12... | collective-permute-start | bytes 589832 | tf_op jit(solution)/shard_map/ppermute | solution.py:833
  221.5 6.9 %collective-permute-start.41 = (bf16[128,768]{1,0:T(8,128)(2,1)S(1)}, bf16[128,768]{1,0:T(8,128)(2,1)S(1)}, u32[]{:S(2)}, u32[]{:S(2)}) collective-permute-start(bf16[128,768]{1,0:T(8,128)(2,1)S(1)} %get-tuple-element.350.g_ref.refs_4_), channel_id=1, source_target_pairs={{0,2},{2,0},{4,6},{6,4},{1,3},{3,1},{5,7},{7,5},{8,10},{10,8},{12,... | collective-permute-start | bytes 589832 | tf_op jit(solution)/shard_map/ppermute | solution.py:833
  222.4 8.0 %collective-permute-start.42 = (bf16[128,768]{1,0:T(8,128)(2,1)S(1)}, bf16[128,768]{1,0:T(8,128)(2,1)S(1)}, u32[]{:S(2)}, u32[]{:S(2)}) collective-permute-start(bf16[128,768]{1,0:T(8,128)(2,1)S(1)} %get-tuple-element.350.g_ref.refs_4_), channel_id=1, source_target_pairs={{0,4},{2,6},{4,0},{6,2},{1,5},{3,7},{5,1},{7,3},{8,12},{10,14},{12... | collective-permute-start | bytes 589832 | tf_op jit(solution)/shard_map/ppermute | solution.py:833
  223.1 9.2 %collective-permute-start.43 = (bf16[128,768]{1,0:T(8,128)(2,1)S(1)}, bf16[128,768]{1,0:T(8,128)(2,1)S(1)}, u32[]{:S(2)}, u32[]{:S(2)}) collective-permute-start(bf16[128,768]{1,0:T(8,128)(2,1)S(1)} %get-tuple-element.350.g_ref.refs_4_), channel_id=1, source_target_pairs={{0,6},{2,4},{4,2},{6,0},{1,7},{3,5},{5,3},{7,1},{8,14},{10,12},{12... | collective-permute-start | bytes 589832 | tf_op jit(solution)/shard_map/ppermute | solution.py:833
  236.5 11.2 %collective-permute-start.46 = (bf16[768,1152]{1,0:T(8,128)(2,1)S(1)}, bf16[768,1152]{1,0:T(8,128)(2,1)S(1)}, u32[]{:S(2)}, u32[]{:S(2)}) collective-permute-start(bf16[768,1152]{1,0:T(8,128)(2,1)S(1)} %feed_weights.6), channel_id=1, source_target_pairs={{0,1},{1,0},{2,3},{3,2},{4,5},{5,4},{6,7},{7,6},{8,9},{9,8},{10,11... | collective-permute-start | bytes 5308424 | tf_op jit(solution)/shard_map/ppermute | solution.py:830
  253.5 11.0 %collective-permute-start.50 = (bf16[128,768]{1,0:T(8,128)(2,1)S(1)}, bf16[128,768]{1,0:T(8,128)(2,1)S(1)}, u32[]{:S(2)}, u32[]{:S(2)}) collective-permute-start(bf16[128,768]{1,0:T(8,128)(2,1)S(1)} %get-tuple-element.392.g0), channel_id=1, source_target_pairs={{0,4},{2,6},{4,0},{6,2},{1,5},{3,7},{5,1},{7,3},{8,12},{10,14},{12... | collective-permute-start | bytes 589832 | tf_op jit(solution)/shard_map/ppermute | solution.py:833
  254.2 10.3 %collective-permute-start.49 = (bf16[128,768]{1,0:T(8,128)(2,1)S(1)}, bf16[128,768]{1,0:T(8,128)(2,1)S(1)}, u32[]{:S(2)}, u32[]{:S(2)}) collective-permute-start(bf16[128,768]{1,0:T(8,128)(2,1)S(1)} %get-tuple-element.392.g0), channel_id=1, source_target_pairs={{0,2},{2,0},{4,6},{6,4},{1,3},{3,1},{5,7},{7,5},{8,10},{10,8},{12,... | collective-permute-start | bytes 589832 | tf_op jit(solution)/shard_map/ppermute | solution.py:833
  275.0 10.7 %collective-permute-start.53 = (bf16[208,384]{1,0:T(8,128)(2,1)S(1)}, bf16[208,384]{1,0:T(8,128)(2,1)S(1)}, u32[]{:S(2)}, u32[]{:S(2)}) collective-permute-start(bf16[208,384]{1,0:T(8,128)(2,1)S(1)} %get-tuple-element.413), channel_id=1, source_target_pairs={{0,8},{8,0},{16,24},{24,16},{1,9},{9,1},{17,25},{25,17},{2,10},{10... | collective-permute-start | bytes 479240 | tf_op jit(solution)/shard_map/ppermute | solution.py:880
  275.2 39.5 %collective-permute-start.61 = (bf16[192,1152]{1,0:T(8,128)(2,1)}, bf16[192,1152]{1,0:T(8,128)(2,1)S(1)}, u32[]{:S(2)}, u32[]{:S(2)}) collective-permute-start(bf16[192,1152]{1,0:T(8,128)(2,1)} %reduce-scatter.3.cloned.1.call-done.refs_0_), channel_id=1, source_target_pairs={{0,6},{2,4},{4,2},{6,0},{1,7},{3,5},{5,3},{7,1},{8,14},{10,12},{12... | collective-permute-start | bytes 1327112 | tf_op jit(solution)/shard_map/ppermute | solution.py:833
  276.3 38.4 %collective-permute-start.60 = (bf16[192,1152]{1,0:T(8,128)(2,1)}, bf16[192,1152]{1,0:T(8,128)(2,1)S(1)}, u32[]{:S(2)}, u32[]{:S(2)}) collective-permute-start(bf16[192,1152]{1,0:T(8,128)(2,1)} %reduce-scatter.3.cloned.1.call-done.refs_0_), channel_id=1, source_target_pairs={{0,4},{2,6},{4,0},{6,2},{1,5},{3,7},{5,1},{7,3},{8,12},{10,14},{12... | collective-permute-start | bytes 1327112 | tf_op jit(solution)/shard_map/ppermute | solution.py:833
  277.0 38.5 %collective-permute-start.59 = (bf16[192,1152]{1,0:T(8,128)(2,1)}, bf16[192,1152]{1,0:T(8,128)(2,1)S(1)}, u32[]{:S(2)}, u32[]{:S(2)}) collective-permute-start(bf16[192,1152]{1,0:T(8,128)(2,1)} %reduce-scatter.3.cloned.1.call-done.refs_0_), channel_id=1, source_target_pairs={{0,2},{2,0},{4,6},{6,4},{1,3},{3,1},{5,7},{7,5},{8,10},{10,8},{12,... | collective-permute-start | bytes 1327112 | tf_op jit(solution)/shard_map/ppermute | solution.py:833
  279.2 18.0 %collective-permute-start.54 = (bf16[208,384]{1,0:T(8,128)(2,1)S(1)}, bf16[208,384]{1,0:T(8,128)(2,1)S(1)}, u32[]{:S(2)}, u32[]{:S(2)}) collective-permute-start(bf16[208,384]{1,0:T(8,128)(2,1)S(1)} %get-tuple-element.414), channel_id=1, source_target_pairs={{0,16},{8,24},{16,0},{24,8},{1,17},{9,25},{17,1},{25,9},{2,18},{10... | collective-permute-start | bytes 479240 | tf_op jit(solution)/shard_map/ppermute | solution.py:880
  285.8 22.7 %collective-permute-start.55 = (bf16[208,384]{1,0:T(8,128)(2,1)S(1)}, bf16[208,384]{1,0:T(8,128)(2,1)S(1)}, u32[]{:S(2)}, u32[]{:S(2)}) collective-permute-start(bf16[208,384]{1,0:T(8,128)(2,1)S(1)} %get-tuple-element.415), channel_id=1, source_target_pairs={{0,24},{8,16},{16,8},{24,0},{1,25},{9,17},{17,9},{25,1},{2,26},{10... | collective-permute-start | bytes 479240 | tf_op jit(solution)/shard_map/ppermute | solution.py:880
  297.2 13.7 %collective-permute-start.57 = (bf16[128,768]{1,0:T(8,128)(2,1)S(1)}, bf16[128,768]{1,0:T(8,128)(2,1)S(1)}, u32[]{:S(2)}, u32[]{:S(2)}) collective-permute-start(bf16[128,768]{1,0:T(8,128)(2,1)S(1)} %get-tuple-element.418), channel_id=1, source_target_pairs={{0,4},{2,6},{4,0},{6,2},{1,5},{3,7},{5,1},{7,3},{8,12},{10,14},{12... | collective-permute-start | bytes 589832 | tf_op jit(solution)/shard_map/ppermute | solution.py:833
  316.3 38.2 %collective-permute-start.67 = (bf16[192,1536]{1,0:T(8,128)(2,1)}, bf16[192,1536]{1,0:T(8,128)(2,1)S(1)}, u32[]{:S(2)}, u32[]{:S(2)}) collective-permute-start(bf16[192,1536]{1,0:T(8,128)(2,1)} %reduce-scatter.5.cloned.1.call-done.refs_4_.refs_0_), channel_id=1, source_target_pairs={{0,6},{2,4},{4,2},{6,0},{1,7},{3,5},{5,3},{7,1},{8,14},{10,12},{12... | collective-permute-start | bytes 1769480 | tf_op jit(solution)/shard_map/ppermute | solution.py:833
  318.8 35.7 %collective-permute-start.66 = (bf16[192,1536]{1,0:T(8,128)(2,1)}, bf16[192,1536]{1,0:T(8,128)(2,1)S(1)}, u32[]{:S(2)}, u32[]{:S(2)}) collective-permute-start(bf16[192,1536]{1,0:T(8,128)(2,1)} %reduce-scatter.5.cloned.1.call-done.refs_4_.refs_0_), channel_id=1, source_target_pairs={{0,4},{2,6},{4,0},{6,2},{1,5},{3,7},{5,1},{7,3},{8,12},{10,14},{12... | collective-permute-start | bytes 1769480 | tf_op jit(solution)/shard_map/ppermute | solution.py:833
  318.8 35.7 %collective-permute-start.65 = (bf16[192,1536]{1,0:T(8,128)(2,1)}, bf16[192,1536]{1,0:T(8,128)(2,1)S(1)}, u32[]{:S(2)}, u32[]{:S(2)}) collective-permute-start(bf16[192,1536]{1,0:T(8,128)(2,1)} %reduce-scatter.5.cloned.1.call-done.refs_4_.refs_0_), channel_id=1, source_target_pairs={{0,2},{2,0},{4,6},{6,4},{1,3},{3,1},{5,7},{7,5},{8,10},{10,8},{12,... | collective-permute-start | bytes 1769480 | tf_op jit(solution)/shard_map/ppermute | solution.py:833
  320.5 27.0 %collective-permute-start.69 = (f32[128,768]{1,0:T(8,128)S(1)}, f32[128,768]{1,0:T(8,128)S(1)}, u32[]{:S(2)}, u32[]{:S(2)}) collective-permute-start(f32[128,768]{1,0:T(8,128)S(1)} %add_add_fusion.own), channel_id=1, source_target_pairs={{0,1},{1,0},{2,3},{3,2},{4,5},{5,4},{6,7},{7,6},{8,9},{9,8},{10,11... | collective-permute-start | bytes 1179656 | tf_op jit(solution)/shard_map/ppermute | solution.py:830
  325.7 20.6 %collective-permute-start.64 = (bf16[208,384]{1,0:T(8,128)(2,1)S(1)}, bf16[208,384]{1,0:T(8,128)(2,1)S(1)}, u32[]{:S(2)}, u32[]{:S(2)}) collective-permute-start(bf16[208,384]{1,0:T(8,128)(2,1)S(1)} %total.1.refs_0_), channel_id=1, source_target_pairs={{0,6},{2,4},{4,2},{6,0},{1,7},{3,5},{5,3},{7,1},{8,14},{10,12},{12... | collective-permute-start | bytes 479240 | tf_op jit(solution)/shard_map/ppermute | solution.py:833
  346.3 8.2 %collective-permute-start.63 = (bf16[208,384]{1,0:T(8,128)(2,1)S(1)}, bf16[208,384]{1,0:T(8,128)(2,1)}, u32[]{:S(2)}, u32[]{:S(2)}) collective-permute-start(bf16[208,384]{1,0:T(8,128)(2,1)S(1)} %total.1.refs_0_), channel_id=1, source_target_pairs={{0,4},{2,6},{4,0},{6,2},{1,5},{3,7},{5,1},{7,3},{8,12},{10,14},{12... | collective-permute-start | bytes 479240 | tf_op jit(solution)/shard_map/ppermute | solution.py:833
  355.8 9.8 %collective-permute-start.70 = (bf16[864,384]{1,0:T(8,128)(2,1)S(1)}, bf16[864,384]{1,0:T(8,128)(2,1)S(1)}, u32[]{:S(2)}, u32[]{:S(2)}) collective-permute-start(bf16[864,384]{1,0:T(8,128)(2,1)S(1)} %choose.1), channel_id=1, source_target_pairs={{0,1},{1,0},{2,3},{3,2},{4,5},{5,4},{6,7},{7,6},{8,9},{9,8},{10,11... | collective-permute-start | bytes 1990664 | tf_op jit(solution)/shard_map/ppermute | solution.py:830
  (56 other events, 416.5 us)
Sparse Core Ops, SparseCore 0:
  15.0 58.0 all-gather.3
  75.2 38.5 all-gather.5
  194.7 35.7 reduce-scatter.2
  250.1 57.8 reduce-scatter.4
